TPU v7x, 32 devices: a whole 2x2x4 slice. The times are simulated.
32 devices in a mesh: groups: 2 (over y), gx: 4 (over z), gy: 2 (over x), col: 2 (over core).
Axes of the slice: x: 2, y: 2, z: 4, core: 2. Of those that a mesh axis runs over, the one named last changes fastest.
Arguments:
- state_in: bfloat16 [64, 2048, 2048], P(('groups', 'col'), 'gx', 'gy'), parts along dimension 0, may hold values from -6 to 6
- tile_class: int32 [256, 128], P(('groups', 'gx'), 'gy'), parts along dimension 0, may hold values from 0 to 7
- class_bias: float32 [8, 32], replicated, may hold values from -4 to 4
- w_point: bfloat16 [32, 32], replicated, may hold values from -1 to 1
- spec_weight: bfloat16 [2, 32, 32, 128, 128], P(None, None, 'col', 'gx', 'gy'), may hold values from -0.75 to 0.75
- grad_out: bfloat16 [64, 2048, 2048], P(('groups', 'col'), 'gx', 'gy'), parts along dimension 0, may hold values from -6 to 6
Outputs:
- act_out: bfloat16 [64, 2048, 2048], P(('groups', 'col'), 'gx', 'gy'), parts along dimension 0
- grad_in: bfloat16 [64, 2048, 2048], P(('groups', 'col'), 'gx', 'gy'), parts along dimension 0
- grad_spec: float32 [4, 32, 32, 128, 128], P('groups', None, 'col', 'gx', 'gy'), parts along dimension 0
- grad_point: float32 [64, 32], P(('groups', 'col')), parts along dimension 0
- grad_bias: float32 [16, 32], P('groups', 'col'), parts along dimension 0
There are 2 independent parts, one for each index of `groups`. A program takes and returns all parts, laid end to end along the dimension named above; an argument that names none is the same for every part. Nothing has to cross between parts.
Inputs may be any that keep to these rules, and one draw needn't show every extreme that they name: `tile_class`: bathymetry class of each 16 x 16 tile of cells.
All inputs are finite; a program needn't handle non-finite values.
Results may differ from a plain program's by a relative error of at most 0.015.
Values may be sent and summed in bfloat16 or wider, within the bound.
No kernel may reach another device: no remote copies, remote signals or barrier semaphores. Data moves between devices by JAX's collectives and lax.ppermute only.
A program may use at most 640 MiB of HBM per device.

v0:
```python
import math

import jax
import jax.numpy as jnp
from jax import lax
from jax.sharding import PartitionSpec as P

NX = 2048
NY = 2048
MX = 128
MY = 128
TILE = 16
NCLASS = 8


root_half = 0.7071067811865476
inv_root_tau = 0.3989422804014327


def y_forward_table(offset, length):
    freq_y = jnp.arange(MY, dtype=jnp.int32)
    points = offset + jnp.arange(length, dtype=jnp.int32)
    angles = (points[:, None] * freq_y[None, :] % NY).astype(jnp.float32) * (2.0 * math.pi / NY)
    return jnp.stack([jnp.cos(angles), -jnp.sin(angles)]).astype(jnp.bfloat16)


def y_inverse_table(offset, length):
    freq_y = jnp.arange(MY, dtype=jnp.int32)
    points = offset + jnp.arange(length, dtype=jnp.int32)
    angles = (freq_y[:, None] * points[None, :] % NY).astype(jnp.float32) * (2.0 * math.pi / NY)
    weight_k = jnp.where(freq_y == 0, 1.0, 2.0).astype(jnp.float32)[:, None]
    return jnp.stack([weight_k * jnp.cos(angles), -weight_k * jnp.sin(angles)]).astype(jnp.bfloat16)


def x_tables(offset, length):
    freq_x = jnp.arange(MX, dtype=jnp.int32)
    signed_x = jnp.where(freq_x < MX // 2, freq_x, freq_x - MX)
    points = offset + jnp.arange(length, dtype=jnp.int32)
    angles = (signed_x[:, None] * points[None, :] % NX).astype(jnp.float32) * (2.0 * math.pi / NX)
    cos_part = jnp.cos(angles)
    sin_part = jnp.sin(angles)
    x_fwd = jnp.stack([jnp.stack([cos_part, -sin_part]), jnp.stack([sin_part, cos_part])]).astype(
        jnp.bfloat16
    )
    x_inv = jnp.stack([jnp.stack([cos_part, sin_part]), jnp.stack([-sin_part, cos_part])]).astype(
        jnp.bfloat16
    )
    return (x_fwd, x_inv)


def mix_modes(weight, spectrum):
    high = lax.Precision.HIGHEST
    real_part = jnp.einsum("iokm,ikm->okm", weight[0], spectrum[0], precision=high) - jnp.einsum(
        "iokm,ikm->okm", weight[1], spectrum[1], precision=high
    )
    imag_part = jnp.einsum("iokm,ikm->okm", weight[0], spectrum[1], precision=high) + jnp.einsum(
        "iokm,ikm->okm", weight[1], spectrum[0], precision=high
    )
    return jnp.stack([real_part, imag_part])


def back_mix(weight, grad_modes):
    high = lax.Precision.HIGHEST
    real_part = jnp.einsum("iokm,okm->ikm", weight[0], grad_modes[0], precision=high) + jnp.einsum(
        "iokm,okm->ikm", weight[1], grad_modes[1], precision=high
    )
    imag_part = jnp.einsum("iokm,okm->ikm", weight[0], grad_modes[1], precision=high) - jnp.einsum(
        "iokm,okm->ikm", weight[1], grad_modes[0], precision=high
    )
    return jnp.stack([real_part, imag_part])


def weight_grad(spectrum, grad_modes):
    real_part = jnp.einsum("ikm,okm->iokm", spectrum[0], grad_modes[0]) + jnp.einsum(
        "ikm,okm->iokm", spectrum[1], grad_modes[1]
    )
    imag_part = jnp.einsum("ikm,okm->iokm", spectrum[0], grad_modes[1]) - jnp.einsum(
        "ikm,okm->iokm", spectrum[1], grad_modes[0]
    )
    return jnp.stack([real_part, imag_part])


def on_device(state_in, tile_class, class_bias, w_point, spec_weight, grad_out):
    own_chan, row_count, col_count = state_in.shape
    gx_index = lax.axis_index("gx")
    gy_index = lax.axis_index("gy")
    col_index = lax.axis_index("col")
    scale_fwd = 1.0 / math.sqrt(NX * NY)
    scale_inv = 1.0 / math.sqrt(2.0 * MX * MY)
    y_fwd = y_forward_table(gy_index * col_count, col_count)
    y_inv = y_inverse_table(gy_index * col_count, col_count)
    fwd_all, inv_all = x_tables(0, NX)
    fwd_own, inv_own = x_tables(gx_index * row_count, row_count)
    state_all = lax.all_gather(state_in, "col", axis=0, tiled=True)
    w_rows = lax.dynamic_slice_in_dim(w_point, col_index * own_chan, own_chan, 0)
    w_cols = lax.dynamic_slice_in_dim(w_point, col_index * own_chan, own_chan, 1)
    point_mix = jnp.einsum("oi,ixy->oxy", w_rows, state_all, preferred_element_type=jnp.float32)
    row_spec = jnp.einsum(
        "cxy,tyk->tckx", state_in, y_fwd, preferred_element_type=jnp.float32
    ).astype(jnp.bfloat16)
    row_full = lax.all_to_all(row_spec, "gx", split_axis=2, concat_axis=3, tiled=True)
    col_terms = jnp.einsum("rckx,rtmx->tckm", row_full, fwd_all, preferred_element_type=jnp.float32)
    spectrum = lax.psum_scatter(col_terms, "gy", scatter_dimension=3, tiled=True) * scale_fwd
    spec_all = lax.all_gather(spectrum, "col", axis=1, tiled=True)
    weight_f = spec_weight.astype(jnp.float32)
    mixed = mix_modes(weight_f, spec_all).astype(jnp.bfloat16)
    mixed_kx = lax.all_gather(mixed, "gy", axis=3, tiled=True)
    mixed_all = lax.all_gather(mixed_kx, "gx", axis=2, tiled=True)
    space_rows = jnp.einsum(
        "rokm,rtmx->tokx", mixed_all, inv_own, preferred_element_type=jnp.float32
    ).astype(jnp.bfloat16)
    spectral = scale_inv * jnp.einsum(
        "tokx,tky->oxy", space_rows, y_inv, preferred_element_type=jnp.float32
    )
    tile_rows = row_count // TILE
    tile_cols = col_count // TILE
    one_hot = (tile_class[:, :, None] == jnp.arange(NCLASS, dtype=jnp.int32)).astype(jnp.float32)
    bias_own = lax.dynamic_slice_in_dim(class_bias, col_index * own_chan, own_chan, 1)
    tile_bias = jnp.einsum("abn,no->oab", one_hot, bias_own)
    summed = (point_mix + spectral).reshape(own_chan, tile_rows, TILE, tile_cols, TILE)
    pre_act = (summed + tile_bias[:, :, None, :, None]).reshape(own_chan, row_count, col_count)
    normal_cdf = 0.5 * (1.0 + jax.scipy.special.erf(pre_act * root_half))
    act_out = (pre_act * normal_cdf).astype(jnp.bfloat16)
    gelu_slope = normal_cdf + pre_act * jnp.exp(-0.5 * pre_act * pre_act) * inv_root_tau
    grad_pre = (grad_out.astype(jnp.float32) * gelu_slope).astype(jnp.bfloat16)
    grad_all = lax.all_gather(grad_pre, "col", axis=0, tiled=True)
    point_grad = scale_fwd * jnp.einsum(
        "oxy,ixy->oi", grad_pre, state_all, preferred_element_type=jnp.float32
    )
    tile_sums = (
        grad_pre.astype(jnp.float32)
        .reshape(own_chan, tile_rows, TILE, tile_cols, TILE)
        .sum(axis=(2, 4))
    )
    bias_grad = scale_fwd * jnp.einsum("abn,oab->no", one_hot, tile_sums)
    point_grad, bias_grad = lax.psum((point_grad, bias_grad), ("gx", "gy"))
    grad_rows = (
        scale_inv * jnp.einsum("oxy,tky->tokx", grad_pre, y_inv, preferred_element_type=jnp.float32)
    ).astype(jnp.bfloat16)
    row_terms = jnp.einsum(
        "tokx,rtmx->rokm", grad_rows, inv_own, preferred_element_type=jnp.float32
    )
    row_sums = lax.psum_scatter(row_terms, "gx", scatter_dimension=2, tiled=True)
    grad_modes = lax.psum_scatter(row_sums, "gy", scatter_dimension=3, tiled=True)
    spec_grad = weight_grad(spec_all, grad_modes)
    input_terms = back_mix(weight_f, grad_modes)
    input_modes = lax.psum_scatter(input_terms, "col", scatter_dimension=1, tiled=True).astype(
        jnp.bfloat16
    )
    input_kx = lax.all_gather(input_modes, "gy", axis=3, tiled=True)
    input_all = lax.all_gather(input_kx, "gx", axis=2, tiled=True)
    grad_space = (
        scale_fwd
        * jnp.einsum("tckm,rtmx->rckx", input_all, fwd_own, preferred_element_type=jnp.float32)
    ).astype(jnp.bfloat16)
    point_back = jnp.einsum("oi,oxy->ixy", w_cols, grad_all, preferred_element_type=jnp.float32)
    spectral_back = jnp.einsum(
        "rckx,ryk->cxy", grad_space, y_fwd, preferred_element_type=jnp.float32
    )
    grad_in = (point_back + spectral_back).astype(jnp.bfloat16)
    return (act_out, grad_in, spec_grad, point_grad, bias_grad)


def solution(mesh):
    return jax.shard_map(
        on_device,
        mesh=mesh,
        in_specs=(
            P(("groups", "col"), "gx", "gy"),
            P(("groups", "gx"), "gy"),
            P(),
            P(),
            P(None, None, "col", "gx", "gy"),
            P(("groups", "col"), "gx", "gy"),
        ),
        out_specs=(
            P(("groups", "col"), "gx", "gy"),
            P(("groups", "col"), "gx", "gy"),
            P("groups", None, "col", "gx", "gy"),
            P(("groups", "col"), None),
            P("groups", "col"),
        ),
        check_vma=False,
    )
```

profile of v0, /device:TPU:0, one launch (start us, length us, event | category | flops | bytes accessed | tf_op | source)
XLA Modules:
  0.0 1171.0 jit_solution(9284038670558054245)
XLA Ops:
  7.2 2.2 cosine_convert_fusion.1
  9.5 8.4 convert_bitcast_fusion
  17.8 4.4 copy.63
  22.2 6.3 all-to-all-start
  28.9 4.9 negate_convert_fusion
  34.0 88.0 %all-to-all-done = bf16[2,16,128,512]{3,1,0,2:T(8,128)(2,1)} async-done(((bf16[2,16,128,512]{3,1,0,2:T(8,128)(2,1)}), bf16[2,16,128,512]{3,1,0,2:T(8,128)(2,1)}, u32[]{:S(2)}, u32[]{:S(2)}) %all-to-all-start) | async-done | bytes 4194336 | tf_op jit(solution)/shard_map/all_to_all | solution.py:101
  122.0 7.4 copy.198
  129.4 7.7 reshape.595
  137.2 3.5 fusion.44
  140.6 1.8 copy.163
  142.5 1.8 reshape.632
  144.3 13.8 %reduce-scatter.13.cloned.1.call-done = f32[64,1024]{1,0:T(8,128)} async-done(((f32[128,1024]{1,0:T(8,128)}), f32[64,1024]{1,0:T(8,128)}) %reduce-scatter.13.cloned.1.call-update) | async-done | bytes 262160
  160.1 3.1 all_gather.22
  164.0 6.3 fusion.15
  171.3 14.6 %all_gather.23 = bf16[2,16,32,128]{2,1,0,3:T(8,128)(2,1)S(1)} all-gather(bf16[2,16,32,64]{2,1,0,3:T(8,128)(2,1)S(1)} %copy.65), channel_id=1, replica_groups=mesh['groups'=2,'gx'=4,'gy'=2,'col'=2] {'gy'}, dimensions={3}, use_global_device_ids=true | all-gather | bytes 393216 | tf_op jit(solution)/shard_map/all_gather | solution.py:107
  185.9 1.8 copy.66
  187.7 18.7 %copy.60 = bf16[16,512,1024]{2,0,1:T(8,128)(2,1)} copy(bf16[16,512,1024]{2,1,0:T(8,128)(2,1)} %param.6) | data formatting | bytes 33554432 | tf_op args[0]
  207.6 99.5 %add.186 = f32[16,32,16,64,16]{4,3,2,1,0:T(8,128)} broadcast(f32[16,32,64]{2,1,0:T(8,128)S(1)} %copy.68), dimensions={0,1,3} | broadcast | bytes 33685504 | tf_op jit(solution)/shard_map/add | solution.py:121
  307.1 211.5 %add.187 = f32[16,512,1024]{2,1,0:T(8,128)} reshape(f32[16,32,16,64,16]{4,3,2,1,0:T(8,128)} %add.186) | data formatting | bytes 67108864 | tf_op jit(solution)/shard_map/add | solution.py:121
  520.8 2.2 multiply_convert_fusion.3
  523.0 2.5 fusion.25
  525.5 15.9 %fusion.29 = f32[16,512,1024,1]{2,0,3,1:T(8,128)} fusion(bf16[2,16,128,512]{2,3,0,1:T(8,128)(2,1)S(1)} %fusion.25, bf16[1,128,1024]{2,1,0:T(8,128)(2,1)S(1)} %get-tuple-element.60, bf16[1,128,1024]{2,1,0:T(8,128)(2,1)S(1)} %get-tuple-element.59), kind=kOutput, calls=%fused_computation.47 | convolution fusion | flops 4295229440 | bytes 38273024 | tf_op jit(solution)/shard_map/tokx,tky->oxy/dot_general | solution.py:112
  541.4 60.1 %fusion.5 = (bf16[16,512,1024]{2,0,1:T(8,128)(2,1)}, bf16[16,512,1024]{2,0,1:T(8,128)(2,1)}) fusion(bf16[16,512,1024]{2,1,0:T(8,128)(2,1)} %param.11, f32[16,512,1024]{2,1,0:T(8,128)} %add.187, f32[16,512,1024,1]{2,0,3,1:T(8,128)} %fusion.29, bf16[32,512,1024]{2,0,1:T(8,128)(2,1)} %all-gather.5.cloned.1.call-done, bf16[32,32]{1,0:T(8,128)(2,1)S(1)} %copy-done, ...), kind=kOutput, calls=%fused_computation.6 | convolution fusion | flops 671088640 | bytes 150999040 | tf_op jit(solution)/shard_map/oi,ixy->oxy/dot_general | solution.py:97
  601.5 33.5 %fusion.37 = f32[2,16,128,128]{2,3,1,0:T(8,128)S(1)} fusion(bf16[16,512,1024,1]{2,0,1,3:T(8,128)(2,1)} %bitcast.235, bf16[1,128,1024]{2,1,0:T(8,128)(2,1)S(1)} %get-tuple-element.60, bf16[1,128,1024]{2,1,0:T(8,128)(2,1)S(1)} %get-tuple-element.59, bf16[1,2,128,512]{2,3,0,1:T(8,128)(2,1)S(1)} %get-tuple-element.54, ...), kind=kOutput, calls=%fused_computation.56 | convolution fusion | flops 5374214144 | bytes 19922944 | tf_op jit(solution)/shard_map/tokx,rtmx->rokm/dot_general | solution.py:140
  634.9 2.0 copy.74
  637.0 44.0 %reduce-scatter.9.cloned.1.call-done = f32[2,16,32,128]{3,1,0,2:T(8,128)} async-done(((f32[2,16,128,128]{3,1,0,2:T(8,128)}), f32[2,16,32,128]{3,1,0,2:T(8,128)}) %reduce-scatter.9.cloned.1.call-update) | async-done | bytes 524304 | tf_op jit(solution)/shard_map/reduce_scatter | solution.py:143
  681.0 5.6 copy.165
  686.6 8.7 reshape.634
  695.4 14.0 %reduce-scatter.15.cloned.1.call-done = f32[64,1024]{1,0:T(8,128)} async-done(((f32[128,1024]{1,0:T(8,128)}), f32[64,1024]{1,0:T(8,128)}) %reduce-scatter.15.cloned.1.call-update) | async-done | bytes 262160
  709.3 3.7 reshape.635
  713.1 3.7 fusion.107
  716.8 2.3 copy.177
  719.1 2.3 copy.175
  721.5 14.4 %add_bitcast_fusion = (f32[1,32,16,32,64]{4,3,2,1,0:T(8,128)}, f32[1,32,16,32,64]{4,3,2,1,0:T(8,128)}, f32[32,64,32]{1,0,2:T(8,128)S(1)}, f32[32,64,32]{1,0,2:T(...) fusion(f32[32,64,16]{1,0,2:T(8,128)S(1)} %bitcast.241, f32[32,64,16]{1,0,2:T(8,128)S(1)} %bitcast.242, ...), kind=kLoop, calls=%fused_computation.39 | loop fusion | flops 16515072 | bytes 14417920 | tf_op jit(solution)/shard_map/stack | solution.py:80
  737.5 8.4 reduce-scatter.11.cloned.1.call-done
  747.8 14.8 %all_gather.26 = bf16[2,16,32,128]{2,1,0,3:T(8,128)(2,1)S(1)} all-gather(bf16[2,16,32,64]{2,1,0,3:T(8,128)(2,1)S(1)} %copy.75), channel_id=1, replica_groups=mesh['groups'=2,'gx'=4,'gy'=2,'col'=2] {'gy'}, dimensions={3}, use_global_device_ids=true | all-gather | bytes 393216 | tf_op jit(solution)/shard_map/all_gather | solution.py:150
  762.6 1.8 copy.76
  765.1 21.9 %copy.81 = f32[16,512,1024]{2,1,0:T(8,128)} copy(bf16[16,512,1024]{2,0,1:T(8,128)(2,1)} %get-tuple-element.39) | data formatting | bytes 50331648 | tf_op jit(solution)/shard_map/reshape | solution.py:132
  787.0 19.3 %copy.83 = bf16[16,512,1024]{2,1,0:T(8,128)(2,1)} copy(bf16[16,512,1024]{2,0,1:T(8,128)(2,1)} %get-tuple-element.40) | data formatting | bytes 33554432
  806.4 142.7 %reshape.590 = f32[16,32,16,64,16]{4,3,2,1,0:T(8,128)} reshape(f32[16,512,1024]{2,1,0:T(8,128)} %copy.81) | data formatting | bytes 67108864 | tf_op jit(solution)/shard_map/reshape | solution.py:132
  949.1 80.2 %reduce_sum.9 = bf16[16,32,64]{2,1,0:T(8,128)(2,1)S(1)} reduce(f32[16,32,16,64,16]{4,3,2,1,0:T(8,128)} %reshape.590, f32[]{:T(128)} %constant.92.clone.1), dimensions={2,4}, to_apply=%region_5.6 | reduce | flops 8355840 | bytes 33619972 | tf_op jit(solution)/shard_map/reduce_sum | solution.py:133
  1029.5 18.6 %fusion.45 = f32[16,32]{1,0:T(8,128)S(1)} fusion(bf16[16,512,1024]{2,0,1:T(8,128)(2,1)} %get-tuple-element.39, bf16[32,512,1024]{2,0,1:T(8,128)(2,1)} %all-gather.5.cloned.1.call-done), kind=kOutput, calls=%fused_computation.62 | convolution fusion | flops 536871424 | bytes 50333696 | tf_op jit(solution)/shard_map/oxy,ixy->oi/dot_general | solution.py:127
  1048.1 37.7 %all-reduce = (f32[16,32]{1,0:T(8,128)}, f32[8,16]{1,0:T(8,128)}) all-reduce(f32[16,32]{1,0:T(8,128)S(1)} %fusion.45, f32[8,16]{1,0:T(8,128)S(1)} %fusion.46), channel_id=1, replica_groups=mesh['groups'=2,'gx'=4,'gy'=2,'col'=2] {'gx','gy'}, use_global_device_ids=true, to_apply=%region_4.5 | all-reduce | flops 640 | bytes 5120 | tf_op jit(solution)/shard_map/psum | solution.py:136
  1085.8 12.3 %pad_maximum_fusion = f32[2,32,16,32,64]{4,3,2,1,0:T(8,128)} fusion(f32[1,32,16,32,64]{4,3,2,1,0:T(8,128)} %get-tuple-element.44, f32[1,32,16,32,64]{4,3,2,1,0:T(8,128)} %get-tuple-element.43), kind=kLoop, calls=%fused_computation.14 | loop fusion | flops 2097152 | bytes 16777216 | tf_op jit(solution)/shard_map/stack | solution.py:80
  1098.2 2.5 fusion.26
  1100.7 15.9 %fusion.27 = f32[16,512,1024,1]{2,0,3,1:T(8,128)} fusion(bf16[2,16,128,512]{2,3,0,1:T(8,128)(2,1)S(1)} %fusion.26, bf16[1,1024,128]{1,2,0:T(8,128)(2,1)S(1)} %copy-done.8, bf16[1,1024,128]{1,2,0:T(8,128)(2,1)S(1)} %copy-done.6), kind=kOutput, calls=%fused_computation.45 | convolution fusion | flops 4295229440 | bytes 38273024 | tf_op jit(solution)/shard_map/rckx,ryk->cxy/dot_general | solution.py:157
  1116.6 28.6 %fusion.6 = bf16[16,512,1024]{2,0,1:T(8,128)(2,1)} fusion(f32[16,512,1024,1]{2,0,3,1:T(8,128)} %fusion.27, bf16[32,512,1024]{2,0,1:T(8,128)(2,1)} %all-gather.9.cloned.1.call-done, bf16[32,32]{1,0:T(8,128)(2,1)S(1)} %copy-done, s32[]{:T(128)S(6)} %select_n.118), kind=kOutput, calls=%fused_computation.8 | convolution fusion | flops 553648128 | bytes 83888128 | tf_op jit(solution)/shard_map/oi,oxy->ixy/dot_general | solution.py:156
  1145.2 18.7 %copy.84 = bf16[16,512,1024]{2,1,0:T(8,128)(2,1)} copy(bf16[16,512,1024]{2,0,1:T(8,128)(2,1)} %fusion.6) | data formatting | bytes 33554432
  (78 shorter events, 12.0 us)
Async XLA Ops:
  7.2 534.2 %copy-start = (bf16[32,32]{1,0:T(8,128)(2,1)S(1)}, bf16[32,32]{1,0:T(8,128)(2,1)}, u32[]{:S(2)}) copy-start(bf16[32,32]{1,0:T(8,128)(2,1)} %param.9) | copy-start | bytes 6148
  7.2 2.3 copy-start.11
  9.4 8.4 copy-start.5
  9.4 8.4 copy-start.7
  22.2 99.7 %all-to-all-start = ((bf16[2,16,128,512]{3,1,0,2:T(8,128)(2,1)}), bf16[2,16,128,512]{3,1,0,2:T(8,128)(2,1)}, u32[]{:S(2)}, u32[]{:S(2)}) async-start(bf16[2,16,128,512]{3,1,0,2:T(8,128)(2,1)} %copy.63), calls=%async_computation | async-start | bytes 8388608 | tf_op jit(solution)/shard_map/all_to_all | solution.py:101
  28.6 129.6 %reduce-scatter.13.cloned.1.call-start = ((), (), s32[]{:S(2)}) async-start(), calls=%async_computation.11 | async-start | bytes 786432
  28.9 4.9 copy-start.15
  144.2 378.7 %all-gather.7.cloned.1.call-start = ((), (), s32[]{:S(2)}) async-start(), calls=%async_computation.6 | async-start | bytes 1310720 | tf_op jit(solution)/shard_map/all_gather | solution.py:108
  163.2 0.8 copy-start.1
  163.2 7.1 copy-start.3
  187.7 353.7 %all-gather.5.cloned.1.call-start = ((), (), s32[]{:S(2)}) async-start(), calls=%async_computation.5 | async-start | bytes 50331648 | tf_op jit(solution)/shard_map/all_gather | solution.py:94
  206.5 0.7 copy-start.13
  206.5 0.7 copy-start.17
  206.5 474.5 %reduce-scatter.9.cloned.1.call-start = ((), (), s32[]{:S(2)}) async-start(), calls=%async_computation.8 | async-start | bytes 2621440 | tf_op jit(solution)/shard_map/reduce_scatter | solution.py:143
  307.1 211.5 %copy-start.16 = (s32[128]{0:T(128)S(1)}, s32[128]{0:T(128)}, u32[]{:S(2)}) copy-start(s32[128]{0:T(128)} %copy-done.15) | copy-start | bytes 1540
  307.1 213.7 %copy-start.12 = (s32[1024]{0:T(1024)S(1)}, s32[1024]{0:T(1024)}, u32[]{:S(2)}) copy-start(s32[1024]{0:T(1024)} %copy-done.11) | copy-start | bytes 12292
  636.9 72.4 %reduce-scatter.15.cloned.1.call-start = ((), (), s32[]{:S(2)}) async-start(), calls=%async_computation.12 | async-start | bytes 786432
  686.6 34.9 %copy-start.2 = (f32[32,64,32]{1,0,2:T(8,128)S(1)}, f32[32,64,32]{1,0,2:T(8,128)}, u32[]{:S(2)}) copy-start(f32[32,64,32]{1,0,2:T(8,128)} %copy-done.1) | copy-start | bytes 786436
  686.6 34.9 %copy-start.4 = (f32[32,64,32]{1,0,2:T(8,128)S(1)}, f32[32,64,32]{1,0,2:T(8,128)}, u32[]{:S(2)}) copy-start(f32[32,64,32]{1,0,2:T(8,128)} %copy-done.3) | copy-start | bytes 786436
  695.3 50.6 %reduce-scatter.11.cloned.1.call-start = ((), (), s32[]{:S(2)}) async-start(), calls=%async_computation.9 | async-start | bytes 1572864 | tf_op jit(solution)/shard_map/reduce_scatter | solution.py:147
  737.2 361.0 %all-gather.11.cloned.1.call-start = ((), (), s32[]{:S(2)}) async-start(), calls=%async_computation.10 | async-start | bytes 1310720 | tf_op jit(solution)/shard_map/all_gather | solution.py:151
  764.4 352.2 %all-gather.9.cloned.1.call-start = ((), (), s32[]{:S(2)}) async-start(), calls=%async_computation.7 | async-start | bytes 50331648 | tf_op jit(solution)/shard_map/all_gather | solution.py:126
  949.1 80.2 %copy-start.14 = (s32[32,64]{1,0:T(8,128)S(1)}, s32[32,64]{1,0:T(8,128)}, u32[]{:S(2)}) copy-start(s32[32,64]{1,0:T(8,128)} %param.7) | copy-start | bytes 24580
  1085.8 12.3 %copy-start.9 = (bf16[1,2,128,512]{2,3,1,0:T(8,128)(2,1)S(1)}, bf16[1,2,128,512]{2,3,1,0:T(8,128)(2,1)}, u32[]{:S(2)}) copy-start(bf16[1,2,128,512]{2,3,1,0:T(8,128)(2,1)} %get-tuple-element.53) | copy-start | bytes 786436
  1085.8 12.3 %copy-start.10 = (bf16[1,2,128,512]{2,3,1,0:T(8,128)(2,1)S(1)}, bf16[1,2,128,512]{2,3,1,0:T(8,128)(2,1)}, u32[]{:S(2)}) copy-start(bf16[1,2,128,512]{2,3,1,0:T(8,128)(2,1)} %get-tuple-element.58) | copy-start | bytes 786436
  1085.8 14.9 %copy-start.6 = (bf16[1,1024,128]{1,2,0:T(8,128)(2,1)S(1)}, bf16[1,1024,128]{1,2,0:T(8,128)(2,1)}, u32[]{:S(2)}) copy-start(bf16[1,1024,128]{1,2,0:T(8,128)(2,1)} %copy-done.5) | copy-start | bytes 786436
  1085.8 14.9 %copy-start.8 = (bf16[1,1024,128]{1,2,0:T(8,128)(2,1)S(1)}, bf16[1,1024,128]{1,2,0:T(8,128)(2,1)}, u32[]{:S(2)}) copy-start(bf16[1,1024,128]{1,2,0:T(8,128)(2,1)} %copy-done.7) | copy-start | bytes 786436
Sparse Core Ops, SparseCore 0:
  144.4 13.7 reduce-scatter.12
  187.8 27.9 all-gather.6
  218.0 50.7 all-gather.4
  637.1 43.8 reduce-scatter.8
  695.4 13.8 reduce-scatter.14
  737.3 8.5 reduce-scatter.10
  764.5 29.1 all-gather.10
  795.8 50.7 all-gather.8
where the time goes:
time: 1190 us; the launch traced here: 1170 us
  local copies, waits for them, and re-layouts  592 us (50%)
  matrix products  190 us (16%)
  waiting for transfers between devices  169 us (14%)
  other arithmetic  127 us (11%)
  blocking collectives  70.2 us (6%)
  between operations  14.8 us (1%)
    add x2, local copies, waits for them, and re-layouts, on_device(): summed + tile_bias[:, :, None, :, None]  311 us
    reshape x2, local copies, waits for them, and re-layouts, on_device(): tile_sums = grad_pre.astype(jnp.float32).reshape(own_chan, tile_rows, TIL...  165 us
    all_to_all x1, waiting for transfers between devices, on_device(): lax.all_to_all(row_spec, 'gx', split_axis=2, concat_axis=3, tiled=True)  88 us
    unnamed x49, local copies, waits for them, and re-layouts  86.4 us
    reduce_sum x1, other arithmetic, on_device(): tile_sums = grad_pre.astype(jnp.float32).reshape(own_chan, tile_rows, TIL...  80.2 us
    dot_general x1, matrix products, on_device(): jnp.einsum('oi,ixy->oxy', w_rows, state_all, preferred_element_type=jnp.f...  60.1 us
    reduce_scatter x1, waiting for transfers between devices, on_device(): lax.psum_scatter(row_terms, 'gx', scatter_dimension=2, tiled=True)  44 us
    psum x1, blocking collectives, on_device(): point_grad, bias_grad = lax.psum((point_grad, bias_grad), ('gx', 'gy'))  37.7 us
  transfers between devices with their start and end apart: 9, of which 5 were waited for; matrix products, arithmetic and copies ran while one was open for 57% of the time, Pallas kernels for 0%

commit v1 on v0

v1 whole, which is shorter than its diff:
```python
import functools
import math

import jax
import jax.numpy as jnp
import numpy as np
from jax import lax
from jax.experimental import pallas as pl
from jax.experimental.pallas import tpu as pltpu
from jax.sharding import PartitionSpec as P

TILE = 16
NCLASS = 8
VMEM_BYTES = 44 * 1024 * 1024
MANY = 16

inv_root_two = 0.7071067811865476
inv_root_tau = 0.3989422804014327

f32 = jnp.float32
bf16 = jnp.bfloat16


def dot_nn(a, b):
    return lax.dot_general(a, b, (((1,), (0,)), ((), ())), preferred_element_type=f32)


def dot_nt(a, b):
    return lax.dot_general(a, b, (((1,), (1,)), ((), ())), preferred_element_type=f32)


def dot_tn(a, b):
    return lax.dot_general(a, b, (((0,), (0,)), ((), ())), preferred_element_type=f32)


def params():
    return pltpu.CompilerParams(vmem_limit_bytes=VMEM_BYTES)


def y_table(n_y, m_y, own_k, offset, length, first):
    freq = np.arange(2 * m_y) % m_y
    turns = (freq[:, None] * np.arange(n_y)[None, :]) % n_y * (2.0 * math.pi / n_y)
    whole = np.stack([np.cos(turns), -np.sin(turns)]).astype(bf16)
    own = lax.dynamic_slice(jnp.asarray(whole), (0, first * own_k, offset), (2, m_y, length))
    return own.reshape(2 * m_y, length)


def x_table(n_x, m_x, own_m, offset, length, first):
    freq = np.arange(m_x)
    signed = np.where(freq < m_x // 2, freq, freq - m_x)
    turns = (np.arange(n_x)[:, None] * signed[None, :]) % n_x * (2.0 * math.pi / n_x)
    cos_part = np.cos(turns).reshape(n_x, m_x // own_m, 1, own_m)
    sin_part = np.sin(turns).reshape(n_x, m_x // own_m, 1, own_m)
    real_row = np.concatenate([cos_part, -sin_part], axis=2).reshape(n_x, 2 * m_x)
    imag_row = np.concatenate([sin_part, cos_part], axis=2).reshape(n_x, 2 * m_x)
    whole = np.stack([real_row, imag_row]).astype(bf16)
    whole = np.concatenate([whole, whole], axis=2)
    return lax.dynamic_slice(
        jnp.asarray(whole), (0, offset, first * 2 * own_m), (2, length, 2 * m_x)
    )


def steps_of(sizes):
    return [(a, b) for a in range(sizes[0]) for b in range(sizes[1])]


def pairs_of(sizes, a, b, sign):
    n_gx, n_gy = sizes
    return [
        (g * n_gy + h, ((g + sign * a) % n_gx) * n_gy + (h + sign * b) % n_gy)
        for g in range(n_gx)
        for h in range(n_gy)
    ]


def turn(stacked, sizes, sign):
    n_gx, n_gy = sizes
    grid = stacked.reshape((n_gx, n_gy) + stacked.shape[1:])
    grid = jnp.roll(grid, sign * lax.axis_index("gx"), axis=0)
    grid = jnp.roll(grid, sign * lax.axis_index("gy"), axis=1)
    return grid.reshape(stacked.shape)


def flip(stacked, sizes):
    n_gx, n_gy = sizes
    order = [((-a) % n_gx) * n_gy + (-b) % n_gy for a, b in steps_of(sizes)]
    return stacked[np.array(order)]


def scatter_chunks(chunks, sizes):
    if len(chunks) == 1 and chunks[0].shape[0] > 1:
        placed = turn(chunks[0], sizes, 1)
        arrived = lax.all_to_all(placed, ("gx", "gy"), 0, 0, tiled=True)
        return arrived.astype(f32).sum(axis=0)
    total = None
    arrived = [chunks[0][0]]
    for (a, b), chunk in list(zip(steps_of(sizes), chunks))[1:]:
        arrived.append(lax.ppermute(chunk[0], ("gx", "gy"), pairs_of(sizes, a, b, 1)))
    for piece in arrived:
        total = piece.astype(f32) if total is None else total + piece.astype(f32)
    return total


def gather_chunks(own, sizes):
    if sizes[0] * sizes[1] > MANY:
        stacked = lax.all_gather(own, ("gx", "gy"), axis=0, tiled=False)
        return [turn(stacked, sizes, -1)]
    return [own[None]] + [
        lax.ppermute(own, ("gx", "gy"), pairs_of(sizes, a, b, -1))[None] for a, b in steps_of(sizes)[1:]
    ]


def sum_over_grid(value, sizes):
    if sizes[0] * sizes[1] > MANY:
        return lax.psum(value, ("gx", "gy"))
    total = value
    for a in range(1, sizes[0]):
        pairs = [(g, (g + a) % sizes[0]) for g in range(sizes[0])]
        total = total + lax.ppermute(value, "gx", pairs)
    value = total
    for b in range(1, sizes[1]):
        pairs = [(h, (h + b) % sizes[1]) for h in range(sizes[1])]
        total = total + lax.ppermute(value, "gy", pairs)
    return total


def chunk_shapes(sizes, channels, own_k, lanes):
    count = sizes[0] * sizes[1]
    lengths = [count] if count > MANY else [1] * count
    return [(length, channels, own_k, lanes) for length in lengths]


def chunk_specs(shapes, at=lambda c: c):
    return [
        pl.BlockSpec((s[0], 1) + s[2:], lambda c: (0, at(c), 0, 0)) for s in shapes
    ]


def put_chunks(refs, value, sizes):
    n_gx, n_gy = sizes
    own_k, lanes = value.shape[0] // n_gx, value.shape[1] // n_gy
    per_ref = refs[0].shape[0]
    for place, (a, b) in enumerate(steps_of(sizes)):
        piece = value[a * own_k : (a + 1) * own_k, b * lanes : (b + 1) * lanes]
        refs[place // per_ref][place % per_ref, 0] = piece.astype(bf16)


def take_chunks(refs, sizes):
    n_gx, n_gy = sizes
    per_ref = refs[0].shape[0]

    def chunk(a, b):
        place = a * n_gy + b
        return refs[place // per_ref][place % per_ref, 0].astype(f32)

    rows = [jnp.concatenate([chunk(a, b) for b in range(n_gy)], axis=1) for a in range(n_gx)]
    return jnp.concatenate(rows, axis=0).astype(bf16)


def forward_kernel(sizes, state_ref, y_ref, x_ref, *out_refs):
    half = y_ref.shape[0] // 2
    rows = dot_nt(y_ref[...], state_ref[0]).astype(bf16)
    terms = dot_nn(rows[:half], x_ref[0]) + dot_nn(rows[half:], x_ref[1])
    put_chunks(out_refs, terms, sizes)


def table_specs(y_tab, x_tab):
    return [
        pl.BlockSpec(y_tab.shape, lambda c: (0, 0)),
        pl.BlockSpec(x_tab.shape, lambda c: (0, 0, 0)),
    ]


def forward_modes(state, y_tab, x_tab, sizes, own_k):
    channels, n_rows, n_cols = state.shape
    shapes = chunk_shapes(sizes, channels, own_k, x_tab.shape[2] // sizes[1])
    return pl.pallas_call(
        functools.partial(forward_kernel, sizes),
        grid=(channels,),
        in_specs=[pl.BlockSpec((1, n_rows, n_cols), lambda c: (c, 0, 0))] + table_specs(y_tab, x_tab),
        out_specs=chunk_specs(shapes),
        out_shape=[jax.ShapeDtypeStruct(s, bf16) for s in shapes],
        compiler_params=params(),
        name="forward_modes",
    )(state, y_tab, x_tab)


def gelu_parts(v):
    size = jnp.abs(v)
    bell = jnp.exp2(v * v * (-0.5 * math.log2(math.e)))
    t = 1.0 / (1.0 + (0.3275911 * inv_root_two) * size)
    series = 0.5 * 1.061405429
    for coefficient in (-1.453152027, 1.421413741, -0.284496736, 0.254829592):
        series = series * t + 0.5 * coefficient
    tail = series * t * bell
    cdf = jnp.where(v < 0.0, tail, 1.0 - tail)
    return v * cdf, cdf + v * bell * inv_root_tau


def middle_kernel(sizes, n_chunks, row_step, mix_ref, out_grad_ref, y_ref, x_ref, *refs):
    mode_refs, (act_ref, pre_ref), out_refs = refs[:n_chunks], refs[n_chunks : n_chunks + 2], refs[n_chunks + 2 :]
    modes = take_chunks(mode_refs, sizes)
    n_rows = mix_ref.shape[1]
    half = y_ref.shape[0] // 2
    real_rows = dot_nt(x_ref[0], modes).astype(bf16)
    imag_rows = dot_nt(x_ref[1], modes).astype(bf16)
    space = jnp.concatenate([real_rows, imag_rows], axis=1)
    back = []
    for start in range(0, n_rows, row_step):
        rows = slice(start, start + row_step)
        v = dot_nn(space[rows], y_ref[...]) + mix_ref[0, rows].astype(f32)
        act, slope = gelu_parts(v)
        act_ref[0, rows] = act.astype(bf16)
        pre = (out_grad_ref[0, rows].astype(f32) * slope).astype(bf16)
        pre_ref[0, rows] = pre
        back.append(dot_nt(pre, y_ref[...]).astype(bf16))
    back = jnp.concatenate(back, axis=0)
    terms = dot_tn(back[:, :half], x_ref[0]) + dot_tn(back[:, half:], x_ref[1])
    put_chunks(out_refs, terms, sizes)


def middle(mix, out_grad, y_tab, x_tab, modes, sizes):
    channels, n_rows, n_cols = mix.shape
    field = pl.BlockSpec((1, n_rows, n_cols), lambda c: (c, 0, 0))
    shapes = [m.shape for m in modes]
    results = pl.pallas_call(
        functools.partial(middle_kernel, sizes, len(modes), min(128, n_rows)),
        grid=(channels,),
        in_specs=[field, field] + table_specs(y_tab, x_tab) + chunk_specs(shapes),
        out_specs=[field, field] + chunk_specs(shapes),
        out_shape=[jax.ShapeDtypeStruct(mix.shape, bf16)] * 2 + [jax.ShapeDtypeStruct(s, bf16) for s in shapes],
        compiler_params=params(),
        name="middle",
    )(mix, out_grad, y_tab, x_tab, *modes)
    return results[0], results[1], list(results[2:])


def last_kernel(sizes, point_ref, y_ref, x_ref, *refs):
    modes = take_chunks(refs[:-1], sizes)
    real_rows = dot_nt(x_ref[0], modes).astype(bf16)
    imag_rows = dot_nt(x_ref[1], modes).astype(bf16)
    space = jnp.concatenate([real_rows, imag_rows], axis=1)
    refs[-1][0] = (dot_nn(space, y_ref[...]) + point_ref[0].astype(f32)).astype(bf16)


def last(point_back, y_tab, x_tab, modes, sizes):
    channels, n_rows, n_cols = point_back.shape
    field = pl.BlockSpec((1, n_rows, n_cols), lambda c: (c, 0, 0))
    return pl.pallas_call(
        functools.partial(last_kernel, sizes),
        grid=(channels,),
        in_specs=[field] + table_specs(y_tab, x_tab) + chunk_specs([m.shape for m in modes]),
        out_specs=field,
        out_shape=jax.ShapeDtypeStruct(point_back.shape, bf16),
        compiler_params=params(),
        name="last",
    )(point_back, y_tab, x_tab, *modes)


def spread(weight):
    n_o, n_i = weight.shape
    same = jnp.eye(TILE, dtype=weight.dtype)
    return (weight[:, None, :, None] * same[None, :, None, :]).reshape(n_o * TILE, n_i * TILE)


def point_kernel(n_fields, with_bias, *refs):
    fields, weights = refs[:n_fields], refs[n_fields : 2 * n_fields]
    out_ref = refs[-1]
    channels, n_rows, n_cols = out_ref.shape
    for tile in range(n_rows // TILE):
        rows = slice(tile * TILE, (tile + 1) * TILE)
        total = None
        for field, weight in zip(fields, weights):
            term = dot_nn(weight[...], field[:, rows].reshape(channels * TILE, n_cols))
            total = term if total is None else total + term
        total = total.reshape(channels, TILE, n_cols)
        if with_bias:
            total = total + refs[2 * n_fields][tile][:, None, :]
        out_ref[:, rows] = total.astype(bf16)


def point_map(fields, weights, bias=None):
    channels, n_rows, n_cols = fields[0].shape
    step = min(32, n_rows)
    field = pl.BlockSpec((channels, step, n_cols), lambda r: (0, r, 0))
    in_specs = [field] * len(fields) + [pl.BlockSpec(w.shape, lambda r: (0, 0)) for w in weights]
    extra = []
    if bias is not None:
        in_specs.append(pl.BlockSpec((step // TILE, channels, n_cols), lambda r: (r, 0, 0)))
        extra.append(bias)
    return pl.pallas_call(
        functools.partial(point_kernel, len(fields), bias is not None),
        grid=(n_rows // step,),
        in_specs=in_specs,
        out_specs=field,
        out_shape=jax.ShapeDtypeStruct(fields[0].shape, bf16),
        compiler_params=params(),
        name="point_map",
    )(*fields, *weights, *extra)


def sums_kernel(n_fields, pre_ref, class_ref, *refs):
    fields, outs, bias_ref = refs[:n_fields], refs[n_fields : 2 * n_fields], refs[2 * n_fields]
    channels, n_rows, n_cols = pre_ref.shape

    @pl.when(pl.program_id(0) == 0)
    def _():
        for out in outs:
            out[...] = jnp.zeros_like(out)
        bias_ref[...] = jnp.zeros_like(bias_ref)

    for tile in range(n_rows // TILE):
        rows = slice(tile * TILE, (tile + 1) * TILE)
        pre = pre_ref[:, rows].reshape(channels * TILE, n_cols)
        for field, out in zip(fields, outs):
            out[...] += dot_nt(pre, field[:, rows].reshape(channels * TILE, n_cols))
        bias_ref[...] += dot_nt(pre, class_ref[tile])


def cell_sums(pre, fields, classes):
    channels, n_rows, n_cols = pre.shape
    step = min(32, n_rows)
    field = pl.BlockSpec((channels, step, n_cols), lambda r: (0, r, 0))
    square = channels * TILE
    return pl.pallas_call(
        functools.partial(sums_kernel, len(fields)),
        grid=(n_rows // step,),
        in_specs=[field, pl.BlockSpec((step // TILE, NCLASS, n_cols), lambda r: (r, 0, 0))]
        + [field] * len(fields),
        out_specs=[pl.BlockSpec((square, square), lambda r: (0, 0))] * len(fields)
        + [pl.BlockSpec((square, NCLASS), lambda r: (0, 0))],
        out_shape=[jax.ShapeDtypeStruct((square, square), f32)] * len(fields)
        + [jax.ShapeDtypeStruct((square, NCLASS), f32)],
        compiler_params=params(),
        name="cell_sums",
    )(pre, classes, *fields)


def swap_halves(value):
    half = value.shape[-1] // 2
    return jnp.concatenate([value[..., half:], value[..., :half]], axis=-1)


def on_device(n_gx, n_gy, state_in, tile_class, class_bias, w_point, spec_weight, grad_out):
    sizes = (n_gx, n_gy)
    own_chan, n_rows, n_cols = state_in.shape
    own_k, own_m = spec_weight.shape[3:]
    m_y, m_x = own_k * n_gx, own_m * n_gy
    n_x, n_y = n_rows * n_gx, n_cols * n_gy
    gx_index = lax.axis_index("gx")
    gy_index = lax.axis_index("gy")
    col_index = lax.axis_index("col")
    scale_fwd = 1.0 / math.sqrt(n_x * n_y)
    scale_inv = 1.0 / math.sqrt(2.0 * m_x * m_y)
    other = [(0, 1), (1, 0)]

    state_other = lax.ppermute(state_in, "col", other)
    y_tab = y_table(n_y, m_y, own_k, gy_index * n_cols, n_cols, gx_index)
    x_tab = x_table(n_x, m_x, own_m, gx_index * n_rows, n_rows, gy_index)
    k_weight = jnp.where(
        (jnp.arange(own_k) + gx_index * own_k) == 0, scale_inv, 2.0 * scale_inv
    ).astype(f32)[None, :, None]

    terms = forward_modes(state_in, y_tab, x_tab, sizes, own_k)
    spectrum = (scatter_chunks(terms, sizes) * scale_fwd).astype(bf16)
    spectrum_other = lax.ppermute(spectrum, "col", other)

    w_real = jnp.concatenate([spec_weight[0], spec_weight[0]], axis=-1)
    w_imag = jnp.concatenate([-spec_weight[1], spec_weight[1]], axis=-1)

    first = col_index == 0
    spec_all = jnp.concatenate(
        [jnp.where(first, spectrum, spectrum_other), jnp.where(first, spectrum_other, spectrum)], axis=0
    ).astype(f32)
    mixed = jnp.sum(
        w_real.astype(f32) * spec_all[:, None] + w_imag.astype(f32) * swap_halves(spec_all)[:, None], axis=0
    )
    mixed_all = gather_chunks((mixed * k_weight).astype(bf16), sizes)

    w_rows = lax.dynamic_slice_in_dim(w_point, col_index * own_chan, own_chan, 0)
    w_cols = lax.dynamic_slice_in_dim(w_point, col_index * own_chan, own_chan, 1)
    own_cols = lax.dynamic_slice_in_dim(w_rows, col_index * own_chan, own_chan, 1)
    other_cols = lax.dynamic_slice_in_dim(w_rows, (1 - col_index) * own_chan, own_chan, 1)
    other_rows = lax.dynamic_slice_in_dim(w_cols, (1 - col_index) * own_chan, own_chan, 0)
    tile_rows, tile_cols = tile_class.shape
    one_hot = (tile_class[:, None, :] == jnp.arange(NCLASS, dtype=jnp.int32)[None, :, None]).astype(f32)
    widen = jnp.asarray(np.repeat(np.eye(tile_cols), TILE, axis=1).astype(np.float32))
    bias_own = lax.dynamic_slice_in_dim(class_bias, col_index * own_chan, own_chan, 1)
    high = lax.Precision.HIGHEST
    tile_bias = jnp.sum(one_hot[:, :, None, :] * bias_own[None, :, :, None], axis=1)
    bias = jnp.dot(tile_bias.reshape(tile_rows * own_chan, tile_cols), widen, precision=high)
    bias = bias.reshape(tile_rows, own_chan, n_cols)
    classes = jnp.dot(
        one_hot.astype(bf16).reshape(tile_rows * NCLASS, tile_cols), widen.astype(bf16), preferred_element_type=f32
    )
    classes = classes.astype(bf16).reshape(tile_rows, NCLASS, n_cols)
    mix = point_map([state_in, state_other], [spread(own_cols), spread(other_cols)], bias)

    act_out, grad_pre, back_terms = middle(mix, grad_out, y_tab, x_tab, mixed_all, sizes)
    pre_other = lax.ppermute(grad_pre, "col", other)
    grad_modes = scatter_chunks(back_terms, sizes) * k_weight

    input_terms = jnp.sum(
        w_real.astype(f32) * grad_modes[None] - w_imag.astype(f32) * swap_halves(grad_modes)[None], axis=1
    )
    lower, upper = input_terms[:own_chan], input_terms[own_chan:]
    input_modes = jnp.where(first, lower, upper) + lax.ppermute(jnp.where(first, upper, lower), "col", other)
    input_all = gather_chunks((input_modes * scale_fwd).astype(bf16), sizes)

    s_real, s_imag = spec_all[:, None, :, :own_m], spec_all[:, None, :, own_m:]
    g_real, g_imag = grad_modes[None, :, :, :own_m], grad_modes[None, :, :, own_m:]
    grad_spec = jnp.stack([g_real * s_real + g_imag * s_imag, g_imag * s_real - g_real * s_imag])

    own_square, other_square, bias_sums = cell_sums(grad_pre, [state_in, state_other], classes)

    def trace(square):
        parts = square.reshape(own_chan, TILE, own_chan, TILE)
        return jnp.sum(parts * jnp.eye(TILE, dtype=f32)[None, :, None, :], axis=(1, 3))

    sums = jnp.concatenate(
        [trace(own_square), trace(other_square), bias_sums.reshape(own_chan, TILE, NCLASS).sum(axis=1)], axis=1
    )
    sums = sum_over_grid(sums * scale_fwd, sizes)
    own_part, other_part = sums[:, :own_chan], sums[:, own_chan : 2 * own_chan]
    grad_point = jnp.where(
        col_index == 0,
        jnp.concatenate([own_part, other_part], axis=1),
        jnp.concatenate([other_part, own_part], axis=1),
    )
    grad_bias = sums[:, 2 * own_chan :].T

    own_rows = lax.dynamic_slice_in_dim(w_cols, col_index * own_chan, own_chan, 0)
    point_back = point_map([grad_pre, pre_other], [spread(own_rows.T), spread(other_rows.T)])
    grad_in = last(point_back, y_tab, x_tab, input_all, sizes)
    return (act_out, grad_in, grad_spec, grad_point, grad_bias)


def solution(mesh):
    return jax.shard_map(
        functools.partial(on_device, mesh.shape["gx"], mesh.shape["gy"]),
        mesh=mesh,
        in_specs=(
            P(("groups", "col"), "gx", "gy"),
            P(("groups", "gx"), "gy"),
            P(),
            P(),
            P(None, None, "col", "gx", "gy"),
            P(("groups", "col"), "gx", "gy"),
        ),
        out_specs=(
            P(("groups", "col"), "gx", "gy"),
            P(("groups", "col"), "gx", "gy"),
            P("groups", None, "col", "gx", "gy"),
            P(("groups", "col"), None),
            P("groups", "col"),
        ),
        check_vma=False,
    )
```

time: 1190 us -> 311 us (0.26); the launches traced: 1170 us -> 309 us
  local copies, waits for them, and re-layouts: 592 us -> 24.1 us
  matrix products: 190 us -> 2.11 us
  Pallas kernels: 0 us -> 162 us
  waiting for transfers between devices: 169 us -> 18.7 us
  other arithmetic: 127 us -> 47.4 us
  blocking collectives: 70.2 us -> 0 us
  starting transfers between devices: 7.28 us -> 54.2 us
  between operations: 14.8 us -> 1.05 us
    add x2 -> x0, local copies, waits for them, and re-layouts: 311 us -> none  [on_device(): summed + tile_bias[:, :, None, :, None]]
    dot_general x12 -> x2, matrix products: 190 us -> 2.11 us  [the longest x1 1.78 us: on_device(): jnp.dot(tile_bias.reshape(tile_rows * own_chan, tile_cols), widen, precis...]
    pallas_call x0 -> x6, Pallas kernels: none -> 162 us  [the longest x2 50.5 us: point_map(): pl.pallas_call(functools.partial(point_kernel, len(fields), bias is not N...]
    reshape x2, local copies, waits for them, and re-layouts: 165 us -> 4 us  [trace(): parts = square.reshape(own_chan, TILE, own_chan, TILE)]
    all_to_all x1 -> x0, waiting for transfers between devices: 88 us -> none  [on_device(): lax.all_to_all(row_spec, 'gx', split_axis=2, concat_axis=3, tiled=True)]
    unnamed x49 -> x27, local copies, waits for them, and re-layouts: 86.4 us -> 1.52 us
    reduce_sum x1 -> x5, other arithmetic: 80.2 us -> 20.1 us  [the longest x1 8.72 us: on_device(): jnp.sum(w_real.astype(f32) * grad_modes[None] - w_imag.astype(f32) * swap...]
    ppermute x0 -> x36, starting transfers between devices: none -> 54.2 us  [the longest x14 26.4 us: gather_chunks(): lax.ppermute(own, ('gx', 'gy'), pairs_of(sizes, a, b, -1))[None]]
  transfers between devices with their start and end apart: 9 -> 36, of which waited for: 5 -> 9; matrix products, arithmetic and copies ran while one was open for 57% -> 24% of each run, Pallas kernels for 0% -> 30%
where the time goes in v1:
time: 311 us; the launch traced here: 309 us
  Pallas kernels  162 us (52%)
  starting transfers between devices  54.2 us (17%)
  other arithmetic  47.4 us (15%)
  local copies, waits for them, and re-layouts  24.1 us (8%)
  waiting for transfers between devices  18.7 us (6%)
    pallas_call x2, Pallas kernels, point_map(): pl.pallas_call(functools.partial(point_kernel, len(fields), bias is not N...  50.5 us
    pallas_call x1, Pallas kernels, middle(): pl.pallas_call(functools.partial(middle_kernel, sizes, len(modes), min(12...  48.5 us
    ppermute x14, starting transfers between devices, gather_chunks(): lax.ppermute(own, ('gx', 'gy'), pairs_of(sizes, a, b, -1))[None]  26.4 us
    pallas_call x1, Pallas kernels, cell_sums(): pl.pallas_call(functools.partial(sums_kernel, len(fields)), grid=(n_rows...  25.2 us
    ppermute x14, starting transfers between devices, scatter_chunks(): lax.ppermute(chunk[0], ('gx', 'gy'), pairs_of(sizes, a, b, 1))  22.5 us
    pallas_call x1, Pallas kernels, last(): pl.pallas_call(functools.partial(last_kernel, sizes), grid=(channels,), i...  20.3 us
    pallas_call x1, Pallas kernels, forward_modes(): pl.pallas_call(functools.partial(forward_kernel, sizes), grid=(channels,)...  17 us
    ppermute x14, waiting for transfers between devices, scatter_chunks(): lax.ppermute(chunk[0], ('gx', 'gy'), pairs_of(sizes, a, b, 1))  15.9 us
  transfers between devices with their start and end apart: 36, of which 9 were waited for; matrix products, arithmetic and copies ran while one was open for 24% of the time, Pallas kernels for 30%

profile of v1, /device:TPU:0, one launch (start us, length us, event | category | flops | bytes accessed | tf_op | source)
XLA Modules:
  0.0 309.2 jit_solution(14002356581969622254)
XLA Ops:
  1.2 1.1 constant_dynamic-slice_fusion.x_ref
  2.3 1.1 constant_dynamic-slice_fusion.1
  3.4 17.0 %forward_modes.1 = (bf16[1,16,32,128]{3,2,1,0:T(8,128)(2,1)S(1)}, bf16[1,16,32,128]{3,2,1,0:T(8,128)(2,1)S(1)}, bf16[1,16,32,128]{3,2,1,0:T(8,128)(2,1)S(1)}, bf...) custom-call(bf16[16,512,1024]{2,1,0:T(8,128)(2,1)} %refs_0_.3, ...), custom_call_target="tpu_custom_call" | custom-call | tf_op jit(solution)/shard_map/forward_modes/pallas_call | solution.py:177
  20.4 2.6 collective-permute-start.1
  23.0 1.6 collective-permute-start.2
  24.5 1.5 collective-permute-start.3
  27.4 2.3 broadcast_multiply_fusion
  29.7 4.7 %fusion.26 = bf16[32,16,32,64]{3,2,1,0:T(8,128)(2,1)} fusion(bf16[2,32,16,32,64]{4,3,2,1,0:T(8,128)(2,1)} %param.13), kind=kLoop, calls=%fused_computation.70 | loop fusion | flops 1048576 | bytes 4194304 | tf_op jit(solution)/shard_map/neg | solution.py:369
  34.4 6.6 %slice_bitcast_fusion = (bf16[32,16,32,64]{3,2,1,0:T(8,128)(2,1)}, bf16[32,16,32,64]{3,2,1,0:T(8,128)(2,1)}) fusion(bf16[2,32,16,32,64]{4,3,2,1,0:T(8,128)(2,1)} %param.13), kind=kLoop, calls=%fused_computation.13 | loop fusion | bytes 8388608 | tf_op jit(solution)/shard_map/squeeze | solution.py:369
  41.0 2.9 collective-permute-start.5
  43.9 2.3 collective-permute-start.6
  46.5 5.3 %collective-permute-done.5 = bf16[16,32,128]{2,1,0:T(8,128)(2,1)S(1)} collective-permute-done((bf16[16,32,128]{2,1,0:T(8,128)(2,1)S(1)}, bf16[16,32,128]{2,1,0:T(8,128)(2,1)S(1)}, u32[]{:S(2)}, u32[]{:S(2)}) %collective-permute-start.5) | collective-permute-done | bytes 131104 | tf_op jit(solution)/shard_map/ppermute | solution.py:98
  52.1 1.4 collective-permute-done.7
  54.1 1.1 collective-permute-done.8
  56.5 8.3 %fusion.1 = f32[16,32,128]{2,1,0:T(8,128)S(1)} fusion(f32[32,32,128]{2,1,0:T(8,128)S(1)} %pad_maximum_fusion.3, f32[32,32,128]{2,1,0:T(8,128)S(1)} %maximum_convert_fusion, bf16[32,16,32,64]{3,2,1,0:T(8,128)(2,1)} %get-tuple-element.70, bf16[32,16,32,64]{3,2,1,0:T(8,128)(2,1)} %get-tuple-element.69, bf16[32,16,32,64]{3,2,1,0:T(8,128)(2,1)S(1)} %copy-done.2), kind=kLoop, calls=%fused_computation.6 | loop fusion | flops 25100288 | bytes 7602176 | tf_op jit(solution)/shard_map/reduce_sum | solution.py:375
  65.6 4.3 %collective-permute-start.15 = (bf16[16,32,128]{2,1,0:T(8,128)(2,1)}, bf16[16,32,128]{2,1,0:T(8,128)(2,1)S(1)}, u32[]{:S(2)}, u32[]{:S(2)}) collective-permute-start(bf16[16,32,128]{2,1,0:T(8,128)(2,1)} %multiply_convert_fusion.1), channel_id=1, source_target_pairs={{0,6},{2,4},{4,10},{6,8},{8,14},{10,12},{12,2},{14,0},{1,7},{3,5},... | collective-permute-start | bytes 393224 | tf_op jit(solution)/shard_map/ppermute | solution.py:109
  69.8 1.8 fusion.30.refs_4_
  71.6 2.2 mul.271.refs_3_
  73.9 2.2 mul.267.refs_2_
  76.1 2.6 collective-permute-start.13
  79.1 4.7 %collective-permute-start.11 = (bf16[16,32,128]{2,1,0:T(8,128)(2,1)}, bf16[16,32,128]{2,1,0:T(8,128)(2,1)S(1)}, u32[]{:S(2)}, u32[]{:S(2)}) collective-permute-start(bf16[16,32,128]{2,1,0:T(8,128)(2,1)} %multiply_convert_fusion.1), channel_id=1, source_target_pairs={{0,14},{2,12},{4,2},{6,0},{8,6},{10,4},{12,10},{14,8},{1,15},{3,13... | collective-permute-start | bytes 393224 | tf_op jit(solution)/shard_map/ppermute | solution.py:109
  85.7 25.3 %point_map.2.mix_ref = bf16[16,512,1024]{2,1,0:T(8,128)(2,1)} custom-call(bf16[16,512,1024]{2,1,0:T(8,128)(2,1)} %refs_0_.3, bf16[16,512,1024]{2,1,0:T(8,128)(2,1)} %collective-permute-done.refs_1_, bf16[256,256]{1,0:T(8,128)(2,1)S(1)} %mul.267.refs_2_, bf16[256,256]{1,0:T(8,128)(2,1)S(1)} %mul.271.refs_3_, f32[32,16,1024]{2,1,0:T(8,128)S(1)} %fusion.30.refs_4_), custom_call_target="tpu_custom_call" | custom-call | tf_op jit(solution)/shard_map/point_map/pallas_call | solution.py:291
  111.0 48.5 %middle.1 = (bf16[16,512,1024]{2,1,0:T(8,128)(2,1)}, bf16[16,512,1024]{2,1,0:T(8,128)(2,1)}, bf16[1,16,32,128]{3,2,1,0:T(8,128)(2,1)S(1)}, bf16[1,16,32,128]{3,2...) custom-call(bf16[16,512,1024]{2,1,0:T(8,128)(2,1)} %point_map.2.mix_, ...), custom_call_target="tpu_custom_call" | custom-call | tf_op jit(solution)/shard_map/middle/pallas_call | solution.py:226
  160.0 25.2 %cell_sums.1 = (f32[256,256]{1,0:T(8,128)S(1)}, f32[256,256]{1,0:T(8,128)S(1)}, f32[256,8]{1,0:T(8,128)S(1)}) custom-call(bf16[16,512,1024]{2,1,0:T(8,128)(2,1)} %get-tuple-element.35.refs_0_.pre_ref, bf16[32,8,1024]{2,1,0:T(8,128)(2,1)S(1)} %fusion.4.class_ref, bf16[16,512,1024]{2,1,0:T(8,128)(2,1)} %refs_0_.3, ...), custom_call_target="tpu_custom_call" | custom-call | tf_op jit(solution)/shard_map/cell_sums/pallas_call | solution.py:325
  185.2 2.0 reshape.133
  187.2 2.0 reshape.134
  189.2 2.7 multiply_reduce_fusion.1
  192.0 2.0 collective-permute-start.34
  194.0 1.3 collective-permute-start.33
  195.3 1.5 collective-permute-start.17
  196.8 2.2 collective-permute-start.18
  199.5 1.3 collective-permute-done.32
  200.8 1.5 collective-permute-start.35
  202.3 2.2 mul.293.refs_3_
  204.5 2.2 mul.290.refs_2_
  207.3 2.4 collective-permute-start.21
  209.7 2.6 collective-permute-start.22
  213.0 5.2 %collective-permute-done.20 = bf16[16,32,128]{2,1,0:T(8,128)(2,1)S(1)} collective-permute-done((bf16[16,32,128]{2,1,0:T(8,128)(2,1)S(1)}, bf16[16,32,128]{2,1,0:T(8,128)(2,1)S(1)}, u32[]{:S(2)}, u32[]{:S(2)}) %collective-permute-start.20) | collective-permute-done | bytes 131104 | tf_op jit(solution)/shard_map/ppermute | solution.py:98
  218.2 2.9 collective-permute-done.21
  222.3 8.7 %fusion.3 = f32[32,32,128]{2,1,0:T(8,128)S(1)} fusion(f32[16,32,128]{2,1,0:T(8,128)S(1)} %pad_maximum_fusion.4, f32[16,32,128]{2,1,0:T(8,128)S(1)} %fusion.11, bf16[32,16,32,64]{3,2,1,0:T(8,128)(2,1)} %get-tuple-element.70, bf16[32,16,32,64]{3,2,1,0:T(8,128)(2,1)} %get-tuple-element.69, bf16[32,16,32,64]{3,2,1,0:T(8,128)(2,1)} %fusion.26), kind=kLoop, calls=%fused_computation.8 | loop fusion | flops 25034752 | bytes 7340032 | tf_op jit(solution)/shard_map/reduce_sum | solution.py:403
  234.7 5.3 %collective-permute-start.31 = (bf16[16,32,128]{2,1,0:T(8,128)(2,1)S(1)}, bf16[16,32,128]{2,1,0:T(8,128)(2,1)S(1)}, u32[]{:S(2)}, u32[]{:S(2)}) collective-permute-start(bf16[16,32,128]{2,1,0:T(8,128)(2,1)S(1)} %multiply_convert_fusion), channel_id=1, source_target_pairs={{0,6},{2,4},{4,10},{6,8},{8,14},{10,12},{12,2},{14,0},{1,7},{3,5},... | collective-permute-start | bytes 393224 | tf_op jit(solution)/shard_map/ppermute | solution.py:109
  240.0 5.2 %multiply_add_fusion = (f32[1,32,16,32,64]{4,3,2,1,0:T(8,128)S(1)}, f32[1,32,16,32,64]{4,3,2,1,0:T(8,128)}) fusion(f32[32,32,64]{2,1,0:T(8,128)S(1)} %copy-done.4, f32[16,32,64]{2,1,0:T(8,128)S(1)} %get-tuple-element.75, f32[32,32,64]{2,1,0:T(8,128)S(1)} %copy-done.6, f32[16,32,64]{2,1,0:T(8,128)S(1)} %get-tuple-element.76), kind=kLoop, calls=%fused_computation.10 | loop fusion | flops 6291456 | bytes 9175040 | tf_op jit(solution)/shard_map/add | solution.py:412
  245.2 1.8 collective-permute-start.29
  246.9 1.2 collective-permute-start.28
  248.1 4.7 %collective-permute-start.27 = (bf16[16,32,128]{2,1,0:T(8,128)(2,1)S(1)}, bf16[16,32,128]{2,1,0:T(8,128)(2,1)S(1)}, u32[]{:S(2)}, u32[]{:S(2)}) collective-permute-start(bf16[16,32,128]{2,1,0:T(8,128)(2,1)S(1)} %multiply_convert_fusion), channel_id=1, source_target_pairs={{0,14},{2,12},{4,2},{6,0},{8,6},{10,4},{12,10},{14,8},{1,15},{3,13... | collective-permute-start | bytes 393224 | tf_op jit(solution)/shard_map/ppermute | solution.py:109
  253.4 10.1 %pad_maximum_fusion = f32[2,32,16,32,64]{4,3,2,1,0:T(8,128)} fusion(f32[1,32,16,32,64]{4,3,2,1,0:T(8,128)} %get-tuple-element.72, f32[1,32,16,32,64]{4,3,2,1,0:T(8,128)S(1)} %get-tuple-element.71), kind=kLoop, calls=%fused_computation | loop fusion | flops 2097152 | bytes 16777216 | tf_op jit(solution)/shard_map/stack | solution.py:412
  263.6 25.2 %point_map.3.point_ref = bf16[16,512,1024]{2,1,0:T(8,128)(2,1)} custom-call(bf16[16,512,1024]{2,1,0:T(8,128)(2,1)} %get-tuple-element.35.refs_0_.pre_ref, bf16[16,512,1024]{2,1,0:T(8,128)(2,1)} %collective-permute-done.16.refs_1_, bf16[256,256]{1,0:T(8,128)(2,1)S(1)} %mul.290.refs_2_, bf16[256,256]{1,0:T(8,128)(2,1)S(1)} %mul.293.refs_3_), custom_call_target="tpu_custom_call" | custom-call | tf_op jit(solution)/shard_map/point_map/pallas_call | solution.py:291
  288.9 20.3 %last.1 = bf16[16,512,1024]{2,1,0:T(8,128)(2,1)} custom-call(bf16[16,512,1024]{2,1,0:T(8,128)(2,1)} %point_map.3.point_ref, bf16[256,1024]{1,0:T(8,128)(2,1)S(1)} %bitcast.74, bf16[2,512,256]{2,1,0:T(8,128)(2,1)S(1)} %constant_dynamic-slice_fusion.x_ref, bf16[1,16,32,128]{3,2,1,0:T(8,128)(2,1)S(1)} %bitcast.75, bf16[1,16,32,128]{3,2,1,0:T(8,128)(2,1)S(1)} %bitcast.88, ...), custom_call_target="tpu_custom_call" | custom-call | tf_op jit(solution)/shard_map/last/pallas_call | solution.py:249
  (105 shorter events, 15.0 us)
Async XLA Ops:
  0.6 45.8 %copy-start = (f32[8,32]{1,0:T(8,128)S(1)}, f32[8,32]{1,0:T(8,128)}, u32[]{:S(2)}) copy-start(f32[8,32]{1,0:T(8,128)} %param.11) | copy-start | bytes 3076
  0.6 83.3 %collective-permute-start = (bf16[16,512,1024]{2,1,0:T(8,128)(2,1)}, bf16[16,512,1024]{2,1,0:T(8,128)(2,1)}, u32[]{:S(2)}, u32[]{:S(2)}) collective-permute-start(bf16[16,512,1024]{2,1,0:T(8,128)(2,1)} %refs_0_.3), channel_id=1, source_target_pairs={{0,1},{1,0},{2,3},{3,2},{4,5},{5,4},{6,7},{7,6},{8,9},{9,8},{10,11... | collective-permute-start | bytes 50331656 | tf_op jit(solution)/shard_map/ppermute | solution.py:357
  3.4 23.8 %copy-start.12 = (bf16[32,32]{1,0:T(8,128)(2,1)S(1)}, bf16[32,32]{1,0:T(8,128)(2,1)}, u32[]{:S(2)}) copy-start(bf16[32,32]{1,0:T(8,128)(2,1)} %param.12) | copy-start | bytes 6148
  20.4 20.7 %collective-permute-start.1 = (bf16[16,32,128]{2,1,0:T(8,128)(2,1)S(1)}, bf16[16,32,128]{2,1,0:T(8,128)(2,1)S(1)}, u32[]{:S(2)}, u32[]{:S(2)}) collective-permute-start(bf16[16,32,128]{2,1,0:T(8,128)(2,1)S(1)} %bitcast.102), channel_id=1, source_target_pairs={{0,2},{2,0},{4,6},{6,4},{8,10},{10,8},{12,14},{14,12},{1,3},{3,1},... | collective-permute-start | bytes 393224 | tf_op jit(solution)/shard_map/ppermute | solution.py:98
  23.0 21.0 %collective-permute-start.2 = (bf16[16,32,128]{2,1,0:T(8,128)(2,1)S(1)}, bf16[16,32,128]{2,1,0:T(8,128)(2,1)S(1)}, u32[]{:S(2)}, u32[]{:S(2)}) collective-permute-start(bf16[16,32,128]{2,1,0:T(8,128)(2,1)S(1)} %bitcast.101), channel_id=1, source_target_pairs={{0,4},{2,6},{4,8},{6,10},{8,12},{10,14},{12,0},{14,2},{1,5},{3,7},... | collective-permute-start | bytes 393224 | tf_op jit(solution)/shard_map/ppermute | solution.py:98
  24.5 21.6 %collective-permute-start.3 = (bf16[16,32,128]{2,1,0:T(8,128)(2,1)S(1)}, bf16[16,32,128]{2,1,0:T(8,128)(2,1)S(1)}, u32[]{:S(2)}, u32[]{:S(2)}) collective-permute-start(bf16[16,32,128]{2,1,0:T(8,128)(2,1)S(1)} %bitcast.100), channel_id=1, source_target_pairs={{0,6},{2,4},{4,10},{6,8},{8,14},{10,12},{12,2},{14,0},{1,7},{3,5},... | collective-permute-start | bytes 393224 | tf_op jit(solution)/shard_map/ppermute | solution.py:98
  26.1 20.4 %collective-permute-start.4 = (bf16[16,32,128]{2,1,0:T(8,128)(2,1)S(1)}, bf16[16,32,128]{2,1,0:T(8,128)(2,1)S(1)}, u32[]{:S(2)}, u32[]{:S(2)}) collective-permute-start(bf16[16,32,128]{2,1,0:T(8,128)(2,1)S(1)} %bitcast.99), channel_id=1, source_target_pairs={{0,8},{2,10},{4,12},{6,14},{8,0},{10,2},{12,4},{14,6},{1,9},{3,11}... | collective-permute-start | bytes 393224 | tf_op jit(solution)/shard_map/ppermute | solution.py:98
  34.4 6.7 %copy-start.10 = (s32[32,64]{1,0:T(8,128)S(1)}, s32[32,64]{1,0:T(8,128)}, u32[]{:S(2)}) copy-start(s32[32,64]{1,0:T(8,128)} %param.10) | copy-start | bytes 24580
  41.0 10.8 %collective-permute-start.5 = (bf16[16,32,128]{2,1,0:T(8,128)(2,1)S(1)}, bf16[16,32,128]{2,1,0:T(8,128)(2,1)S(1)}, u32[]{:S(2)}, u32[]{:S(2)}) collective-permute-start(bf16[16,32,128]{2,1,0:T(8,128)(2,1)S(1)} %bitcast.98), channel_id=1, source_target_pairs={{0,10},{2,8},{4,14},{6,12},{8,2},{10,0},{12,6},{14,4},{1,11},{3,9}... | collective-permute-start | bytes 393224 | tf_op jit(solution)/shard_map/ppermute | solution.py:98
  43.9 8.2 %collective-permute-start.6 = (bf16[16,32,128]{2,1,0:T(8,128)(2,1)S(1)}, bf16[16,32,128]{2,1,0:T(8,128)(2,1)S(1)}, u32[]{:S(2)}, u32[]{:S(2)}) collective-permute-start(bf16[16,32,128]{2,1,0:T(8,128)(2,1)S(1)} %bitcast.96), channel_id=1, source_target_pairs={{0,12},{2,14},{4,0},{6,2},{8,4},{10,6},{12,8},{14,10},{1,13},{3,15... | collective-permute-start | bytes 393224 | tf_op jit(solution)/shard_map/ppermute | solution.py:98
  46.2 7.4 %collective-permute-start.7 = (bf16[16,32,128]{2,1,0:T(8,128)(2,1)S(1)}, bf16[16,32,128]{2,1,0:T(8,128)(2,1)S(1)}, u32[]{:S(2)}, u32[]{:S(2)}) collective-permute-start(bf16[16,32,128]{2,1,0:T(8,128)(2,1)S(1)} %bitcast.95), channel_id=1, source_target_pairs={{0,14},{2,12},{4,2},{6,0},{8,6},{10,4},{12,10},{14,8},{1,15},{3,13... | collective-permute-start | bytes 393224 | tf_op jit(solution)/shard_map/ppermute | solution.py:98
  46.4 10.0 %copy-start.2 = (bf16[32,16,32,64]{3,2,1,0:T(8,128)(2,1)S(1)}, bf16[32,16,32,64]{3,2,1,0:T(8,128)(2,1)}, u32[]{:S(2)}) copy-start(bf16[32,16,32,64]{3,2,1,0:T(8,128)(2,1)} %fusion.26) | copy-start | bytes 6291460
  53.7 1.4 collective-permute-start.8
  55.4 1.0 copy-start.5
  55.4 14.4 %copy-start.8 = (f32[64,1024,1]{1,0,2:T(8,128)S(1)}, f32[64,1024,1]{1,0,2:T(8,128)}, u32[]{:S(2)}) copy-start(f32[64,1024,1]{1,0,2:T(8,128)} %constant.91) | copy-start | bytes 786436
  64.8 6.8 %copy-start.7 = (f32[16,32,128]{2,1,0:T(8,128)}, f32[16,32,128]{2,1,0:T(8,128)S(1)}, u32[]{:S(2)}) copy-start(f32[16,32,128]{2,1,0:T(8,128)S(1)} %fusion.1) | copy-start | bytes 786436
  65.6 13.5 %collective-permute-start.15 = (bf16[16,32,128]{2,1,0:T(8,128)(2,1)}, bf16[16,32,128]{2,1,0:T(8,128)(2,1)S(1)}, u32[]{:S(2)}, u32[]{:S(2)}) collective-permute-start(bf16[16,32,128]{2,1,0:T(8,128)(2,1)} %multiply_convert_fusion.1), channel_id=1, source_target_pairs={{0,6},{2,4},{4,10},{6,8},{8,14},{10,12},{12,2},{14,0},{1,7},{3,5},... | collective-permute-start | bytes 393224 | tf_op jit(solution)/shard_map/ppermute | solution.py:109
  69.8 14.0 %collective-permute-start.14 = (bf16[16,32,128]{2,1,0:T(8,128)(2,1)}, bf16[16,32,128]{2,1,0:T(8,128)(2,1)}, u32[]{:S(2)}, u32[]{:S(2)}) collective-permute-start(bf16[16,32,128]{2,1,0:T(8,128)(2,1)} %multiply_convert_fusion.1), channel_id=1, source_target_pairs={{0,4},{2,6},{4,8},{6,10},{8,12},{10,14},{12,0},{14,2},{1,5},{3,7},... | collective-permute-start | bytes 393224 | tf_op jit(solution)/shard_map/ppermute | solution.py:109
  76.1 34.9 %collective-permute-start.13 = (bf16[16,32,128]{2,1,0:T(8,128)(2,1)}, bf16[16,32,128]{2,1,0:T(8,128)(2,1)S(1)}, u32[]{:S(2)}, u32[]{:S(2)}) collective-permute-start(bf16[16,32,128]{2,1,0:T(8,128)(2,1)} %multiply_convert_fusion.1), channel_id=1, source_target_pairs={{0,10},{2,8},{4,14},{6,12},{8,2},{10,0},{12,6},{14,4},{1,11},{3,9}... | collective-permute-start | bytes 393224 | tf_op jit(solution)/shard_map/ppermute | solution.py:109
  78.7 32.3 %collective-permute-start.12 = (bf16[16,32,128]{2,1,0:T(8,128)(2,1)}, bf16[16,32,128]{2,1,0:T(8,128)(2,1)S(1)}, u32[]{:S(2)}, u32[]{:S(2)}) collective-permute-start(bf16[16,32,128]{2,1,0:T(8,128)(2,1)} %multiply_convert_fusion.1), channel_id=1, source_target_pairs={{0,8},{2,10},{4,12},{6,14},{8,0},{10,2},{12,4},{14,6},{1,9},{3,11}... | collective-permute-start | bytes 393224 | tf_op jit(solution)/shard_map/ppermute | solution.py:109
  79.1 31.9 %collective-permute-start.11 = (bf16[16,32,128]{2,1,0:T(8,128)(2,1)}, bf16[16,32,128]{2,1,0:T(8,128)(2,1)S(1)}, u32[]{:S(2)}, u32[]{:S(2)}) collective-permute-start(bf16[16,32,128]{2,1,0:T(8,128)(2,1)} %multiply_convert_fusion.1), channel_id=1, source_target_pairs={{0,14},{2,12},{4,2},{6,0},{8,6},{10,4},{12,10},{14,8},{1,15},{3,13... | collective-permute-start | bytes 393224 | tf_op jit(solution)/shard_map/ppermute | solution.py:109
  83.8 27.2 %collective-permute-start.10 = (bf16[16,32,128]{2,1,0:T(8,128)(2,1)}, bf16[16,32,128]{2,1,0:T(8,128)(2,1)S(1)}, u32[]{:S(2)}, u32[]{:S(2)}) collective-permute-start(bf16[16,32,128]{2,1,0:T(8,128)(2,1)} %multiply_convert_fusion.1), channel_id=1, source_target_pairs={{0,12},{2,14},{4,0},{6,2},{8,4},{10,6},{12,8},{14,10},{1,13},{3,15... | collective-permute-start | bytes 393224 | tf_op jit(solution)/shard_map/ppermute | solution.py:109
  84.0 27.0 %collective-permute-start.9 = (bf16[16,32,128]{2,1,0:T(8,128)(2,1)}, bf16[16,32,128]{2,1,0:T(8,128)(2,1)S(1)}, u32[]{:S(2)}, u32[]{:S(2)}) collective-permute-start(bf16[16,32,128]{2,1,0:T(8,128)(2,1)} %multiply_convert_fusion.1), channel_id=1, source_target_pairs={{0,2},{2,0},{4,6},{6,4},{8,10},{10,8},{12,14},{14,12},{1,3},{3,1},... | collective-permute-start | bytes 393224 | tf_op jit(solution)/shard_map/ppermute | solution.py:109
  111.0 48.6 %copy-start.9 = (bf16[64,1024]{1,0:T(8,128)(2,1)S(1)}, bf16[64,1024]{1,0:T(8,128)(2,1)}, u32[]{:S(2)}) copy-start(bf16[64,1024]{1,0:T(8,128)(2,1)} %constant.90) | copy-start | bytes 393220
  111.0 48.6 %copy-start.11 = (s32[32,64]{1,0:T(8,128)S(1)}, s32[32,64]{1,0:T(8,128)}, u32[]{:S(2)}) copy-start(s32[32,64]{1,0:T(8,128)} %param.10) | copy-start | bytes 24580
  159.5 93.3 %collective-permute-start.16 = (bf16[16,512,1024]{2,1,0:T(8,128)(2,1)}, bf16[16,512,1024]{2,1,0:T(8,128)(2,1)}, u32[]{:S(2)}, u32[]{:S(2)}) collective-permute-start(bf16[16,512,1024]{2,1,0:T(8,128)(2,1)} %get-tuple-element.35.refs_0_.pre_ref), channel_id=1, source_target_pairs={{0,1},{1,0},{2,3},{3,2},{4,5},{5,4},{6,7},{7,6},{8,9},{9,8},{10,11... | collective-permute-start | bytes 50331656 | tf_op jit(solution)/shard_map/ppermute | solution.py:400
  192.0 4.7 %collective-permute-start.34 = (f32[16,40]{1,0:T(8,128)S(1)}, f32[16,40]{1,0:T(8,128)S(1)}, u32[]{:S(2)}, u32[]{:S(2)}) collective-permute-start(f32[16,40]{1,0:T(8,128)S(1)} %maximum_multiply_fusion), channel_id=1, source_target_pairs={{0,12},{4,0},{8,4},{12,8},{1,13},{5,1},{9,5},{13,9},{2,14},{6,2},{... | collective-permute-start | bytes 7688 | tf_op jit(solution)/shard_map/ppermute | solution.py:119
  194.0 5.0 %collective-permute-start.33 = (f32[16,40]{1,0:T(8,128)S(1)}, f32[16,40]{1,0:T(8,128)S(1)}, u32[]{:S(2)}, u32[]{:S(2)}) collective-permute-start(f32[16,40]{1,0:T(8,128)S(1)} %maximum_multiply_fusion), channel_id=1, source_target_pairs={{0,8},{4,12},{8,0},{12,4},{1,9},{5,13},{9,1},{13,5},{2,10},{6,14},... | collective-permute-start | bytes 7688 | tf_op jit(solution)/shard_map/ppermute | solution.py:119
  195.3 5.4 %collective-permute-start.32 = (f32[16,40]{1,0:T(8,128)S(1)}, f32[16,40]{1,0:T(8,128)S(1)}, u32[]{:S(2)}, u32[]{:S(2)}) collective-permute-start(f32[16,40]{1,0:T(8,128)S(1)} %maximum_multiply_fusion), channel_id=1, source_target_pairs={{0,4},{4,8},{8,12},{12,0},{1,5},{5,9},{9,13},{13,1},{2,6},{6,10},{... | collective-permute-start | bytes 7688 | tf_op jit(solution)/shard_map/ppermute | solution.py:119
  195.3 12.0 %collective-permute-start.17 = (bf16[16,32,128]{2,1,0:T(8,128)(2,1)S(1)}, bf16[16,32,128]{2,1,0:T(8,128)(2,1)S(1)}, u32[]{:S(2)}, u32[]{:S(2)}) collective-permute-start(bf16[16,32,128]{2,1,0:T(8,128)(2,1)S(1)} %bitcast.97), channel_id=1, source_target_pairs={{0,2},{2,0},{4,6},{6,4},{8,10},{10,8},{12,14},{14,12},{1,3},{3,1},... | collective-permute-start | bytes 393224 | tf_op jit(solution)/shard_map/ppermute | solution.py:98
  196.8 12.9 %collective-permute-start.18 = (bf16[16,32,128]{2,1,0:T(8,128)(2,1)S(1)}, bf16[16,32,128]{2,1,0:T(8,128)(2,1)S(1)}, u32[]{:S(2)}, u32[]{:S(2)}) collective-permute-start(bf16[16,32,128]{2,1,0:T(8,128)(2,1)S(1)} %bitcast.94), channel_id=1, source_target_pairs={{0,4},{2,6},{4,8},{6,10},{8,12},{10,14},{12,0},{14,2},{1,5},{3,7},... | collective-permute-start | bytes 393224 | tf_op jit(solution)/shard_map/ppermute | solution.py:98
  199.0 13.3 %collective-permute-start.19 = (bf16[16,32,128]{2,1,0:T(8,128)(2,1)S(1)}, bf16[16,32,128]{2,1,0:T(8,128)(2,1)S(1)}, u32[]{:S(2)}, u32[]{:S(2)}) collective-permute-start(bf16[16,32,128]{2,1,0:T(8,128)(2,1)S(1)} %bitcast.93), channel_id=1, source_target_pairs={{0,6},{2,4},{4,10},{6,8},{8,14},{10,12},{12,2},{14,0},{1,7},{3,5},... | collective-permute-start | bytes 393224 | tf_op jit(solution)/shard_map/ppermute | solution.py:98
  200.8 6.0 %collective-permute-start.35 = (f32[16,40]{1,0:T(8,128)S(1)}, f32[16,40]{1,0:T(8,128)S(1)}, u32[]{:S(2)}, u32[]{:S(2)}) collective-permute-start(f32[16,40]{1,0:T(8,128)S(1)} %add_add_fusion), channel_id=1, source_target_pairs={{0,2},{2,0},{1,3},{3,1},{4,6},{6,4},{5,7},{7,5},{8,10},{10,8},{9,1... | collective-permute-start | bytes 7688 | tf_op jit(solution)/shard_map/ppermute | solution.py:123
  206.7 11.5 %collective-permute-start.20 = (bf16[16,32,128]{2,1,0:T(8,128)(2,1)S(1)}, bf16[16,32,128]{2,1,0:T(8,128)(2,1)S(1)}, u32[]{:S(2)}, u32[]{:S(2)}) collective-permute-start(bf16[16,32,128]{2,1,0:T(8,128)(2,1)S(1)} %bitcast.92), channel_id=1, source_target_pairs={{0,8},{2,10},{4,12},{6,14},{8,0},{10,2},{12,4},{14,6},{1,9},{3,11}... | collective-permute-start | bytes 393224 | tf_op jit(solution)/shard_map/ppermute | solution.py:98
  207.3 13.9 %collective-permute-start.21 = (bf16[16,32,128]{2,1,0:T(8,128)(2,1)S(1)}, bf16[16,32,128]{2,1,0:T(8,128)(2,1)S(1)}, u32[]{:S(2)}, u32[]{:S(2)}) collective-permute-start(bf16[16,32,128]{2,1,0:T(8,128)(2,1)S(1)} %bitcast.91), channel_id=1, source_target_pairs={{0,10},{2,8},{4,14},{6,12},{8,2},{10,0},{12,6},{14,4},{1,11},{3,9}... | collective-permute-start | bytes 393224 | tf_op jit(solution)/shard_map/ppermute | solution.py:98
  209.7 11.5 %collective-permute-start.22 = (bf16[16,32,128]{2,1,0:T(8,128)(2,1)S(1)}, bf16[16,32,128]{2,1,0:T(8,128)(2,1)S(1)}, u32[]{:S(2)}, u32[]{:S(2)}) collective-permute-start(bf16[16,32,128]{2,1,0:T(8,128)(2,1)S(1)} %bitcast.90), channel_id=1, source_target_pairs={{0,12},{2,14},{4,0},{6,2},{8,4},{10,6},{12,8},{14,10},{1,13},{3,15... | collective-permute-start | bytes 393224 | tf_op jit(solution)/shard_map/ppermute | solution.py:98
  212.3 9.6 %collective-permute-start.23 = (bf16[16,32,128]{2,1,0:T(8,128)(2,1)S(1)}, bf16[16,32,128]{2,1,0:T(8,128)(2,1)S(1)}, u32[]{:S(2)}, u32[]{:S(2)}) collective-permute-start(bf16[16,32,128]{2,1,0:T(8,128)(2,1)S(1)} %bitcast.89), channel_id=1, source_target_pairs={{0,14},{2,12},{4,2},{6,0},{8,6},{10,4},{12,10},{14,8},{1,15},{3,13... | collective-permute-start | bytes 393224 | tf_op jit(solution)/shard_map/ppermute | solution.py:98
  222.0 18.0 %copy-start.4 = (f32[32,32,64]{2,1,0:T(8,128)S(1)}, f32[32,32,64]{2,1,0:T(8,128)}, u32[]{:S(2)}) copy-start(f32[32,32,64]{2,1,0:T(8,128)} %copy-done.3) | copy-start | bytes 786436
  222.0 18.0 %copy-start.6 = (f32[32,32,64]{2,1,0:T(8,128)S(1)}, f32[32,32,64]{2,1,0:T(8,128)}, u32[]{:S(2)}) copy-start(f32[32,32,64]{2,1,0:T(8,128)} %copy-done.5) | copy-start | bytes 786436
  231.7 1.9 collective-permute-start.24
  234.7 13.5 %collective-permute-start.31 = (bf16[16,32,128]{2,1,0:T(8,128)(2,1)S(1)}, bf16[16,32,128]{2,1,0:T(8,128)(2,1)S(1)}, u32[]{:S(2)}, u32[]{:S(2)}) collective-permute-start(bf16[16,32,128]{2,1,0:T(8,128)(2,1)S(1)} %multiply_convert_fusion), channel_id=1, source_target_pairs={{0,6},{2,4},{4,10},{6,8},{8,14},{10,12},{12,2},{14,0},{1,7},{3,5},... | collective-permute-start | bytes 393224 | tf_op jit(solution)/shard_map/ppermute | solution.py:109
  240.0 12.8 %collective-permute-start.30 = (bf16[16,32,128]{2,1,0:T(8,128)(2,1)S(1)}, bf16[16,32,128]{2,1,0:T(8,128)(2,1)S(1)}, u32[]{:S(2)}, u32[]{:S(2)}) collective-permute-start(bf16[16,32,128]{2,1,0:T(8,128)(2,1)S(1)} %multiply_convert_fusion), channel_id=1, source_target_pairs={{0,4},{2,6},{4,8},{6,10},{8,12},{10,14},{12,0},{14,2},{1,5},{3,7},... | collective-permute-start | bytes 393224 | tf_op jit(solution)/shard_map/ppermute | solution.py:109
  245.2 43.6 %collective-permute-start.29 = (bf16[16,32,128]{2,1,0:T(8,128)(2,1)S(1)}, bf16[16,32,128]{2,1,0:T(8,128)(2,1)S(1)}, u32[]{:S(2)}, u32[]{:S(2)}) collective-permute-start(bf16[16,32,128]{2,1,0:T(8,128)(2,1)S(1)} %multiply_convert_fusion), channel_id=1, source_target_pairs={{0,10},{2,8},{4,14},{6,12},{8,2},{10,0},{12,6},{14,4},{1,11},{3,9}... | collective-permute-start | bytes 393224 | tf_op jit(solution)/shard_map/ppermute | solution.py:109
  246.9 41.9 %collective-permute-start.28 = (bf16[16,32,128]{2,1,0:T(8,128)(2,1)S(1)}, bf16[16,32,128]{2,1,0:T(8,128)(2,1)S(1)}, u32[]{:S(2)}, u32[]{:S(2)}) collective-permute-start(bf16[16,32,128]{2,1,0:T(8,128)(2,1)S(1)} %multiply_convert_fusion), channel_id=1, source_target_pairs={{0,8},{2,10},{4,12},{6,14},{8,0},{10,2},{12,4},{14,6},{1,9},{3,11}... | collective-permute-start | bytes 393224 | tf_op jit(solution)/shard_map/ppermute | solution.py:109
  248.1 40.7 %collective-permute-start.27 = (bf16[16,32,128]{2,1,0:T(8,128)(2,1)S(1)}, bf16[16,32,128]{2,1,0:T(8,128)(2,1)S(1)}, u32[]{:S(2)}, u32[]{:S(2)}) collective-permute-start(bf16[16,32,128]{2,1,0:T(8,128)(2,1)S(1)} %multiply_convert_fusion), channel_id=1, source_target_pairs={{0,14},{2,12},{4,2},{6,0},{8,6},{10,4},{12,10},{14,8},{1,15},{3,13... | collective-permute-start | bytes 393224 | tf_op jit(solution)/shard_map/ppermute | solution.py:109
  252.8 36.0 %collective-permute-start.26 = (bf16[16,32,128]{2,1,0:T(8,128)(2,1)S(1)}, bf16[16,32,128]{2,1,0:T(8,128)(2,1)S(1)}, u32[]{:S(2)}, u32[]{:S(2)}) collective-permute-start(bf16[16,32,128]{2,1,0:T(8,128)(2,1)S(1)} %multiply_convert_fusion), channel_id=1, source_target_pairs={{0,12},{2,14},{4,0},{6,2},{8,4},{10,6},{12,8},{14,10},{1,13},{3,15... | collective-permute-start | bytes 393224 | tf_op jit(solution)/shard_map/ppermute | solution.py:109
  252.8 36.0 %collective-permute-start.25 = (bf16[16,32,128]{2,1,0:T(8,128)(2,1)S(1)}, bf16[16,32,128]{2,1,0:T(8,128)(2,1)S(1)}, u32[]{:S(2)}, u32[]{:S(2)}) collective-permute-start(bf16[16,32,128]{2,1,0:T(8,128)(2,1)S(1)} %multiply_convert_fusion), channel_id=1, source_target_pairs={{0,2},{2,0},{4,6},{6,4},{8,10},{10,8},{12,14},{14,12},{1,3},{3,1},... | collective-permute-start | bytes 393224 | tf_op jit(solution)/shard_map/ppermute | solution.py:109
  288.8 20.3 %copy-start.1 = (f32[8,32]{1,0:T(8,128)S(1)}, f32[8,32]{1,0:T(8,128)}, u32[]{:S(2)}) copy-start(f32[8,32]{1,0:T(8,128)} %param.11) | copy-start | bytes 3076
  (1 other events, 0.8 us)

commit v2 on v0

v2 whole, which is shorter than its diff:
```python
import functools
import math

import jax
import jax.numpy as jnp
import numpy as np
from jax import lax
from jax.experimental import pallas as pl
from jax.experimental.pallas import tpu as pltpu
from jax.sharding import PartitionSpec as P

TILE = 16
NCLASS = 8
VMEM_BYTES = 48 * 1024 * 1024
SPLITS = 2

inv_root_two = 0.7071067811865476
inv_root_tau = 0.3989422804014327

f32 = jnp.float32
bf16 = jnp.bfloat16


def dot_nn(a, b):
    return lax.dot_general(a, b, (((1,), (0,)), ((), ())), preferred_element_type=f32)


def dot_nt(a, b):
    return lax.dot_general(a, b, (((1,), (1,)), ((), ())), preferred_element_type=f32)


def dot_tn(a, b):
    return lax.dot_general(a, b, (((0,), (0,)), ((), ())), preferred_element_type=f32)


def params():
    return pltpu.CompilerParams(vmem_limit_bytes=VMEM_BYTES)


def cost(flops, *arrays, transcendentals=0):
    size = sum(math.prod(a.shape) * jnp.dtype(a.dtype).itemsize for a in arrays)
    return pl.CostEstimate(flops=int(flops), bytes_accessed=int(size), transcendentals=int(transcendentals))


def divisor(length, limit):
    return max(d for d in range(1, limit + 1) if length % d == 0)


def y_table(n_y, m_y, offset, length):
    turns = (np.arange(m_y)[:, None] * np.arange(n_y)[None, :]) % n_y * (2.0 * math.pi / n_y)
    whole = np.concatenate([np.cos(turns), -np.sin(turns)]).astype(bf16)
    return lax.dynamic_slice_in_dim(jnp.asarray(whole), offset, length, 1)


def x_table(n_x, m_x, own_m, offset, length):
    freq = np.arange(m_x)
    signed = np.where(freq < m_x // 2, freq, freq - m_x)
    turns = (np.arange(n_x)[:, None] * signed[None, :]) % n_x * (2.0 * math.pi / n_x)
    cos_part = np.cos(turns).reshape(n_x, m_x // own_m, 1, own_m)
    sin_part = np.sin(turns).reshape(n_x, m_x // own_m, 1, own_m)
    real_row = np.concatenate([cos_part, -sin_part], axis=2).reshape(n_x, 2 * m_x)
    imag_row = np.concatenate([sin_part, cos_part], axis=2).reshape(n_x, 2 * m_x)
    whole = np.stack([real_row, imag_row]).astype(bf16)
    return lax.dynamic_slice_in_dim(jnp.asarray(whole), offset, length, 1)


def exchange(chunks):
    return lax.all_to_all(chunks, ("gx", "gy"), 0, 0, tiled=True)


def put_chunks(ref, channel, value, n_gy):
    own_k, lanes = ref.shape[2:]
    for place in range(ref.shape[0]):
        a, b = divmod(place, n_gy)
        piece = value[a * own_k : (a + 1) * own_k, b * lanes : (b + 1) * lanes]
        ref[place, channel] = piece.astype(bf16)


def take_chunks(ref, channel, n_gy):
    own_k, lanes = ref.shape[2:]
    kind = bf16 if own_k % 16 == 0 and lanes % 128 == 0 else f32
    rows = [
        jnp.concatenate([ref[a + b, channel].astype(kind) for b in range(n_gy)], axis=1)
        for a in range(0, ref.shape[0], n_gy)
    ]
    return jnp.concatenate(rows, axis=0).astype(bf16)


def rows_of_modes(modes, x_ref):
    return [dot_nt(x_ref[part], modes).astype(bf16) for part in range(2)]


def forward_kernel(n_gy, state_ref, y_ref, x_ref, out_ref):
    half = y_ref.shape[0] // 2
    for c in range(state_ref.shape[0]):
        rows = dot_nt(y_ref[...], state_ref[c]).astype(bf16)
        terms = dot_nn(rows[:half], x_ref[0]) + dot_nn(rows[half:], x_ref[1])
        put_chunks(out_ref, c, terms, n_gy)


def table_specs(y_tab, x_tab):
    return [
        pl.BlockSpec(y_tab.shape, lambda c: (0, 0)),
        pl.BlockSpec(x_tab.shape, lambda c: (0, 0, 0)),
    ]


def transform_flops(channels, y_tab, x_tab):
    n_rows, wide = x_tab.shape[1:]
    return 2 * channels * n_rows * (y_tab.shape[0] * y_tab.shape[1] + y_tab.shape[0] * wide)


def forward_modes(state, y_tab, x_tab, sizes, own_k):
    channels, n_rows, n_cols = state.shape
    out = jax.ShapeDtypeStruct((sizes[0] * sizes[1], channels, own_k, x_tab.shape[2] // sizes[1]), bf16)
    step = divisor(channels, 4)
    return pl.pallas_call(
        functools.partial(forward_kernel, sizes[1]),
        grid=(channels // step,),
        in_specs=[pl.BlockSpec((step, n_rows, n_cols), lambda c: (c, 0, 0))] + table_specs(y_tab, x_tab),
        out_specs=pl.BlockSpec((out.shape[0], step) + out.shape[2:], lambda c: (0, c, 0, 0)),
        out_shape=out,
        compiler_params=params(),
        cost_estimate=cost(transform_flops(channels, y_tab, x_tab), state, out),
        name="forward_modes",
    )(state, y_tab, x_tab)


def gelu_parts(v):
    v = v.astype(bf16)
    half = jnp.asarray(0.5, bf16)
    bell = jnp.exp2(v * v * jnp.asarray(-0.5 * math.log2(math.e), bf16)) * jnp.asarray(inv_root_tau, bf16)
    cdf = lax.erf(v * jnp.asarray(inv_root_two, bf16)).astype(bf16) * half + half
    return v * cdf, cdf + v * bell


def middle_kernel(n_gy, row_step, mix_ref, out_grad_ref, y_ref, x_ref, mode_ref, *refs):
    act_ref, pre_ref, out_ref = refs[-3:]
    n_rows = mix_ref.shape[1]
    half = y_ref.shape[0] // 2
    for c in range(mix_ref.shape[0]):
        space = jnp.concatenate(rows_of_modes(take_chunks(mode_ref, c, n_gy), x_ref), axis=1)
        back = []
        for start in range(0, n_rows, row_step):
            rows = slice(start, start + row_step)
            v = dot_nn(space[rows], y_ref[...]) + mix_ref[c, rows].astype(f32)
            act, slope = gelu_parts(v)
            act_ref[c, rows] = act
            pre = out_grad_ref[c, rows] * slope
            pre_ref[c, rows] = pre
            back.append(dot_nt(pre, y_ref[...]).astype(bf16))
        back = jnp.concatenate(back, axis=0)
        terms = dot_tn(back[:, :half], x_ref[0]) + dot_tn(back[:, half:], x_ref[1])
        put_chunks(out_ref, c, terms, n_gy)


def middle(mix, out_grad, y_tab, x_tab, modes, sizes, first=0, before=()):
    channels, n_rows, n_cols = mix.shape
    step = divisor(modes.shape[1], 2)
    skip = first // step
    field = pl.BlockSpec((step, n_rows, n_cols), lambda c: (c + skip, 0, 0))
    chunk = (modes.shape[0], step) + modes.shape[2:]
    chunks = jax.ShapeDtypeStruct((modes.shape[0], channels) + modes.shape[2:], bf16)
    flops = 2 * transform_flops(modes.shape[1], y_tab, x_tab)
    moved = jax.ShapeDtypeStruct((4 * modes.shape[1], n_rows, n_cols), bf16)
    return pl.pallas_call(
        functools.partial(middle_kernel, sizes[1], min(256, n_rows)),
        grid=(modes.shape[1] // step,),
        in_specs=[field, field]
        + table_specs(y_tab, x_tab)
        + [pl.BlockSpec(chunk, lambda c: (0, c, 0, 0))]
        + [pl.BlockSpec(memory_space=pl.ANY)] * len(before),
        out_specs=[field, field, pl.BlockSpec(chunk, lambda c: (0, c + skip, 0, 0))],
        out_shape=[jax.ShapeDtypeStruct(mix.shape, bf16)] * 2 + [chunks],
        input_output_aliases={5 + n: n for n in range(len(before))},
        compiler_params=params(),
        cost_estimate=cost(flops, moved),
        name="middle",
    )(mix, out_grad, y_tab, x_tab, modes, *before)


def last_kernel(n_gy, point_ref, y_ref, x_ref, mode_ref, out_ref):
    for c in range(point_ref.shape[0]):
        space = jnp.concatenate(rows_of_modes(take_chunks(mode_ref, c, n_gy), x_ref), axis=1)
        out_ref[c] = (dot_nn(space, y_ref[...]) + point_ref[c].astype(f32)).astype(bf16)


def last(point_back, y_tab, x_tab, modes, sizes):
    channels, n_rows, n_cols = point_back.shape
    step = divisor(channels, 4)
    field = pl.BlockSpec((step, n_rows, n_cols), lambda c: (c, 0, 0))
    return pl.pallas_call(
        functools.partial(last_kernel, sizes[1]),
        grid=(channels // step,),
        in_specs=[field]
        + table_specs(y_tab, x_tab)
        + [pl.BlockSpec((modes.shape[0], step) + modes.shape[2:], lambda c: (0, c, 0, 0))],
        out_specs=field,
        out_shape=jax.ShapeDtypeStruct(point_back.shape, bf16),
        compiler_params=params(),
        cost_estimate=cost(transform_flops(channels, y_tab, x_tab), point_back, point_back),
        name="last",
    )(point_back, y_tab, x_tab, modes)


def chooser(rows, columns, first):
    channel = lax.broadcasted_iota(jnp.int32, (rows, columns), 0) // TILE + first
    return channel == lax.broadcasted_iota(jnp.int32, (rows, columns), 1)


def same_row(rows, columns):
    return lax.broadcasted_iota(jnp.int32, (rows, columns), 0) % TILE == (
        lax.broadcasted_iota(jnp.int32, (rows, columns), 1) % TILE
    )


def spread(weight, out_first, in_first, wide, transposed):
    channels = weight.shape[0]
    picks_out = chooser(wide, channels, out_first).astype(bf16)
    picks_in = chooser(wide, channels, in_first).astype(bf16)
    half = dot_nt(picks_out, weight) if transposed else dot_nn(picks_out, weight)
    return jnp.where(same_row(wide, wide), dot_nt(half.astype(bf16), picks_in), 0.0).astype(bf16)


def point_kernel(transposed, where_ref, own_ref, other_ref, weight_ref, *refs):
    bias_ref, (out_ref, spread_ref) = refs[:-2], refs[-2:]
    channels, n_rows, n_cols = out_ref.shape
    wide = channels * TILE

    @pl.when(pl.program_id(0) == 0)
    def _():
        own = where_ref[0] * channels
        for n, first in enumerate((own, channels - own)):
            spread_ref[n] = spread(weight_ref[...], own, first, wide, transposed)

    for tile in range(n_rows // TILE):
        rows = slice(tile * TILE, (tile + 1) * TILE)
        total = dot_nn(spread_ref[0], own_ref[:, rows].reshape(wide, n_cols))
        total = total + dot_nn(spread_ref[1], other_ref[:, rows].reshape(wide, n_cols))
        total = total.reshape(channels, TILE, n_cols)
        for ref in bias_ref:
            total = total + ref[tile][:, None, :]
        out_ref[:, rows] = total.astype(bf16)


def over_rows(kernel, where, fields, others, other_specs, out_specs, out_shape, scratch, step, flops, name):
    channels, n_rows, n_cols = fields[0].shape
    field = pl.BlockSpec((channels, step, n_cols), lambda r, w: (0, r, 0))
    outs = out_shape if isinstance(out_shape, list) else [out_shape]
    return pl.pallas_call(
        kernel,
        grid_spec=pltpu.PrefetchScalarGridSpec(
            num_scalar_prefetch=1,
            grid=(n_rows // step,),
            in_specs=[field] * len(fields) + other_specs,
            out_specs=out_specs,
            scratch_shapes=scratch,
        ),
        out_shape=out_shape,
        compiler_params=params(),
        cost_estimate=cost(flops, *fields, *others, *outs),
        name=name,
    )(where, *fields, *others)


def whole_spec(array):
    return pl.BlockSpec(array.shape, lambda r, w: (0,) * array.ndim)


def row_step(n_rows, limit):
    return TILE * divisor(n_rows // TILE, limit // TILE)


def point_mixing(where, fields, weight, transposed, bias=()):
    channels, n_rows, n_cols = fields[0].shape
    step = row_step(n_rows, 128)
    wide = channels * TILE
    return over_rows(
        functools.partial(point_kernel, transposed),
        where,
        fields,
        [weight, *bias],
        [whole_spec(weight)]
        + [pl.BlockSpec((step // TILE, channels, n_cols), lambda r, w: (r, 0, 0)) for _ in bias],
        pl.BlockSpec((channels, step, n_cols), lambda r, w: (0, r, 0)),
        jax.ShapeDtypeStruct(fields[0].shape, bf16),
        [pltpu.VMEM((2, wide, wide), bf16)],
        step,
        4 * wide * wide * n_cols * (n_rows // TILE),
        "point_mixing",
    )


def sums_kernel(scale, where_ref, pre_ref, own_ref, other_ref, class_ref, out_ref, square_ref, bias_ref):
    channels, n_rows, n_cols = pre_ref.shape
    wide = channels * TILE
    step, last_step = pl.program_id(0), pl.num_programs(0) - 1

    @pl.when(step == 0)
    def _():
        square_ref[...] = jnp.zeros_like(square_ref)
        bias_ref[...] = jnp.zeros_like(bias_ref)

    for tile in range(n_rows // TILE):
        rows = slice(tile * TILE, (tile + 1) * TILE)
        pre = pre_ref[:, rows].reshape(wide, n_cols)
        square_ref[0] += dot_nt(pre, own_ref[:, rows].reshape(wide, n_cols))
        square_ref[1] += dot_nt(pre, other_ref[:, rows].reshape(wide, n_cols))
        bias_ref[...] += dot_nt(pre, class_ref[tile])

    @pl.when(step == last_step)
    def _():
        own = where_ref[0] * channels
        lanes = out_ref.shape[1]
        high = lax.Precision.HIGHEST
        total = jnp.zeros((wide, lanes), f32)
        for n, first in enumerate((own, channels - own)):
            kept = jnp.where(same_row(wide, wide), square_ref[n], 0.0)
            total = total + jnp.dot(kept, chooser(wide, lanes, first).astype(f32), precision=high)
        shift = lax.broadcasted_iota(jnp.int32, (NCLASS, lanes), 0) + 2 * channels
        shift = (shift == lax.broadcasted_iota(jnp.int32, (NCLASS, lanes), 1)).astype(f32)
        total = total + jnp.dot(bias_ref[...], shift, precision=high)
        out_ref[...] = total.reshape(channels, TILE, lanes).sum(axis=1) * scale


def cell_sums(where, pre, state_own, state_other, classes, scale):
    channels, n_rows, n_cols = pre.shape
    step = row_step(n_rows, 64)
    wide = channels * TILE
    return over_rows(
        functools.partial(sums_kernel, scale),
        where,
        [pre, state_own, state_other],
        [classes],
        [pl.BlockSpec((step // TILE, NCLASS, n_cols), lambda r, w: (r, 0, 0))],
        pl.BlockSpec((channels, 128), lambda r, w: (0, 0)),
        jax.ShapeDtypeStruct((channels, 128), f32),
        [pltpu.VMEM((2, wide, wide), f32), pltpu.VMEM((wide, NCLASS), f32)],
        step,
        4 * wide * wide * n_cols * (n_rows // TILE),
        "cell_sums",
    )


def mode_weight(where_ref, own_k, scale):
    k = where_ref[1] * own_k + lax.broadcasted_iota(jnp.int32, (own_k, 1), 0)
    return jnp.where(k == 0, scale, 2.0 * scale).astype(f32)


def swap_parts(value):
    half = value.shape[-1] // 2
    return jnp.concatenate([value[..., half:], value[..., :half]], axis=-1)


def widen_kernel(weight_ref, real_ref, imag_ref):
    real_part, imag_part = weight_ref[0], weight_ref[1]
    real_ref[...] = jnp.concatenate([real_part, real_part], axis=-1)
    imag_ref[...] = jnp.concatenate([-imag_part, imag_part], axis=-1)


def widen_weights(weight):
    n_in, n_out, own_k, own_m = weight.shape[1:]
    step = divisor(n_in, 4)
    out = jax.ShapeDtypeStruct((n_in, n_out, own_k, 2 * own_m), bf16)
    out_spec = pl.BlockSpec((step, n_out, own_k, 2 * own_m), lambda i: (i, 0, 0, 0))
    return pl.pallas_call(
        widen_kernel,
        grid=(n_in // step,),
        in_specs=[pl.BlockSpec((2, step, n_out, own_k, own_m), lambda i: (0, i, 0, 0, 0))],
        out_specs=[out_spec, out_spec],
        out_shape=[out, out],
        compiler_params=params(),
        cost_estimate=cost(0, weight, weight, out, out),
        name="widen_weights",
    )(weight)


def mix_kernel(scale, where_ref, real_ref, imag_ref, own_ref, other_ref, out_ref, spec_ref, swap_ref):
    channels, own_k, lanes = own_ref.shape

    @pl.when(pl.program_id(0) == 0)
    def _():
        own = where_ref[0] * channels
        for source, first in ((own_ref, own), (other_ref, channels - own)):
            for c in range(channels):
                value = source[c].astype(f32)
                spec_ref[first + c] = value
                swap_ref[first + c] = swap_parts(value)

    factor = mode_weight(where_ref, own_k, scale)
    for o in range(real_ref.shape[1]):
        total = jnp.zeros((own_k, lanes), f32)
        for i in range(2 * channels):
            total = total + (
                real_ref[i, o].astype(f32) * spec_ref[i] + imag_ref[i, o].astype(f32) * swap_ref[i]
            )
        value = (total * factor).astype(bf16)
        for place in range(out_ref.shape[0]):
            out_ref[place, o] = value


def mix_modes(where, w_real, w_imag, own, other, copies, scale, first, count):
    n_in, n_out, own_k, lanes = w_real.shape
    step = divisor(count, 4)
    skip = first // step
    spec = pl.BlockSpec(own.shape, lambda o, w: (0, 0, 0))
    weight = pl.BlockSpec((n_in, step, own_k, lanes), lambda o, w: (0, o + skip, 0, 0))
    return pl.pallas_call(
        functools.partial(mix_kernel, scale),
        grid_spec=pltpu.PrefetchScalarGridSpec(
            num_scalar_prefetch=1,
            grid=(count // step,),
            in_specs=[weight, weight, spec, spec],
            out_specs=pl.BlockSpec((copies, step, own_k, lanes), lambda o, w: (0, o, 0, 0)),
            scratch_shapes=[pltpu.VMEM((n_in, own_k, lanes), f32)] * 2,
        ),
        out_shape=jax.ShapeDtypeStruct((copies, count, own_k, lanes), bf16),
        compiler_params=params(),
        cost_estimate=cost(4 * n_in * count * own_k * lanes, w_real, w_imag),
        name="mix_modes",
    )(where, w_real, w_imag, own, other)


def sum_chunks(where_ref, chunk_refs, scale):
    own_k = chunk_refs[0].shape[2]
    factor = mode_weight(where_ref, own_k, scale)
    for ref in chunk_refs:
        for channel in range(ref.shape[1]):
            total = ref[0, channel].astype(f32)
            for place in range(1, ref.shape[0]):
                total = total + ref[place, channel].astype(f32)
            yield total * factor


def back_kernel(scale, scale_out, n_chunks, where_ref, real_ref, imag_ref, *refs):
    out_ref, grad_ref, swap_ref = refs[n_chunks:]

    @pl.when(pl.program_id(0) == 0)
    def _():
        for o, value in enumerate(sum_chunks(where_ref, refs[:n_chunks], scale)):
            grad_ref[o] = value
            swap_ref[o] = swap_parts(value)

    for i in range(real_ref.shape[0]):
        total = jnp.zeros(out_ref.shape[1:], f32)
        for o in range(real_ref.shape[1]):
            total = total + (
                real_ref[i, o].astype(f32) * grad_ref[o] - imag_ref[i, o].astype(f32) * swap_ref[o]
            )
        out_ref[i] = total * scale_out


def back_mix(where, w_real, w_imag, chunks, scale, scale_out):
    n_in, n_out, own_k, lanes = w_real.shape
    step = divisor(n_in // 2, 8)
    blocks = n_in // step
    half = blocks // 2
    weight = pl.BlockSpec((step, n_out, own_k, lanes), lambda i, w: ((i + (1 - w[0]) * half) % blocks, 0, 0, 0))
    return pl.pallas_call(
        functools.partial(back_kernel, scale, scale_out, len(chunks)),
        grid_spec=pltpu.PrefetchScalarGridSpec(
            num_scalar_prefetch=1,
            grid=(blocks,),
            in_specs=[weight, weight] + [pl.BlockSpec(c.shape, lambda i, w: (0, 0, 0, 0)) for c in chunks],
            out_specs=pl.BlockSpec((step, own_k, lanes), lambda i, w: (i, 0, 0)),
            scratch_shapes=[pltpu.VMEM((n_out, own_k, lanes), f32)] * 2,
        ),
        out_shape=jax.ShapeDtypeStruct((n_in, own_k, lanes), f32),
        compiler_params=params(),
        cost_estimate=cost(4 * n_in * n_out * own_k * lanes, w_real, w_imag),
        name="back_mix",
    )(where, w_real, w_imag, *chunks)


def weight_kernel(scale, n_chunks, where_ref, spec_ref, *refs):
    out_ref, real_ref, imag_ref = refs[n_chunks:]
    n_out, own_k, own_m = real_ref.shape

    @pl.when(pl.program_id(0) == 0)
    def _():
        for o, value in enumerate(sum_chunks(where_ref, refs[:n_chunks], scale)):
            real_ref[o] = value[:, :own_m]
            imag_ref[o] = value[:, own_m:]

    for i in range(out_ref.shape[1]):
        value = spec_ref[i].astype(f32)
        s_real, s_imag = value[:, :own_m], value[:, own_m:]
        for o in range(n_out):
            g_real, g_imag = real_ref[o], imag_ref[o]
            out_ref[0, i, o] = g_real * s_real + g_imag * s_imag
            out_ref[1, i, o] = g_imag * s_real - g_real * s_imag


def weight_grad(where, chunks, spec_all, n_out, scale):
    n_in, own_k, lanes = spec_all.shape
    own_m = lanes // 2
    step = divisor(n_in, 4)
    out = jax.ShapeDtypeStruct((2, n_in, n_out, own_k, own_m), f32)
    return pl.pallas_call(
        functools.partial(weight_kernel, scale, len(chunks)),
        grid_spec=pltpu.PrefetchScalarGridSpec(
            num_scalar_prefetch=1,
            grid=(n_in // step,),
            in_specs=[pl.BlockSpec((step, own_k, lanes), lambda i, w: (i, 0, 0))]
            + [pl.BlockSpec(c.shape, lambda i, w: (0, 0, 0, 0)) for c in chunks],
            out_specs=pl.BlockSpec((2, step, n_out, own_k, own_m), lambda i, w: (0, i, 0, 0, 0)),
            scratch_shapes=[pltpu.VMEM((n_out, own_k, own_m), f32)] * 2,
        ),
        out_shape=out,
        compiler_params=params(),
        cost_estimate=cost(6 * n_in * n_out * own_k * own_m, out, out),
        name="weight_grad",
    )(where, spec_all, *chunks)


def slabs_of(value, shape):
    high = lax.reduce_precision(value, 8, 7)
    middle_part = lax.reduce_precision(value - high, 8, 7)
    parts = jnp.stack([high, middle_part, value - high - middle_part]).astype(bf16).reshape(-1)
    size = math.prod(shape)
    count = -(-parts.shape[0] // size)
    return jnp.pad(parts, (0, count * size - parts.shape[0])).reshape((count,) + shape)


def sum_of_slabs(slabs, shape):
    total = slabs.astype(f32).sum(axis=0).reshape(-1)
    return total[: 3 * math.prod(shape)].reshape((3,) + shape).sum(axis=0)


def on_device(n_gx, n_gy, state_in, tile_class, class_bias, w_point, spec_weight, grad_out):
    sizes = (n_gx, n_gy)
    n_grid = n_gx * n_gy
    own_chan, n_rows, n_cols = state_in.shape
    own_k, own_m = spec_weight.shape[3:]
    m_y, m_x = own_k * n_gx, own_m * n_gy
    n_x, n_y = n_rows * n_gx, n_cols * n_gy
    gx_index = lax.axis_index("gx")
    gy_index = lax.axis_index("gy")
    col_index = lax.axis_index("col")
    scale_fwd = 1.0 / math.sqrt(n_x * n_y)
    scale_inv = 1.0 / math.sqrt(2.0 * m_x * m_y)
    other = [(0, 1), (1, 0)]
    where = jnp.stack([col_index, gx_index]).astype(jnp.int32)

    state_other = lax.ppermute(state_in, "col", other)
    y_tab = y_table(n_y, m_y, gy_index * n_cols, n_cols)
    x_tab = x_table(n_x, m_x, own_m, gx_index * n_rows, n_rows)

    w_real, w_imag = widen_weights(spec_weight)

    tile_rows, tile_cols = tile_class.shape
    one_hot = (tile_class[:, None, :] == jnp.arange(NCLASS, dtype=jnp.int32)[None, :, None]).astype(f32)
    widen = jnp.asarray(np.repeat(np.eye(tile_cols), TILE, axis=1).astype(np.float32))
    bias_own = lax.dynamic_slice_in_dim(class_bias, col_index * own_chan, own_chan, 1)
    tile_bias = jnp.sum(one_hot[:, :, None, :] * bias_own[None, :, :, None], axis=1)
    bias = jnp.dot(
        tile_bias.reshape(tile_rows * own_chan, tile_cols), widen, precision=lax.Precision.HIGHEST
    ).reshape(tile_rows, own_chan, n_cols)
    classes = jnp.dot(
        one_hot.astype(bf16).reshape(tile_rows * NCLASS, tile_cols), widen.astype(bf16), preferred_element_type=f32
    )
    classes = classes.astype(bf16).reshape(tile_rows, NCLASS, n_cols)
    mix = point_mixing(where, [state_in, state_other], w_point, False, [bias])

    terms = exchange(forward_modes(state_in, y_tab, x_tab, sizes, own_k))
    terms, mix, w_real, w_imag = lax.optimization_barrier((terms, mix, w_real, w_imag))
    spectrum = (terms.astype(f32).sum(axis=0) * scale_fwd).astype(bf16)
    spectrum_other = lax.ppermute(spectrum, "col", other)
    halves = SPLITS if own_chan % SPLITS == 0 else 1
    count = own_chan // halves
    mixed = [
        exchange(
            mix_modes(where, w_real, w_imag, spectrum, spectrum_other, n_grid, scale_inv, n * count, count)
        )
        for n in range(halves)
    ]

    done = ()
    for n in range(halves):
        done = middle(mix, grad_out, y_tab, x_tab, mixed[n], sizes, n * count, done)
    act_out, grad_pre, back_terms = done
    back_terms = [exchange(back_terms)]
    pre_other = lax.ppermute(grad_pre, "col", other)

    sums = cell_sums(where, grad_pre, state_in, state_other, classes, scale_fwd)
    sums, *back_terms = lax.optimization_barrier((sums, *back_terms))

    input_terms = back_mix(where, w_real, w_imag, back_terms, scale_inv, scale_fwd)
    input_modes = input_terms[own_chan:] + lax.ppermute(input_terms[:own_chan], "col", other)
    sent = jnp.concatenate([input_modes.astype(bf16), slabs_of(sums, input_modes.shape[1:])], axis=0)
    arrived = exchange(jnp.broadcast_to(sent[None], (n_grid,) + sent.shape))

    first = col_index == 0
    spec_all = jnp.concatenate(
        [jnp.where(first, spectrum, spectrum_other), jnp.where(first, spectrum_other, spectrum)], axis=0
    )
    grad_spec = weight_grad(where, back_terms, spec_all, own_chan, scale_inv)
    point_back = point_mixing(where, [grad_pre, pre_other], w_point, True)
    arrived, grad_spec, point_back = lax.optimization_barrier((arrived, grad_spec, point_back))

    grad_in = last(point_back, y_tab, x_tab, arrived, sizes)
    sums = sum_of_slabs(arrived[:, own_chan:], sums.shape)
    grad_point = sums[:, : 2 * own_chan]
    grad_bias = sums[:, 2 * own_chan : 2 * own_chan + NCLASS].T
    return (act_out, grad_in, grad_spec, grad_point, grad_bias)


def solution(mesh):
    return jax.shard_map(
        functools.partial(on_device, mesh.shape["gx"], mesh.shape["gy"]),
        mesh=mesh,
        in_specs=(
            P(("groups", "col"), "gx", "gy"),
            P(("groups", "gx"), "gy"),
            P(),
            P(),
            P(None, None, "col", "gx", "gy"),
            P(("groups", "col"), "gx", "gy"),
        ),
        out_specs=(
            P(("groups", "col"), "gx", "gy"),
            P(("groups", "col"), "gx", "gy"),
            P("groups", None, "col", "gx", "gy"),
            P(("groups", "col"), None),
            P("groups", "col"),
        ),
        check_vma=False,
    )
```

time: 1190 us -> 212 us (0.18); the launches traced: 1170 us -> 211 us
  local copies, waits for them, and re-layouts: 592 us -> 13.3 us
  matrix products: 190 us -> 2.11 us
  waiting for transfers between devices: 169 us -> 14.8 us
  Pallas kernels: 0 us -> 151 us
  other arithmetic: 127 us -> 1.62 us
  blocking collectives: 70.2 us -> 0 us
  starting transfers between devices: 7.28 us -> 27.2 us
  between operations: 14.8 us -> 0.86 us
    add x2 -> x0, local copies, waits for them, and re-layouts: 311 us -> none  [on_device(): summed + tile_bias[:, :, None, :, None]]
    dot_general x12 -> x2, matrix products: 190 us -> 2.11 us  [the longest x1 1.78 us: on_device(): jnp.dot(tile_bias.reshape(tile_rows * own_chan, tile_cols), widen, precis...]
    reshape x2 -> x0, local copies, waits for them, and re-layouts: 165 us -> none  [on_device(): tile_sums = grad_pre.astype(jnp.float32).reshape(own_chan, tile_rows, TIL...]
    pallas_call x0 -> x12, Pallas kernels: none -> 151 us  [the longest x3 62.3 us: over_rows(): pl.pallas_call(kernel, grid_spec=pltpu.PrefetchScalarGridSpec(num_scalar_...]
    reduce_sum x1 -> x4, other arithmetic: 80.2 us -> 0.43 us  [the longest x1 0.26 us: on_device(): jnp.sum(one_hot[:, :, None, :] * bias_own[None, :, :, None], axis=1)]
    unnamed x49 -> x25, local copies, waits for them, and re-layouts: 86.4 us -> 9.64 us
    all_to_all x1 -> x5, waiting for transfers between devices: 88 us -> 12.5 us  [exchange(): return lax.all_to_all(chunks, ('gx', 'gy'), 0, 0, tiled=True)]
    reduce_scatter x2 -> x0, waiting for transfers between devices: 52.4 us -> none  [the longest x1 44 us: on_device(): lax.psum_scatter(row_terms, 'gx', scatter_dimension=2, tiled=True)]
  transfers between devices with their start and end apart: 9 -> 9, of which waited for: 5 -> 4; matrix products, arithmetic and copies ran while one was open for 57% -> 3% of each run, Pallas kernels for 0% -> 55%
where the time goes in v2:
time: 212 us; the launch traced here: 211 us
  Pallas kernels  151 us (71%)
  starting transfers between devices  27.2 us (13%)
  waiting for transfers between devices  14.8 us (7%)
  local copies, waits for them, and re-layouts  13.3 us (6%)
    pallas_call x3, Pallas kernels, over_rows(): pl.pallas_call(kernel, grid_spec=pltpu.PrefetchScalarGridSpec(num_scalar_...  62.3 us
    pallas_call x2, Pallas kernels, middle(): pl.pallas_call(functools.partial(middle_kernel, sizes[1], min(256, n_rows...  32.5 us
    all_to_all x5, starting transfers between devices, exchange(): return lax.all_to_all(chunks, ('gx', 'gy'), 0, 0, tiled=True)  26.3 us
    pallas_call x1, Pallas kernels, last(): pl.pallas_call(functools.partial(last_kernel, sizes[1]), grid=(channels /...  14.8 us
    all_to_all x5, waiting for transfers between devices, exchange(): return lax.all_to_all(chunks, ('gx', 'gy'), 0, 0, tiled=True)  12.5 us
    pallas_call x1, Pallas kernels, forward_modes(): pl.pallas_call(functools.partial(forward_kernel, sizes[1]), grid=(channel...  11.9 us
    unnamed x25, local copies, waits for them, and re-layouts  9.64 us
    pallas_call x1, Pallas kernels, widen_weights(): pl.pallas_call(widen_kernel, grid=(n_in // step,), in_specs=[pl.BlockSpec...  8.72 us
  transfers between devices with their start and end apart: 9, of which 4 were waited for; matrix products, arithmetic and copies ran while one was open for 3% of the time, Pallas kernels for 55%

profile of v2, /device:TPU:0, one launch (start us, length us, event | category | flops | bytes accessed | tf_op | source)
XLA Modules:
  0.0 210.5 jit_solution(4473411148224469416)
XLA Ops:
  0.6 0.0 copy-start
  0.6 0.5 collective-permute-start
  1.2 1.1 constant_dynamic-slice_fusion.1.x_ref
  2.2 1.1 constant_dynamic-slice_fusion.2.y_ref
  3.3 11.9 %forward_modes.1 = bf16[8,16,32,128]{3,2,1,0:T(8,128)(2,1)} custom-call(bf16[16,512,1024]{2,1,0:T(8,128)(2,1)} %own_ref.3, bf16[256,1024]{1,0:T(8,128)(2,1)S(1)} %constant_dynamic-slice_fusion.2.y_ref, bf16[2,512,256]{2,1,0:T(8,128)(2,1)S(1)} %constant_dynamic-slice_fusion.1.x_ref), custom_call_target="tpu_custom_call" | custom-call | flops 5368709120 | bytes 17825792 | tf_op jit(solution)/shard_map/forward_modes/pallas_call | solution.py:117
  15.3 7.0 %all-to-all-start = ((bf16[8,16,32,128]{3,2,1,0:T(8,128)(2,1)}), bf16[8,16,32,128]{3,2,1,0:T(8,128)(2,1)S(1)}, u32[]{:S(2)}, u32[]{:S(2)}) async-start(bf16[8,16,32,128]{3,2,1,0:T(8,128)(2,1)} %forward_modes.1), calls=%async_computation | async-start | bytes 2097152 | tf_op jit(solution)/shard_map/all_to_all | solution.py:68
  22.2 8.7 %widen_weights.1 = (bf16[32,16,32,128]{3,2,1,0:T(8,128)(2,1)S(1)}, bf16[32,16,32,128]{3,2,1,0:T(8,128)(2,1)}) custom-call(bf16[2,32,16,32,64]{4,3,2,1,0:T(8,128)(2,1)} %weight_ref.4), custom_call_target="tpu_custom_call" | custom-call | bytes 16777216 | tf_op jit(solution)/shard_map/widen_weights/pallas_call | solution.py:366
  30.9 2.0 copy-done.2
  32.9 0.1 pad_add_fusion.where_ref
  33.0 0.1 constant_dynamic-slice_fusion
  33.1 0.3 multiply_reduce_fusion
  33.4 1.8 fusion.9.refs_0_
  35.2 0.0 collective-permute-done.other_ref
  35.2 20.0 %point_mixing.2.mix_ref = bf16[16,512,1024]{2,1,0:T(8,128)(2,1)} custom-call(s32[2]{0:T(128)S(1)} %pad_add_fusion.where_ref, bf16[16,512,1024]{2,1,0:T(8,128)(2,1)} %own_ref.3, bf16[16,512,1024]{2,1,0:T(8,128)(2,1)} %collective-permute-done.other_ref, bf16[32,32]{1,0:T(8,128)(2,1)S(1)} %copy-done.6, f32[32,16,1024]{2,1,0:T(8,128)S(1)} %fusion.9.refs_0_), custom_call_target="tpu_custom_call" | custom-call | flops 8589934592 | bytes 52430848 | tf_op jit(solution)/shard_map/point_mixing/pallas_call | solution.py:250
  55.1 0.0 all-to-all-done
  55.2 0.1 convert_reduce_fusion
  55.3 0.3 collective-permute-start.1
  55.6 0.4 copy-done.7
  56.0 0.8 collective-permute-done.1.other_ref
  56.8 2.2 %copy-done.3 = bf16[32,16,32,128]{3,2,1,0:T(8,128)(2,1)S(1)} copy-done((bf16[32,16,32,128]{3,2,1,0:T(8,128)(2,1)S(1)}, bf16[32,16,32,128]{3,2,1,0:T(8,128)(2,1)}, u32[]{:S(2)}) %copy-start.3) | copy-done | bytes 4194328
  58.9 3.7 %mix_modes.3 = bf16[8,8,32,128]{3,2,1,0:T(8,128)(2,1)} custom-call(s32[2]{0:T(128)S(1)} %pad_add_fusion.where_ref, bf16[32,16,32,128]{3,2,1,0:T(8,128)(2,1)S(1)} %copy-done.3, bf16[32,16,32,128]{3,2,1,0:T(8,128)(2,1)} %get-tuple-element.26.imag_ref, bf16[16,32,128]{2,1,0:T(8,128)(2,1)S(1)} %multiply_convert_fusion.own_ref, ...), custom_call_target="tpu_custom_call" | custom-call | flops 4194304 | bytes 8388608 | tf_op jit(solution)/shard_map/mix_modes/pallas_call | solution.py:408
  62.6 6.0 %all-to-all-start.2 = ((bf16[8,8,32,128]{3,2,1,0:T(8,128)(2,1)}), bf16[8,8,32,128]{3,2,1,0:T(8,128)(2,1)S(1)}, u32[]{:S(2)}, u32[]{:S(2)}) async-start(bf16[8,8,32,128]{3,2,1,0:T(8,128)(2,1)} %mix_modes.3), calls=%async_computation.2 | async-start | bytes 1048576 | tf_op jit(solution)/shard_map/all_to_all | solution.py:68
  68.6 2.2 %copy-done.4 = bf16[32,16,32,128]{3,2,1,0:T(8,128)(2,1)S(1)} copy-done((bf16[32,16,32,128]{3,2,1,0:T(8,128)(2,1)S(1)}, bf16[32,16,32,128]{3,2,1,0:T(8,128)(2,1)}, u32[]{:S(2)}) %copy-start.4) | copy-done | bytes 4194328
  70.8 3.7 %mix_modes.2 = bf16[8,8,32,128]{3,2,1,0:T(8,128)(2,1)} custom-call(s32[2]{0:T(128)S(1)} %pad_add_fusion.where_ref, bf16[32,16,32,128]{3,2,1,0:T(8,128)(2,1)S(1)} %copy-done.4, bf16[32,16,32,128]{3,2,1,0:T(8,128)(2,1)} %get-tuple-element.26.imag_ref, bf16[16,32,128]{2,1,0:T(8,128)(2,1)S(1)} %multiply_convert_fusion.own_ref, ...), custom_call_target="tpu_custom_call" | custom-call | flops 4194304 | bytes 8388608 | tf_op jit(solution)/shard_map/mix_modes/pallas_call | solution.py:408
  74.4 9.0 %all-to-all-done.2.mode_ref = bf16[8,8,32,128]{3,2,1,0:T(8,128)(2,1)S(1)} async-done(((bf16[8,8,32,128]{3,2,1,0:T(8,128)(2,1)}), bf16[8,8,32,128]{3,2,1,0:T(8,128)(2,1)S(1)}, u32[]{:S(2)}, u32[]{:S(2)}) %all-to-all-start.2) | async-done | bytes 524320 | tf_op jit(solution)/shard_map/all_to_all | solution.py:68
  83.4 3.7 %all-to-all-start.1 = ((bf16[8,8,32,128]{3,2,1,0:T(8,128)(2,1)}), bf16[8,8,32,128]{3,2,1,0:T(8,128)(2,1)S(1)}, u32[]{:S(2)}, u32[]{:S(2)}) async-start(bf16[8,8,32,128]{3,2,1,0:T(8,128)(2,1)} %mix_modes.2), calls=%async_computation.1 | async-start | bytes 1048576 | tf_op jit(solution)/shard_map/all_to_all | solution.py:68
  87.1 16.2 %middle.2 = (bf16[16,512,1024]{2,1,0:T(8,128)(2,1)}, bf16[16,512,1024]{2,1,0:T(8,128)(2,1)}, bf16[8,16,32,128]{3,2,1,0:T(8,128)(2,1)}) custom-call(bf16[16,512,1024]{2,1,0:T(8,128)(2,1)} %point_mixing.2.mix_ref, bf16[16,512,1024]{2,1,0:T(8,128)(2,1)} %out_grad_ref.3, bf16[256,1024]{1,0:T(8,128)(2,1)S(1)} %constant_dynamic-slice_fusion.2.y_ref, ...), custom_call_target="tpu_custom_call" | custom-call | flops 5368709120 | bytes 33554432 | tf_op jit(solution)/shard_map/middle/pallas_call | solution.py:166
  103.3 0.0 all-to-all-done.1.mode_ref
  103.3 16.3 %middle.3 = (bf16[16,512,1024]{2,1,0:T(8,128)(2,1)}, bf16[16,512,1024]{2,1,0:T(8,128)(2,1)}, bf16[8,16,32,128]{3,2,1,0:T(8,128)(2,1)}) custom-call(bf16[16,512,1024]{2,1,0:T(8,128)(2,1)} %point_mixing.2.mix_ref, bf16[16,512,1024]{2,1,0:T(8,128)(2,1)} %out_grad_ref.3, ...), custom_call_target="tpu_custom_call", output_to_operand_aliasing={{0}: (5, {}), {1}: (6, {}), {2}: (7, {})} | custom-call | flops 5368709120 | bytes 33554432 | tf_op jit(solution)/shard_map/middle/pallas_call | solution.py:166
  119.6 0.0 collective-permute-start.3
  119.6 5.9 %all-to-all-start.3 = ((bf16[8,16,32,128]{3,2,1,0:T(8,128)(2,1)}), bf16[8,16,32,128]{3,2,1,0:T(8,128)(2,1)S(1)}, u32[]{:S(2)}, u32[]{:S(2)}) async-start(bf16[8,16,32,128]{3,2,1,0:T(8,128)(2,1)} %get-tuple-element.33), calls=%async_computation.3 | async-start | bytes 2097152 | tf_op jit(solution)/shard_map/all_to_all | solution.py:68
  125.5 0.1 eq.36
  125.6 0.3 fusion.class_ref
  125.9 22.4 %cell_sums.1 = f32[16,128]{1,0:T(8,128)S(1)} custom-call(s32[2]{0:T(128)S(1)} %pad_add_fusion.where_ref, bf16[16,512,1024]{2,1,0:T(8,128)(2,1)} %get-tuple-element.32.pre_ref.own_ref, bf16[16,512,1024]{2,1,0:T(8,128)(2,1)} %own_ref.3, bf16[16,512,1024]{2,1,0:T(8,128)(2,1)} %collective-permute-done.other_ref, bf16[32,8,1024]{2,1,0:T(8,128)(2,1)S(1)} %fusion.class_ref), custom_call_target="tpu_custom_call" | custom-call | flops 8589934592 | bytes 50864128 | tf_op jit(solution)/shard_map/cell_sums/pallas_call | solution.py:250
  148.4 3.6 %all-to-all-done.3.refs_0_ = bf16[8,16,32,128]{3,2,1,0:T(8,128)(2,1)S(1)} async-done(((bf16[8,16,32,128]{3,2,1,0:T(8,128)(2,1)}), bf16[8,16,32,128]{3,2,1,0:T(8,128)(2,1)S(1)}, u32[]{:S(2)}, u32[]{:S(2)}) %all-to-all-start.3) | async-done | bytes 1048608 | tf_op jit(solution)/shard_map/all_to_all | solution.py:68
  151.9 2.2 %copy-done.5 = bf16[32,16,32,128]{3,2,1,0:T(8,128)(2,1)S(1)} copy-done((bf16[32,16,32,128]{3,2,1,0:T(8,128)(2,1)S(1)}, bf16[32,16,32,128]{3,2,1,0:T(8,128)(2,1)}, u32[]{:S(2)}) %copy-start.5) | copy-done | bytes 4194328
  154.1 4.7 %back_mix.1 = f32[32,32,128]{2,1,0:T(8,128)S(1)} custom-call(s32[2]{0:T(128)S(1)} %pad_add_fusion.where_ref, bf16[32,16,32,128]{3,2,1,0:T(8,128)(2,1)S(1)} %copy-done.5, bf16[32,16,32,128]{3,2,1,0:T(8,128)(2,1)} %get-tuple-element.26.imag_ref, bf16[8,16,32,128]{3,2,1,0:T(8,128)(2,1)S(1)} %all-to-all-done.3.refs_0_), custom_call_target="tpu_custom_call" | custom-call | flops 8388608 | bytes 8388608 | tf_op jit(solution)/shard_map/back_mix/pallas_call | solution.py:459
  158.9 0.1 collective-permute-start.2
  159.0 1.5 collective-permute-done.2
  160.5 1.2 broadcast_in_dim.2
  161.8 3.8 %all-to-all-start.4 = ((bf16[8,18,32,128]{3,2,1,0:T(8,128)(2,1)}), bf16[8,18,32,128]{3,2,1,0:T(8,128)(2,1)S(1)}, u32[]{:S(2)}, u32[]{:S(2)}) async-start(bf16[8,18,32,128]{3,2,1,0:T(8,128)(2,1)} %broadcast_in_dim.2), calls=%async_computation.4 | async-start | bytes 2359296 | tf_op jit(solution)/shard_map/all_to_all | solution.py:68
  165.6 1.0 broadcast_select_fusion.1
  166.6 8.4 %weight_grad.1 = f32[2,32,16,32,64]{4,3,2,1,0:T(8,128)} custom-call(s32[2]{0:T(128)S(1)} %pad_add_fusion.where_ref, bf16[32,32,128]{2,1,0:T(8,128)(2,1)S(1)} %pad_maximum_fusion.spec_ref, bf16[8,16,32,128]{3,2,1,0:T(8,128)(2,1)S(1)} %all-to-all-done.3.refs_0_), custom_call_target="tpu_custom_call" | custom-call | flops 6291456 | bytes 16777216 | tf_op jit(solution)/shard_map/weight_grad/pallas_call | solution.py:499
  175.0 19.9 %point_mixing.3.point_ref = bf16[16,512,1024]{2,1,0:T(8,128)(2,1)} custom-call(s32[2]{0:T(128)S(1)} %pad_add_fusion.where_ref, bf16[16,512,1024]{2,1,0:T(8,128)(2,1)} %get-tuple-element.32.pre_ref.own_ref, bf16[16,512,1024]{2,1,0:T(8,128)(2,1)} %collective-permute-done.3.other_ref, bf16[32,32]{1,0:T(8,128)(2,1)S(1)} %copy-done.6), custom_call_target="tpu_custom_call" | custom-call | flops 8589934592 | bytes 50333696 | tf_op jit(solution)/shard_map/point_mixing/pallas_call | solution.py:250
  194.9 0.0 copy-start.1
  194.9 14.8 %last.1 = bf16[16,512,1024]{2,1,0:T(8,128)(2,1)} custom-call(bf16[16,512,1024]{2,1,0:T(8,128)(2,1)} %point_mixing.3.point_ref, bf16[256,1024]{1,0:T(8,128)(2,1)S(1)} %constant_dynamic-slice_fusion.2.y_ref, bf16[2,512,256]{2,1,0:T(8,128)(2,1)S(1)} %constant_dynamic-slice_fusion.1.x_ref, bf16[8,18,32,128]{3,2,1,0:T(8,128)(2,1)S(1)} %all-to-all-done.4.mode_ref), custom_call_target="tpu_custom_call" | custom-call | flops 5368709120 | bytes 33554432 | tf_op jit(solution)/shard_map/last/pallas_call | solution.py:192
  209.8 0.1 slice_bitcast_fusion
  209.8 0.7 copy.19
  (31 shorter events, 0.2 us)
Async XLA Ops:
  0.6 32.4 %copy-start = (f32[8,32]{1,0:T(8,128)S(1)}, f32[8,32]{1,0:T(8,128)}, u32[]{:S(2)}) copy-start(f32[8,32]{1,0:T(8,128)} %param.11) | copy-start | bytes 3076
  0.6 34.5 %collective-permute-start = (bf16[16,512,1024]{2,1,0:T(8,128)(2,1)}, bf16[16,512,1024]{2,1,0:T(8,128)(2,1)}, u32[]{:S(2)}, u32[]{:S(2)}) collective-permute-start(bf16[16,512,1024]{2,1,0:T(8,128)(2,1)} %own_ref.3), channel_id=1, source_target_pairs={{0,1},{1,0},{2,3},{3,2},{4,5},{5,4},{6,7},{7,6},{8,9},{9,8},{10,11... | collective-permute-start | bytes 50331656 | tf_op jit(solution)/shard_map/ppermute | solution.py:545
  15.2 17.8 %copy-start.10 = (s32[32,64]{1,0:T(8,128)S(1)}, s32[32,64]{1,0:T(8,128)}, u32[]{:S(2)}) copy-start(s32[32,64]{1,0:T(8,128)} %param.10) | copy-start | bytes 24580
  15.2 18.1 %copy-start.8 = (f32[64,1024,1]{1,0,2:T(8,128)S(1)}, f32[64,1024,1]{1,0,2:T(8,128)}, u32[]{:S(2)}) copy-start(f32[64,1024,1]{1,0,2:T(8,128)} %constant.41) | copy-start | bytes 786436
  15.3 19.9 %copy-start.6 = (bf16[32,32]{1,0:T(8,128)(2,1)S(1)}, bf16[32,32]{1,0:T(8,128)(2,1)}, u32[]{:S(2)}) copy-start(bf16[32,32]{1,0:T(8,128)(2,1)} %weight_ref.5) | copy-start | bytes 6148
  15.3 39.9 %all-to-all-start = ((bf16[8,16,32,128]{3,2,1,0:T(8,128)(2,1)}), bf16[8,16,32,128]{3,2,1,0:T(8,128)(2,1)S(1)}, u32[]{:S(2)}, u32[]{:S(2)}) async-start(bf16[8,16,32,128]{3,2,1,0:T(8,128)(2,1)} %forward_modes.1), calls=%async_computation | async-start | bytes 2097152 | tf_op jit(solution)/shard_map/all_to_all | solution.py:68
  30.9 2.0 copy-start.2
  55.3 0.7 copy-start.7
  55.3 1.4 collective-permute-start.1
  56.8 2.2 %copy-start.3 = (bf16[32,16,32,128]{3,2,1,0:T(8,128)(2,1)S(1)}, bf16[32,16,32,128]{3,2,1,0:T(8,128)(2,1)}, u32[]{:S(2)}) copy-start(bf16[32,16,32,128]{3,2,1,0:T(8,128)(2,1)} %copy-done.2) | copy-start | bytes 12582916
  62.6 20.8 %all-to-all-start.2 = ((bf16[8,8,32,128]{3,2,1,0:T(8,128)(2,1)}), bf16[8,8,32,128]{3,2,1,0:T(8,128)(2,1)S(1)}, u32[]{:S(2)}, u32[]{:S(2)}) async-start(bf16[8,8,32,128]{3,2,1,0:T(8,128)(2,1)} %mix_modes.3), calls=%async_computation.2 | async-start | bytes 1048576 | tf_op jit(solution)/shard_map/all_to_all | solution.py:68
  68.6 2.2 %copy-start.4 = (bf16[32,16,32,128]{3,2,1,0:T(8,128)(2,1)S(1)}, bf16[32,16,32,128]{3,2,1,0:T(8,128)(2,1)}, u32[]{:S(2)}) copy-start(bf16[32,16,32,128]{3,2,1,0:T(8,128)(2,1)} %copy-done.2) | copy-start | bytes 12582916
  83.4 19.9 %all-to-all-start.1 = ((bf16[8,8,32,128]{3,2,1,0:T(8,128)(2,1)}), bf16[8,8,32,128]{3,2,1,0:T(8,128)(2,1)S(1)}, u32[]{:S(2)}, u32[]{:S(2)}) async-start(bf16[8,8,32,128]{3,2,1,0:T(8,128)(2,1)} %mix_modes.2), calls=%async_computation.1 | async-start | bytes 1048576 | tf_op jit(solution)/shard_map/all_to_all | solution.py:68
  103.3 22.3 %copy-start.9 = (bf16[64,1024]{1,0:T(8,128)(2,1)S(1)}, bf16[64,1024]{1,0:T(8,128)(2,1)}, u32[]{:S(2)}) copy-start(bf16[64,1024]{1,0:T(8,128)(2,1)} %constant.40) | copy-start | bytes 393220
  119.6 55.4 %collective-permute-start.3 = (bf16[16,512,1024]{2,1,0:T(8,128)(2,1)}, bf16[16,512,1024]{2,1,0:T(8,128)(2,1)}, u32[]{:S(2)}, u32[]{:S(2)}) collective-permute-start(bf16[16,512,1024]{2,1,0:T(8,128)(2,1)} %get-tuple-element.32.pre_ref.own_ref), channel_id=1, source_target_pairs={{0,1},{1,0},{2,3},{3,2},{4,5},{5,4},{6,7},{7,6},{8,9},{9,8},{10,11... | collective-permute-start | bytes 50331656 | tf_op jit(solution)/shard_map/ppermute | solution.py:583
  119.6 32.4 %all-to-all-start.3 = ((bf16[8,16,32,128]{3,2,1,0:T(8,128)(2,1)}), bf16[8,16,32,128]{3,2,1,0:T(8,128)(2,1)S(1)}, u32[]{:S(2)}, u32[]{:S(2)}) async-start(bf16[8,16,32,128]{3,2,1,0:T(8,128)(2,1)} %get-tuple-element.33), calls=%async_computation.3 | async-start | bytes 2097152 | tf_op jit(solution)/shard_map/all_to_all | solution.py:68
  151.9 2.2 %copy-start.5 = (bf16[32,16,32,128]{3,2,1,0:T(8,128)(2,1)S(1)}, bf16[32,16,32,128]{3,2,1,0:T(8,128)(2,1)}, u32[]{:S(2)}) copy-start(bf16[32,16,32,128]{3,2,1,0:T(8,128)(2,1)} %copy-done.2) | copy-start | bytes 12582916
  158.9 1.6 collective-permute-start.2
  161.8 33.1 %all-to-all-start.4 = ((bf16[8,18,32,128]{3,2,1,0:T(8,128)(2,1)}), bf16[8,18,32,128]{3,2,1,0:T(8,128)(2,1)S(1)}, u32[]{:S(2)}, u32[]{:S(2)}) async-start(bf16[8,18,32,128]{3,2,1,0:T(8,128)(2,1)} %broadcast_in_dim.2), calls=%async_computation.4 | async-start | bytes 2359296 | tf_op jit(solution)/shard_map/all_to_all | solution.py:68
  194.9 15.6 %copy-start.1 = (f32[8,32]{1,0:T(8,128)S(1)}, f32[8,32]{1,0:T(8,128)}, u32[]{:S(2)}) copy-start(f32[8,32]{1,0:T(8,128)} %param.11) | copy-start | bytes 3076
  209.8 0.7 copy-start.11

commit v3 on v2

--- a/solution.py
+++ b/solution.py
@@ -33,8 +33,8 @@
     return lax.dot_general(a, b, (((0,), (0,)), ((), ())), preferred_element_type=f32)
 
 
-def params():
-    return pltpu.CompilerParams(vmem_limit_bytes=VMEM_BYTES)
+def params(limit=VMEM_BYTES):
+    return pltpu.CompilerParams(vmem_limit_bytes=limit)
 
 
 def cost(flops, *arrays, transcendentals=0):
@@ -90,7 +90,7 @@
     return [dot_nt(x_ref[part], modes).astype(bf16) for part in range(2)]
 
 
-def forward_kernel(n_gy, state_ref, y_ref, x_ref, out_ref):
+def forward_kernel(n_gy, where_ref, state_ref, y_ref, x_ref, out_ref):
     half = y_ref.shape[0] // 2
     for c in range(state_ref.shape[0]):
         rows = dot_nt(y_ref[...], state_ref[c]).astype(bf16)
@@ -98,32 +98,55 @@
         put_chunks(out_ref, c, terms, n_gy)
 
 
-def table_specs(y_tab, x_tab):
-    return [
-        pl.BlockSpec(y_tab.shape, lambda c: (0, 0)),
-        pl.BlockSpec(x_tab.shape, lambda c: (0, 0, 0)),
+def over_channels(kernel, where, fields, tables, modes, out_specs, out_shape, steps, flops, name, limit, before=(), aliases=None):
+    n_rows, n_cols = fields[0][0].shape[1:]
+    y_tab, x_tab = tables
+    table_specs = [
+        pl.BlockSpec(y_tab.shape, lambda c, w: (0, 0)),
+        pl.BlockSpec(x_tab.shape, lambda c, w: (0, 0, 0)),
     ]
-
-
-def transform_flops(channels, y_tab, x_tab):
-    n_rows, wide = x_tab.shape[1:]
-    return 2 * channels * n_rows * (y_tab.shape[0] * y_tab.shape[1] + y_tab.shape[0] * wide)
-
-
-def forward_modes(state, y_tab, x_tab, sizes, own_k):
+    moved = [jax.ShapeDtypeStruct((steps,) + spec.block_shape, bf16) for _, spec in fields]
+    return pl.pallas_call(
+        kernel,
+        grid_spec=pltpu.PrefetchScalarGridSpec(
+            num_scalar_prefetch=1,
+            grid=(steps,),
+            in_specs=[spec for _, spec in fields]
+            + table_specs
+            + [spec for _, spec in modes]
+            + [pl.BlockSpec(memory_space=pl.ANY)] * len(before),
+            out_specs=out_specs,
+        ),
+        out_shape=out_shape,
+        input_output_aliases=aliases or {},
+        compiler_params=params(limit),
+        cost_estimate=cost(flops, *moved, *moved),
+        name=name,
+    )(where, *[a for a, _ in fields], y_tab, x_tab, *[a for a, _ in modes], *before)
+
+
+def transform_flops(shape, y_tab, x_tab):
+    channels, n_rows, n_cols = shape
+    return 2 * channels * n_rows * y_tab.shape[0] * (n_cols + x_tab.shape[2])
+
+
+def forward_modes(where, state, tables, sizes, own_k):
     channels, n_rows, n_cols = state.shape
-    out = jax.ShapeDtypeStruct((sizes[0] * sizes[1], channels, own_k, x_tab.shape[2] // sizes[1]), bf16)
+    out = jax.ShapeDtypeStruct((sizes[0] * sizes[1], channels, own_k, tables[1].shape[2] // sizes[1]), bf16)
     step = divisor(channels, 4)
-    return pl.pallas_call(
+    return over_channels(
         functools.partial(forward_kernel, sizes[1]),
-        grid=(channels // step,),
-        in_specs=[pl.BlockSpec((step, n_rows, n_cols), lambda c: (c, 0, 0))] + table_specs(y_tab, x_tab),
-        out_specs=pl.BlockSpec((out.shape[0], step) + out.shape[2:], lambda c: (0, c, 0, 0)),
-        out_shape=out,
-        compiler_params=params(),
-        cost_estimate=cost(transform_flops(channels, y_tab, x_tab), state, out),
-        name="forward_modes",
-    )(state, y_tab, x_tab)
+        where,
+        [(state, pl.BlockSpec((step, n_rows, n_cols), lambda c, w: (c, 0, 0)))],
+        tables,
+        [],
+        pl.BlockSpec((out.shape[0], step) + out.shape[2:], lambda c, w: (0, c, 0, 0)),
+        out,
+        channels // step,
+        transform_flops(state.shape, *tables),
+        "forward_modes",
+        VMEM_BYTES,
+    )
 
 
 def gelu_parts(v):
@@ -134,7 +157,7 @@
     return v * cdf, cdf + v * bell
 
 
-def middle_kernel(n_gy, row_step, mix_ref, out_grad_ref, y_ref, x_ref, mode_ref, *refs):
+def middle_kernel(n_gy, row_step, where_ref, mix_ref, out_grad_ref, y_ref, x_ref, mode_ref, *refs):
     act_ref, pre_ref, out_ref = refs[-3:]
     n_rows = mix_ref.shape[1]
     half = y_ref.shape[0] // 2
@@ -154,53 +177,56 @@
         put_chunks(out_ref, c, terms, n_gy)
 
 
-def middle(mix, out_grad, y_tab, x_tab, modes, sizes, first=0, before=()):
+def middle(where, mix, out_grad, tables, modes, sizes, first=0, before=()):
     channels, n_rows, n_cols = mix.shape
-    step = divisor(modes.shape[1], 2)
+    count = modes.shape[1]
+    step = divisor(count, 2)
     skip = first // step
-    field = pl.BlockSpec((step, n_rows, n_cols), lambda c: (c + skip, 0, 0))
+    field = pl.BlockSpec((step, n_rows, n_cols), lambda c, w: (c + skip, 0, 0))
     chunk = (modes.shape[0], step) + modes.shape[2:]
     chunks = jax.ShapeDtypeStruct((modes.shape[0], channels) + modes.shape[2:], bf16)
-    flops = 2 * transform_flops(modes.shape[1], y_tab, x_tab)
-    moved = jax.ShapeDtypeStruct((4 * modes.shape[1], n_rows, n_cols), bf16)
-    return pl.pallas_call(
+    return over_channels(
         functools.partial(middle_kernel, sizes[1], min(256, n_rows)),
-        grid=(modes.shape[1] // step,),
-        in_specs=[field, field]
-        + table_specs(y_tab, x_tab)
-        + [pl.BlockSpec(chunk, lambda c: (0, c, 0, 0))]
-        + [pl.BlockSpec(memory_space=pl.ANY)] * len(before),
-        out_specs=[field, field, pl.BlockSpec(chunk, lambda c: (0, c + skip, 0, 0))],
-        out_shape=[jax.ShapeDtypeStruct(mix.shape, bf16)] * 2 + [chunks],
-        input_output_aliases={5 + n: n for n in range(len(before))},
-        compiler_params=params(),
-        cost_estimate=cost(flops, moved),
-        name="middle",
-    )(mix, out_grad, y_tab, x_tab, modes, *before)
-
-
-def last_kernel(n_gy, point_ref, y_ref, x_ref, mode_ref, out_ref):
+        where,
+        [(mix, field), (out_grad, field)],
+        tables,
+        [(modes, pl.BlockSpec(chunk, lambda c, w: (0, c, 0, 0)))],
+        [field, field, pl.BlockSpec(chunk, lambda c, w: (0, c + skip, 0, 0))],
+        [jax.ShapeDtypeStruct(mix.shape, bf16)] * 2 + [chunks],
+        count // step,
+        2 * transform_flops((count, n_rows, n_cols), *tables),
+        "middle",
+        VMEM_BYTES,
+        before,
+        {6 + n: n for n in range(len(before))},
+    )
+
+
+def last_kernel(n_gy, where_ref, point_ref, y_ref, x_ref, mode_ref, mark_ref, out_ref):
     for c in range(point_ref.shape[0]):
         space = jnp.concatenate(rows_of_modes(take_chunks(mode_ref, c, n_gy), x_ref), axis=1)
         out_ref[c] = (dot_nn(space, y_ref[...]) + point_ref[c].astype(f32)).astype(bf16)
 
 
-def last(point_back, y_tab, x_tab, modes, sizes):
+def last(where, point_back, tables, modes, sizes, mark):
     channels, n_rows, n_cols = point_back.shape
     step = divisor(channels, 4)
-    field = pl.BlockSpec((step, n_rows, n_cols), lambda c: (c, 0, 0))
-    return pl.pallas_call(
+    field = pl.BlockSpec((step, n_rows, n_cols), lambda c, w: (c, 0, 0))
+    chunk = pl.BlockSpec((modes.shape[0], step) + modes.shape[2:], lambda c, w: (0, c, 0, 0))
+    return over_channels(
         functools.partial(last_kernel, sizes[1]),
-        grid=(channels // step,),
-        in_specs=[field]
-        + table_specs(y_tab, x_tab)
-        + [pl.BlockSpec((modes.shape[0], step) + modes.shape[2:], lambda c: (0, c, 0, 0))],
-        out_specs=field,
-        out_shape=jax.ShapeDtypeStruct(point_back.shape, bf16),
-        compiler_params=params(),
-        cost_estimate=cost(transform_flops(channels, y_tab, x_tab), point_back, point_back),
-        name="last",
-    )(point_back, y_tab, x_tab, modes)
+        where,
+        [(point_back, field)],
+        tables,
+        [(modes, chunk)],
+        field,
+        jax.ShapeDtypeStruct(point_back.shape, bf16),
+        channels // step,
+        transform_flops(point_back.shape, *tables),
+        "last",
+        VMEM_BYTES,
+        [mark],
+    )
 
 
 def chooser(rows, columns, first):
@@ -223,7 +249,7 @@
 
 
 def point_kernel(transposed, where_ref, own_ref, other_ref, weight_ref, *refs):
-    bias_ref, (out_ref, spread_ref) = refs[:-2], refs[-2:]
+    bias_ref, (out_ref, mark_ref, spread_ref) = refs[:-3], refs[-3:]
     channels, n_rows, n_cols = out_ref.shape
     wide = channels * TILE
 
@@ -232,6 +258,7 @@
         own = where_ref[0] * channels
         for n, first in enumerate((own, channels - own)):
             spread_ref[n] = spread(weight_ref[...], own, first, wide, transposed)
+        mark_ref[...] = jnp.zeros_like(mark_ref)
 
     for tile in range(n_rows // TILE):
         rows = slice(tile * TILE, (tile + 1) * TILE)
@@ -243,7 +270,7 @@
         out_ref[:, rows] = total.astype(bf16)
 
 
-def over_rows(kernel, where, fields, others, other_specs, out_specs, out_shape, scratch, step, flops, name):
+def over_rows(kernel, where, fields, others, other_specs, out_specs, out_shape, scratch, step, flops, name, limit):
     channels, n_rows, n_cols = fields[0].shape
     field = pl.BlockSpec((channels, step, n_cols), lambda r, w: (0, r, 0))
     outs = out_shape if isinstance(out_shape, list) else [out_shape]
@@ -257,7 +284,7 @@
             scratch_shapes=scratch,
         ),
         out_shape=out_shape,
-        compiler_params=params(),
+        compiler_params=params(limit),
         cost_estimate=cost(flops, *fields, *others, *outs),
         name=name,
     )(where, *fields, *others)
@@ -282,12 +309,13 @@
         [weight, *bias],
         [whole_spec(weight)]
         + [pl.BlockSpec((step // TILE, channels, n_cols), lambda r, w: (r, 0, 0)) for _ in bias],
-        pl.BlockSpec((channels, step, n_cols), lambda r, w: (0, r, 0)),
-        jax.ShapeDtypeStruct(fields[0].shape, bf16),
+        [pl.BlockSpec((channels, step, n_cols), lambda r, w: (0, r, 0)), pl.BlockSpec((8, 128), lambda r, w: (0, 0))],
+        [jax.ShapeDtypeStruct(fields[0].shape, bf16), jax.ShapeDtypeStruct((8, 128), f32)],
         [pltpu.VMEM((2, wide, wide), bf16)],
         step,
         4 * wide * wide * n_cols * (n_rows // TILE),
         "point_mixing",
+        VMEM_BYTES,
     )
 
 
@@ -339,6 +367,7 @@
         step,
         4 * wide * wide * n_cols * (n_rows // TILE),
         "cell_sums",
+        VMEM_BYTES,
     )
 
 
@@ -347,35 +376,16 @@
     return jnp.where(k == 0, scale, 2.0 * scale).astype(f32)
 
 
-def swap_parts(value):
+def times_i(value):
     half = value.shape[-1] // 2
-    return jnp.concatenate([value[..., half:], value[..., :half]], axis=-1)
-
-
-def widen_kernel(weight_ref, real_ref, imag_ref):
-    real_part, imag_part = weight_ref[0], weight_ref[1]
-    real_ref[...] = jnp.concatenate([real_part, real_part], axis=-1)
-    imag_ref[...] = jnp.concatenate([-imag_part, imag_part], axis=-1)
-
-
-def widen_weights(weight):
-    n_in, n_out, own_k, own_m = weight.shape[1:]
-    step = divisor(n_in, 4)
-    out = jax.ShapeDtypeStruct((n_in, n_out, own_k, 2 * own_m), bf16)
-    out_spec = pl.BlockSpec((step, n_out, own_k, 2 * own_m), lambda i: (i, 0, 0, 0))
-    return pl.pallas_call(
-        widen_kernel,
-        grid=(n_in // step,),
-        in_specs=[pl.BlockSpec((2, step, n_out, own_k, own_m), lambda i: (0, i, 0, 0, 0))],
-        out_specs=[out_spec, out_spec],
-        out_shape=[out, out],
-        compiler_params=params(),
-        cost_estimate=cost(0, weight, weight, out, out),
-        name="widen_weights",
-    )(weight)
-
-
-def mix_kernel(scale, where_ref, real_ref, imag_ref, own_ref, other_ref, out_ref, spec_ref, swap_ref):
+    return jnp.concatenate([-value[..., half:], value[..., :half]], axis=-1)
+
+
+def twice(value):
+    return jnp.concatenate([value, value], axis=-1)
+
+
+def mix_kernel(scale, where_ref, weight_ref, own_ref, other_ref, out_ref, spec_ref, turned_ref):
     channels, own_k, lanes = own_ref.shape
 
     @pl.when(pl.program_id(0) == 0)
@@ -383,42 +393,41 @@
         own = where_ref[0] * channels
         for source, first in ((own_ref, own), (other_ref, channels - own)):
             for c in range(channels):
-                value = source[c].astype(f32)
-                spec_ref[first + c] = value
-                swap_ref[first + c] = swap_parts(value)
+                spec_ref[first + c] = source[c]
+                turned_ref[first + c] = times_i(source[c])
 
     factor = mode_weight(where_ref, own_k, scale)
-    for o in range(real_ref.shape[1]):
+    for o in range(weight_ref.shape[2]):
         total = jnp.zeros((own_k, lanes), f32)
         for i in range(2 * channels):
-            total = total + (
-                real_ref[i, o].astype(f32) * spec_ref[i] + imag_ref[i, o].astype(f32) * swap_ref[i]
-            )
+            w_real, w_imag = twice(weight_ref[0, i, o]), twice(weight_ref[1, i, o])
+            total = total + (w_real * spec_ref[i] + w_imag * turned_ref[i]).astype(f32)
         value = (total * factor).astype(bf16)
         for place in range(out_ref.shape[0]):
             out_ref[place, o] = value
 
 
-def mix_modes(where, w_real, w_imag, own, other, copies, scale, first, count):
-    n_in, n_out, own_k, lanes = w_real.shape
+def mix_modes(where, weights, own, other, copies, scale, first, count):
+    n_in, n_out, own_k, own_m = weights.shape[1:]
+    lanes = 2 * own_m
     step = divisor(count, 4)
     skip = first // step
     spec = pl.BlockSpec(own.shape, lambda o, w: (0, 0, 0))
-    weight = pl.BlockSpec((n_in, step, own_k, lanes), lambda o, w: (0, o + skip, 0, 0))
+    weight = pl.BlockSpec((2, n_in, step, own_k, own_m), lambda o, w: (0, 0, o + skip, 0, 0))
     return pl.pallas_call(
         functools.partial(mix_kernel, scale),
         grid_spec=pltpu.PrefetchScalarGridSpec(
             num_scalar_prefetch=1,
             grid=(count // step,),
-            in_specs=[weight, weight, spec, spec],
+            in_specs=[weight, spec, spec],
             out_specs=pl.BlockSpec((copies, step, own_k, lanes), lambda o, w: (0, o, 0, 0)),
-            scratch_shapes=[pltpu.VMEM((n_in, own_k, lanes), f32)] * 2,
+            scratch_shapes=[pltpu.VMEM((n_in, own_k, lanes), bf16)] * 2,
         ),
         out_shape=jax.ShapeDtypeStruct((copies, count, own_k, lanes), bf16),
         compiler_params=params(),
-        cost_estimate=cost(4 * n_in * count * own_k * lanes, w_real, w_imag),
+        cost_estimate=cost(4 * n_in * count * own_k * lanes, weights),
         name="mix_modes",
-    )(where, w_real, w_imag, own, other)
+    )(where, weights, own, other)
 
 
 def sum_chunks(where_ref, chunk_refs, scale):
@@ -432,44 +441,46 @@
             yield total * factor
 
 
-def back_kernel(scale, scale_out, n_chunks, where_ref, real_ref, imag_ref, *refs):
-    out_ref, grad_ref, swap_ref = refs[n_chunks:]
+def back_kernel(scale, scale_out, n_chunks, where_ref, weight_ref, *refs):
+    out_ref, grad_ref, turned_ref = refs[n_chunks:]
 
     @pl.when(pl.program_id(0) == 0)
     def _():
         for o, value in enumerate(sum_chunks(where_ref, refs[:n_chunks], scale)):
-            grad_ref[o] = value
-            swap_ref[o] = swap_parts(value)
-
-    for i in range(real_ref.shape[0]):
+            grad_ref[o] = value.astype(bf16)
+            turned_ref[o] = times_i(value).astype(bf16)
+
+    for i in range(weight_ref.shape[1]):
         total = jnp.zeros(out_ref.shape[1:], f32)
-        for o in range(real_ref.shape[1]):
-            total = total + (
-                real_ref[i, o].astype(f32) * grad_ref[o] - imag_ref[i, o].astype(f32) * swap_ref[o]
-            )
+        for o in range(weight_ref.shape[2]):
+            w_real, w_imag = twice(weight_ref[0, i, o]), twice(weight_ref[1, i, o])
+            total = total + (w_real * grad_ref[o] - w_imag * turned_ref[o]).astype(f32)
         out_ref[i] = total * scale_out
 
 
-def back_mix(where, w_real, w_imag, chunks, scale, scale_out):
-    n_in, n_out, own_k, lanes = w_real.shape
+def back_mix(where, weights, chunks, scale, scale_out):
+    n_in, n_out, own_k, own_m = weights.shape[1:]
+    lanes = 2 * own_m
     step = divisor(n_in // 2, 8)
     blocks = n_in // step
     half = blocks // 2
-    weight = pl.BlockSpec((step, n_out, own_k, lanes), lambda i, w: ((i + (1 - w[0]) * half) % blocks, 0, 0, 0))
+    weight = pl.BlockSpec(
+        (2, step, n_out, own_k, own_m), lambda i, w: (0, (i + (1 - w[0]) * half) % blocks, 0, 0, 0)
+    )
     return pl.pallas_call(
         functools.partial(back_kernel, scale, scale_out, len(chunks)),
         grid_spec=pltpu.PrefetchScalarGridSpec(
             num_scalar_prefetch=1,
             grid=(blocks,),
-            in_specs=[weight, weight] + [pl.BlockSpec(c.shape, lambda i, w: (0, 0, 0, 0)) for c in chunks],
+            in_specs=[weight] + [pl.BlockSpec(c.shape, lambda i, w: (0, 0, 0, 0)) for c in chunks],
             out_specs=pl.BlockSpec((step, own_k, lanes), lambda i, w: (i, 0, 0)),
-            scratch_shapes=[pltpu.VMEM((n_out, own_k, lanes), f32)] * 2,
+            scratch_shapes=[pltpu.VMEM((n_out, own_k, lanes), bf16)] * 2,
         ),
         out_shape=jax.ShapeDtypeStruct((n_in, own_k, lanes), f32),
         compiler_params=params(),
-        cost_estimate=cost(4 * n_in * n_out * own_k * lanes, w_real, w_imag),
+        cost_estimate=cost(4 * n_in * n_out * own_k * lanes, weights),
         name="back_mix",
-    )(where, w_real, w_imag, *chunks)
+    )(where, weights, *chunks)
 
 
 def weight_kernel(scale, n_chunks, where_ref, spec_ref, *refs):
@@ -515,8 +526,7 @@
 
 def slabs_of(value, shape):
     high = lax.reduce_precision(value, 8, 7)
-    middle_part = lax.reduce_precision(value - high, 8, 7)
-    parts = jnp.stack([high, middle_part, value - high - middle_part]).astype(bf16).reshape(-1)
+    parts = jnp.stack([high, value - high]).astype(bf16).reshape(-1)
     size = math.prod(shape)
     count = -(-parts.shape[0] // size)
     return jnp.pad(parts, (0, count * size - parts.shape[0])).reshape((count,) + shape)
@@ -524,7 +534,7 @@
 
 def sum_of_slabs(slabs, shape):
     total = slabs.astype(f32).sum(axis=0).reshape(-1)
-    return total[: 3 * math.prod(shape)].reshape((3,) + shape).sum(axis=0)
+    return total[: 2 * math.prod(shape)].reshape((2,) + shape).sum(axis=0)
 
 
 def on_device(n_gx, n_gy, state_in, tile_class, class_bias, w_point, spec_weight, grad_out):
@@ -545,8 +555,7 @@
     state_other = lax.ppermute(state_in, "col", other)
     y_tab = y_table(n_y, m_y, gy_index * n_cols, n_cols)
     x_tab = x_table(n_x, m_x, own_m, gx_index * n_rows, n_rows)
-
-    w_real, w_imag = widen_weights(spec_weight)
+    tables = (y_tab, x_tab)
 
     tile_rows, tile_cols = tile_class.shape
     one_hot = (tile_class[:, None, :] == jnp.arange(NCLASS, dtype=jnp.int32)[None, :, None]).astype(f32)
@@ -560,24 +569,24 @@
         one_hot.astype(bf16).reshape(tile_rows * NCLASS, tile_cols), widen.astype(bf16), preferred_element_type=f32
     )
     classes = classes.astype(bf16).reshape(tile_rows, NCLASS, n_cols)
-    mix = point_mixing(where, [state_in, state_other], w_point, False, [bias])
-
-    terms = exchange(forward_modes(state_in, y_tab, x_tab, sizes, own_k))
-    terms, mix, w_real, w_imag = lax.optimization_barrier((terms, mix, w_real, w_imag))
+    mix, _ = point_mixing(where, [state_in, state_other], w_point, False, [bias])
+
+    terms = exchange(forward_modes(where, state_in, tables, sizes, own_k))
+    terms, mix = lax.optimization_barrier((terms, mix))
     spectrum = (terms.astype(f32).sum(axis=0) * scale_fwd).astype(bf16)
     spectrum_other = lax.ppermute(spectrum, "col", other)
     halves = SPLITS if own_chan % SPLITS == 0 else 1
     count = own_chan // halves
     mixed = [
         exchange(
-            mix_modes(where, w_real, w_imag, spectrum, spectrum_other, n_grid, scale_inv, n * count, count)
+            mix_modes(where, spec_weight, spectrum, spectrum_other, n_grid, scale_inv, n * count, count)
         )
         for n in range(halves)
     ]
 
     done = ()
     for n in range(halves):
-        done = middle(mix, grad_out, y_tab, x_tab, mixed[n], sizes, n * count, done)
+        done = middle(where, mix, grad_out, tables, mixed[n], sizes, n * count, done)
     act_out, grad_pre, back_terms = done
     back_terms = [exchange(back_terms)]
     pre_other = lax.ppermute(grad_pre, "col", other)
@@ -585,7 +594,7 @@
     sums = cell_sums(where, grad_pre, state_in, state_other, classes, scale_fwd)
     sums, *back_terms = lax.optimization_barrier((sums, *back_terms))
 
-    input_terms = back_mix(where, w_real, w_imag, back_terms, scale_inv, scale_fwd)
+    input_terms = back_mix(where, spec_weight, back_terms, scale_inv, scale_fwd)
     input_modes = input_terms[own_chan:] + lax.ppermute(input_terms[:own_chan], "col", other)
     sent = jnp.concatenate([input_modes.astype(bf16), slabs_of(sums, input_modes.shape[1:])], axis=0)
     arrived = exchange(jnp.broadcast_to(sent[None], (n_grid,) + sent.shape))
@@ -595,10 +604,10 @@
         [jnp.where(first, spectrum, spectrum_other), jnp.where(first, spectrum_other, spectrum)], axis=0
     )
     grad_spec = weight_grad(where, back_terms, spec_all, own_chan, scale_inv)
-    point_back = point_mixing(where, [grad_pre, pre_other], w_point, True)
-    arrived, grad_spec, point_back = lax.optimization_barrier((arrived, grad_spec, point_back))
-
-    grad_in = last(point_back, y_tab, x_tab, arrived, sizes)
+    point_back, mark = point_mixing(where, [grad_pre, pre_other], w_point, True)
+    arrived, grad_spec, mark = lax.optimization_barrier((arrived, grad_spec, mark))
+
+    grad_in = last(where, point_back, tables, arrived, sizes, mark)
     sums = sum_of_slabs(arrived[:, own_chan:], sums.shape)
     grad_point = sums[:, : 2 * own_chan]
     grad_bias = sums[:, 2 * own_chan : 2 * own_chan + NCLASS].T

time: 212 us -> 203 us (0.958)
  local copies, waits for them, and re-layouts: 13.3 us -> 4.95 us
  waiting for transfers between devices: 14.8 us -> 21.1 us
  Pallas kernels: 151 us -> 146 us
    unnamed x25 -> x17, local copies, waits for them, and re-layouts: 9.64 us -> 1.36 us
    pallas_call x5 -> x4, Pallas kernels: 67.9 us -> 60.9 us  [over_channels(): pl.pallas_call(kernel, grid_spec=pltpu.PrefetchScalarGridSpec(num_scalar_...]
    all_to_all x5, waiting for transfers between devices: 12.5 us -> 16.8 us  [exchange(): return lax.all_to_all(chunks, ('gx', 'gy'), 0, 0, tiled=True)]
  transfers between devices with their start and end apart: 9 -> 9, of which waited for: 4 -> 6; matrix products, arithmetic and copies ran while one was open for 3% -> 3% of each run, Pallas kernels for 55% -> 54%
where the time goes in v3:
time: 203 us; the launch traced here: 202 us
  Pallas kernels  146 us (72%)
  starting transfers between devices  25.3 us (12%)
  waiting for transfers between devices  21.1 us (10%)
  local copies, waits for them, and re-layouts  4.95 us (2%)
  matrix products  2.11 us (1%)
    pallas_call x3, Pallas kernels, over_rows(): pl.pallas_call(kernel, grid_spec=pltpu.PrefetchScalarGridSpec(num_scalar_...  62.3 us
    pallas_call x4, Pallas kernels, over_channels(): pl.pallas_call(kernel, grid_spec=pltpu.PrefetchScalarGridSpec(num_scalar_...  60.9 us
    all_to_all x5, starting transfers between devices, exchange(): return lax.all_to_all(chunks, ('gx', 'gy'), 0, 0, tiled=True)  24.7 us
    all_to_all x5, waiting for transfers between devices, exchange(): return lax.all_to_all(chunks, ('gx', 'gy'), 0, 0, tiled=True)  16.8 us
    pallas_call x2, Pallas kernels, mix_modes(): pl.pallas_call(functools.partial(mix_kernel, scale), grid_spec=pltpu.Pref...  8.68 us
    pallas_call x1, Pallas kernels, weight_grad(): pl.pallas_call(functools.partial(weight_kernel, scale, len(chunks)), grid...  8.43 us
    pallas_call x1, Pallas kernels, back_mix(): pl.pallas_call(functools.partial(back_kernel, scale, scale_out, len(chunk...  6.06 us
  transfers between devices with their start and end apart: 9, of which 6 were waited for; matrix products, arithmetic and copies ran while one was open for 3% of the time, Pallas kernels for 54%

profile of v3, /device:TPU:0, one launch (start us, length us, event | category | flops | bytes accessed | tf_op | source)
XLA Modules:
  0.0 202.3 jit_solution(8610889859425898673)
XLA Ops:
  0.6 0.0 copy-start
  0.6 0.0 copy-start.4
  0.7 0.0 copy-start.6
  0.7 0.0 copy-start.2
  0.7 0.5 collective-permute-start
  1.2 0.1 pad_add_fusion.where_ref
  1.3 1.1 constant_dynamic-slice_fusion.1.x_ref
  2.4 1.1 constant_dynamic-slice_fusion.2.y_ref
  3.4 12.4 %forward_modes.1 = bf16[8,16,32,128]{3,2,1,0:T(8,128)(2,1)} custom-call(s32[2]{0:T(128)S(1)} %pad_add_fusion.where_ref, bf16[16,512,1024]{2,1,0:T(8,128)(2,1)} %own_ref.3, bf16[256,1024]{1,0:T(8,128)(2,1)S(1)} %constant_dynamic-slice_fusion.2.y_ref, bf16[2,512,256]{2,1,0:T(8,128)(2,1)S(1)} %constant_dynamic-slice_fusion.1.x_ref), custom_call_target="tpu_custom_call" | custom-call | flops 5368709120 | bytes 33554432 | tf_op jit(solution)/shard_map/forward_modes/pallas_call | solution.py:109
  15.8 6.8 %all-to-all-start = ((bf16[8,16,32,128]{3,2,1,0:T(8,128)(2,1)}), bf16[8,16,32,128]{3,2,1,0:T(8,128)(2,1)S(1)}, u32[]{:S(2)}, u32[]{:S(2)}) async-start(bf16[8,16,32,128]{3,2,1,0:T(8,128)(2,1)} %forward_modes.1), calls=%async_computation | async-start | bytes 2097152 | tf_op jit(solution)/shard_map/all_to_all | solution.py:68
  22.6 0.1 constant_dynamic-slice_fusion
  22.7 0.3 multiply_reduce_fusion
  23.0 1.8 fusion.8.refs_0_
  24.8 1.5 collective-permute-done.other_ref
  26.3 20.0 %point_mixing.2 = (bf16[16,512,1024]{2,1,0:T(8,128)(2,1)}, f32[8,128]{1,0:T(8,128)}) custom-call(s32[2]{0:T(128)S(1)} %pad_add_fusion.where_ref, bf16[16,512,1024]{2,1,0:T(8,128)(2,1)} %own_ref.3, bf16[16,512,1024]{2,1,0:T(8,128)(2,1)} %collective-permute-done.other_ref, bf16[32,32]{1,0:T(8,128)(2,1)S(1)} %copy-done.2, f32[32,16,1024]{2,1,0:T(8,128)S(1)} %fusion.8.refs_0_), custom_call_target="tpu_custom_call" | custom-call | flops 8589934592 | bytes 52434944 | tf_op jit(solution)/shard_map/point_mixing/pallas_call | solution.py:277
  46.3 2.7 %all-to-all-done = bf16[8,16,32,128]{3,2,1,0:T(8,128)(2,1)S(1)} async-done(((bf16[8,16,32,128]{3,2,1,0:T(8,128)(2,1)}), bf16[8,16,32,128]{3,2,1,0:T(8,128)(2,1)S(1)}, u32[]{:S(2)}, u32[]{:S(2)}) %all-to-all-start) | async-done | bytes 1048608 | tf_op jit(solution)/shard_map/all_to_all | solution.py:68
  49.0 0.1 convert_reduce_fusion
  49.2 0.7 copy-done.3
  49.9 0.0 collective-permute-start.1
  49.9 1.3 collective-permute-done.1.other_ref
  51.2 4.3 %mix_modes.3 = bf16[8,8,32,128]{3,2,1,0:T(8,128)(2,1)} custom-call(s32[2]{0:T(128)S(1)} %pad_add_fusion.where_ref, bf16[2,32,16,32,64]{4,3,2,1,0:T(8,128)(2,1)} %weight_ref.9, bf16[16,32,128]{2,1,0:T(8,128)(2,1)S(1)} %multiply_convert_fusion.own_ref, bf16[16,32,128]{2,1,0:T(8,128)(2,1)S(1)} %collective-permute-done.1.other_ref), custom_call_target="tpu_custom_call" | custom-call | flops 4194304 | bytes 4194304 | tf_op jit(solution)/shard_map/mix_modes/pallas_call | solution.py:417
  55.6 4.4 %all-to-all-start.2 = ((bf16[8,8,32,128]{3,2,1,0:T(8,128)(2,1)}), bf16[8,8,32,128]{3,2,1,0:T(8,128)(2,1)S(1)}, u32[]{:S(2)}, u32[]{:S(2)}) async-start(bf16[8,8,32,128]{3,2,1,0:T(8,128)(2,1)} %mix_modes.3), calls=%async_computation.2 | async-start | bytes 1048576 | tf_op jit(solution)/shard_map/all_to_all | solution.py:68
  60.0 4.3 %mix_modes.2 = bf16[8,8,32,128]{3,2,1,0:T(8,128)(2,1)} custom-call(s32[2]{0:T(128)S(1)} %pad_add_fusion.where_ref, bf16[2,32,16,32,64]{4,3,2,1,0:T(8,128)(2,1)} %weight_ref.9, bf16[16,32,128]{2,1,0:T(8,128)(2,1)S(1)} %multiply_convert_fusion.own_ref, bf16[16,32,128]{2,1,0:T(8,128)(2,1)S(1)} %collective-permute-done.1.other_ref), custom_call_target="tpu_custom_call" | custom-call | flops 4194304 | bytes 4194304 | tf_op jit(solution)/shard_map/mix_modes/pallas_call | solution.py:417
  64.3 10.5 %all-to-all-done.2.mode_ref = bf16[8,8,32,128]{3,2,1,0:T(8,128)(2,1)S(1)} async-done(((bf16[8,8,32,128]{3,2,1,0:T(8,128)(2,1)}), bf16[8,8,32,128]{3,2,1,0:T(8,128)(2,1)S(1)}, u32[]{:S(2)}, u32[]{:S(2)}) %all-to-all-start.2) | async-done | bytes 524320 | tf_op jit(solution)/shard_map/all_to_all | solution.py:68
  74.8 3.7 %all-to-all-start.1 = ((bf16[8,8,32,128]{3,2,1,0:T(8,128)(2,1)}), bf16[8,8,32,128]{3,2,1,0:T(8,128)(2,1)S(1)}, u32[]{:S(2)}, u32[]{:S(2)}) async-start(bf16[8,8,32,128]{3,2,1,0:T(8,128)(2,1)} %mix_modes.2), calls=%async_computation.1 | async-start | bytes 1048576 | tf_op jit(solution)/shard_map/all_to_all | solution.py:68
  78.5 16.6 %middle.2 = (bf16[16,512,1024]{2,1,0:T(8,128)(2,1)}, bf16[16,512,1024]{2,1,0:T(8,128)(2,1)}, bf16[8,16,32,128]{3,2,1,0:T(8,128)(2,1)}) custom-call(s32[2]{0:T(128)S(1)} %pad_add_fusion.where_ref, bf16[16,512,1024]{2,1,0:T(8,128)(2,1)} %get-tuple-element.22.mix_ref, bf16[16,512,1024]{2,1,0:T(8,128)(2,1)} %out_grad_ref.3, ...), custom_call_target="tpu_custom_call" | custom-call | flops 5368709120 | bytes 33554432 | tf_op jit(solution)/shard_map/middle/pallas_call | solution.py:109
  95.1 0.0 all-to-all-done.1.mode_ref
  95.1 16.6 %middle.3 = (bf16[16,512,1024]{2,1,0:T(8,128)(2,1)}, bf16[16,512,1024]{2,1,0:T(8,128)(2,1)}, bf16[8,16,32,128]{3,2,1,0:T(8,128)(2,1)}) custom-call(s32[2]{0:T(128)S(1)} %pad_add_fusion.where_ref, bf16[16,512,1024]{2,1,0:T(8,128)(2,1)} %get-tuple-element.22.mix_ref, ...), custom_call_target="tpu_custom_call", output_to_operand_aliasing={{0}: (6, {}), {1}: (7, {}), {2}: (8, {})} | custom-call | flops 5368709120 | bytes 33554432 | tf_op jit(solution)/shard_map/middle/pallas_call | solution.py:109
  111.7 0.0 collective-permute-start.2
  111.7 6.0 %all-to-all-start.3 = ((bf16[8,16,32,128]{3,2,1,0:T(8,128)(2,1)}), bf16[8,16,32,128]{3,2,1,0:T(8,128)(2,1)S(1)}, u32[]{:S(2)}, u32[]{:S(2)}) async-start(bf16[8,16,32,128]{3,2,1,0:T(8,128)(2,1)} %get-tuple-element.30), calls=%async_computation.3 | async-start | bytes 2097152 | tf_op jit(solution)/shard_map/all_to_all | solution.py:68
  117.7 0.1 eq.36
  117.8 0.3 fusion.class_ref
  118.1 22.4 %cell_sums.1 = f32[16,128]{1,0:T(8,128)S(1)} custom-call(s32[2]{0:T(128)S(1)} %pad_add_fusion.where_ref, bf16[16,512,1024]{2,1,0:T(8,128)(2,1)} %get-tuple-element.28.own_ref.pre_ref, bf16[16,512,1024]{2,1,0:T(8,128)(2,1)} %own_ref.3, bf16[16,512,1024]{2,1,0:T(8,128)(2,1)} %collective-permute-done.other_ref, bf16[32,8,1024]{2,1,0:T(8,128)(2,1)S(1)} %fusion.class_ref), custom_call_target="tpu_custom_call" | custom-call | flops 8589934592 | bytes 50864128 | tf_op jit(solution)/shard_map/cell_sums/pallas_call | solution.py:277
  140.6 3.6 %all-to-all-done.3.refs_0_ = bf16[8,16,32,128]{3,2,1,0:T(8,128)(2,1)S(1)} async-done(((bf16[8,16,32,128]{3,2,1,0:T(8,128)(2,1)}), bf16[8,16,32,128]{3,2,1,0:T(8,128)(2,1)S(1)}, u32[]{:S(2)}, u32[]{:S(2)}) %all-to-all-start.3) | async-done | bytes 1048608 | tf_op jit(solution)/shard_map/all_to_all | solution.py:68
  144.1 6.1 %back_mix.1 = f32[32,32,128]{2,1,0:T(8,128)S(1)} custom-call(s32[2]{0:T(128)S(1)} %pad_add_fusion.where_ref, bf16[2,32,16,32,64]{4,3,2,1,0:T(8,128)(2,1)} %weight_ref.9, bf16[8,16,32,128]{3,2,1,0:T(8,128)(2,1)S(1)} %all-to-all-done.3.refs_0_), custom_call_target="tpu_custom_call" | custom-call | flops 8388608 | bytes 4194304 | tf_op jit(solution)/shard_map/back_mix/pallas_call | solution.py:470
  150.2 0.1 collective-permute-start.3
  150.3 1.5 collective-permute-done.3
  151.9 1.2 broadcast_in_dim.2
  153.0 3.8 %all-to-all-start.4 = ((bf16[8,17,32,128]{3,2,1,0:T(8,128)(2,1)}), bf16[8,17,32,128]{3,2,1,0:T(8,128)(2,1)S(1)}, u32[]{:S(2)}, u32[]{:S(2)}) async-start(bf16[8,17,32,128]{3,2,1,0:T(8,128)(2,1)} %broadcast_in_dim.2), calls=%async_computation.4 | async-start | bytes 2228224 | tf_op jit(solution)/shard_map/all_to_all | solution.py:68
  156.8 1.0 broadcast_select_fusion.1
  157.9 8.4 %weight_grad.1 = f32[2,32,16,32,64]{4,3,2,1,0:T(8,128)} custom-call(s32[2]{0:T(128)S(1)} %pad_add_fusion.where_ref, bf16[32,32,128]{2,1,0:T(8,128)(2,1)S(1)} %pad_maximum_fusion.spec_ref, bf16[8,16,32,128]{3,2,1,0:T(8,128)(2,1)S(1)} %all-to-all-done.3.refs_0_), custom_call_target="tpu_custom_call" | custom-call | flops 6291456 | bytes 16777216 | tf_op jit(solution)/shard_map/weight_grad/pallas_call | solution.py:510
  166.3 0.0 collective-permute-done.2.other_ref
  166.3 19.9 %point_mixing.3 = (bf16[16,512,1024]{2,1,0:T(8,128)(2,1)}, f32[8,128]{1,0:T(8,128)S(1)}) custom-call(s32[2]{0:T(128)S(1)} %pad_add_fusion.where_ref, bf16[16,512,1024]{2,1,0:T(8,128)(2,1)} %get-tuple-element.28.own_ref.pre_ref, bf16[16,512,1024]{2,1,0:T(8,128)(2,1)} %collective-permute-done.2.other_ref, bf16[32,32]{1,0:T(8,128)(2,1)S(1)} %copy-done.2), custom_call_target="tpu_custom_call" | custom-call | flops 8589934592 | bytes 50337792 | tf_op jit(solution)/shard_map/point_mixing/pallas_call | solution.py:277
  186.2 0.0 all-to-all-done.4.mode_ref
  186.2 0.0 copy-start.7
  186.2 0.1 slice_bitcast_fusion
  186.3 0.7 copy.19
  187.0 15.3 %last.1 = bf16[16,512,1024]{2,1,0:T(8,128)(2,1)} custom-call(s32[2]{0:T(128)S(1)} %pad_add_fusion.where_ref, bf16[16,512,1024]{2,1,0:T(8,128)(2,1)} %get-tuple-element.29.point_ref, bf16[256,1024]{1,0:T(8,128)(2,1)S(1)} %constant_dynamic-slice_fusion.2.y_ref, bf16[2,512,256]{2,1,0:T(8,128)(2,1)S(1)} %constant_dynamic-slice_fusion.1.x_ref, ...), custom_call_target="tpu_custom_call" | custom-call | flops 5368709120 | bytes 33554432 | tf_op jit(solution)/shard_map/last/pallas_call | solution.py:109
  (21 shorter events, 0.2 us)
Async XLA Ops:
  0.6 22.0 %copy-start = (f32[8,32]{1,0:T(8,128)S(1)}, f32[8,32]{1,0:T(8,128)}, u32[]{:S(2)}) copy-start(f32[8,32]{1,0:T(8,128)} %param.11) | copy-start | bytes 3076
  0.6 22.3 %copy-start.4 = (f32[64,1024,1]{1,0,2:T(8,128)S(1)}, f32[64,1024,1]{1,0,2:T(8,128)}, u32[]{:S(2)}) copy-start(f32[64,1024,1]{1,0,2:T(8,128)} %constant.37) | copy-start | bytes 786436
  0.7 22.0 %copy-start.6 = (s32[32,64]{1,0:T(8,128)S(1)}, s32[32,64]{1,0:T(8,128)}, u32[]{:S(2)}) copy-start(s32[32,64]{1,0:T(8,128)} %param.10) | copy-start | bytes 24580
  0.7 25.7 %copy-start.2 = (bf16[32,32]{1,0:T(8,128)(2,1)S(1)}, bf16[32,32]{1,0:T(8,128)(2,1)}, u32[]{:S(2)}) copy-start(bf16[32,32]{1,0:T(8,128)(2,1)} %weight_ref.8) | copy-start | bytes 6148
  0.7 25.6 %collective-permute-start = (bf16[16,512,1024]{2,1,0:T(8,128)(2,1)}, bf16[16,512,1024]{2,1,0:T(8,128)(2,1)}, u32[]{:S(2)}, u32[]{:S(2)}) collective-permute-start(bf16[16,512,1024]{2,1,0:T(8,128)(2,1)} %own_ref.3), channel_id=1, source_target_pairs={{0,1},{1,0},{2,3},{3,2},{4,5},{5,4},{6,7},{7,6},{8,9},{9,8},{10,11... | collective-permute-start | bytes 50331656 | tf_op jit(solution)/shard_map/ppermute | solution.py:555
  15.8 33.2 %all-to-all-start = ((bf16[8,16,32,128]{3,2,1,0:T(8,128)(2,1)}), bf16[8,16,32,128]{3,2,1,0:T(8,128)(2,1)S(1)}, u32[]{:S(2)}, u32[]{:S(2)}) async-start(bf16[8,16,32,128]{3,2,1,0:T(8,128)(2,1)} %forward_modes.1), calls=%async_computation | async-start | bytes 2097152 | tf_op jit(solution)/shard_map/all_to_all | solution.py:68
  49.2 0.7 copy-start.3
  49.9 1.3 collective-permute-start.1
  55.6 19.2 %all-to-all-start.2 = ((bf16[8,8,32,128]{3,2,1,0:T(8,128)(2,1)}), bf16[8,8,32,128]{3,2,1,0:T(8,128)(2,1)S(1)}, u32[]{:S(2)}, u32[]{:S(2)}) async-start(bf16[8,8,32,128]{3,2,1,0:T(8,128)(2,1)} %mix_modes.3), calls=%async_computation.2 | async-start | bytes 1048576 | tf_op jit(solution)/shard_map/all_to_all | solution.py:68
  74.8 20.3 %all-to-all-start.1 = ((bf16[8,8,32,128]{3,2,1,0:T(8,128)(2,1)}), bf16[8,8,32,128]{3,2,1,0:T(8,128)(2,1)S(1)}, u32[]{:S(2)}, u32[]{:S(2)}) async-start(bf16[8,8,32,128]{3,2,1,0:T(8,128)(2,1)} %mix_modes.2), calls=%async_computation.1 | async-start | bytes 1048576 | tf_op jit(solution)/shard_map/all_to_all | solution.py:68
  95.1 22.7 %copy-start.5 = (bf16[64,1024]{1,0:T(8,128)(2,1)S(1)}, bf16[64,1024]{1,0:T(8,128)(2,1)}, u32[]{:S(2)}) copy-start(bf16[64,1024]{1,0:T(8,128)(2,1)} %constant.36) | copy-start | bytes 393220
  111.7 54.6 %collective-permute-start.2 = (bf16[16,512,1024]{2,1,0:T(8,128)(2,1)}, bf16[16,512,1024]{2,1,0:T(8,128)(2,1)}, u32[]{:S(2)}, u32[]{:S(2)}) collective-permute-start(bf16[16,512,1024]{2,1,0:T(8,128)(2,1)} %get-tuple-element.28.own_ref.pre_ref), channel_id=1, source_target_pairs={{0,1},{1,0},{2,3},{3,2},{4,5},{5,4},{6,7},{7,6},{8,9},{9,8},{10,11... | collective-permute-start | bytes 50331656 | tf_op jit(solution)/shard_map/ppermute | solution.py:592
  111.7 32.4 %all-to-all-start.3 = ((bf16[8,16,32,128]{3,2,1,0:T(8,128)(2,1)}), bf16[8,16,32,128]{3,2,1,0:T(8,128)(2,1)S(1)}, u32[]{:S(2)}, u32[]{:S(2)}) async-start(bf16[8,16,32,128]{3,2,1,0:T(8,128)(2,1)} %get-tuple-element.30), calls=%async_computation.3 | async-start | bytes 2097152 | tf_op jit(solution)/shard_map/all_to_all | solution.py:68
  150.2 1.6 collective-permute-start.3
  153.0 33.1 %all-to-all-start.4 = ((bf16[8,17,32,128]{3,2,1,0:T(8,128)(2,1)}), bf16[8,17,32,128]{3,2,1,0:T(8,128)(2,1)S(1)}, u32[]{:S(2)}, u32[]{:S(2)}) async-start(bf16[8,17,32,128]{3,2,1,0:T(8,128)(2,1)} %broadcast_in_dim.2), calls=%async_computation.4 | async-start | bytes 2228224 | tf_op jit(solution)/shard_map/all_to_all | solution.py:68
  186.2 16.0 %copy-start.7 = (f32[16,128]{1,0:T(8,128)}, f32[16,128]{1,0:T(8,128)S(1)}, u32[]{:S(2)}) copy-start(f32[16,128]{1,0:T(8,128)S(1)} %reduce_sum.39) | copy-start | bytes 24580
  187.0 15.3 %copy-start.1 = (f32[8,32]{1,0:T(8,128)S(1)}, f32[8,32]{1,0:T(8,128)}, u32[]{:S(2)}) copy-start(f32[8,32]{1,0:T(8,128)} %param.11) | copy-start | bytes 3076

commit v4 on v3

--- a/solution.py
+++ b/solution.py
@@ -505,7 +505,7 @@
 def weight_grad(where, chunks, spec_all, n_out, scale):
     n_in, own_k, lanes = spec_all.shape
     own_m = lanes // 2
-    step = divisor(n_in, 4)
+    step = divisor(n_in, 8)
     out = jax.ShapeDtypeStruct((2, n_in, n_out, own_k, own_m), f32)
     return pl.pallas_call(
         functools.partial(weight_kernel, scale, len(chunks)),
@@ -592,17 +592,17 @@
     pre_other = lax.ppermute(grad_pre, "col", other)
 
     sums = cell_sums(where, grad_pre, state_in, state_other, classes, scale_fwd)
-    sums, *back_terms = lax.optimization_barrier((sums, *back_terms))
+    first = col_index == 0
+    spec_all = jnp.concatenate(
+        [jnp.where(first, spectrum, spectrum_other), jnp.where(first, spectrum_other, spectrum)], axis=0
+    )
+    sums, spec_all, *back_terms = lax.optimization_barrier((sums, spec_all, *back_terms))
 
     input_terms = back_mix(where, spec_weight, back_terms, scale_inv, scale_fwd)
     input_modes = input_terms[own_chan:] + lax.ppermute(input_terms[:own_chan], "col", other)
     sent = jnp.concatenate([input_modes.astype(bf16), slabs_of(sums, input_modes.shape[1:])], axis=0)
     arrived = exchange(jnp.broadcast_to(sent[None], (n_grid,) + sent.shape))
 
-    first = col_index == 0
-    spec_all = jnp.concatenate(
-        [jnp.where(first, spectrum, spectrum_other), jnp.where(first, spectrum_other, spectrum)], axis=0
-    )
     grad_spec = weight_grad(where, back_terms, spec_all, own_chan, scale_inv)
     point_back, mark = point_mixing(where, [grad_pre, pre_other], w_point, True)
     arrived, grad_spec, mark = lax.optimization_barrier((arrived, grad_spec, mark))

time: 203 us -> 201 us (level)
  transfers between devices with their start and end apart: 9 -> 9, of which waited for: 6 -> 6; matrix products, arithmetic and copies ran while one was open for 3% -> 3% of each run, Pallas kernels for 54% -> 55%
where the time goes in v4:
time: 201 us
  Pallas kernels  146 us (73%)
  starting transfers between devices  25.3 us (13%)
  waiting for transfers between devices  21.1 us (10%)
  local copies, waits for them, and re-layouts  4.28 us (2%)
  matrix products  2.11 us (1%)
    pallas_call x3, Pallas kernels, over_rows(): pl.pallas_call(kernel, grid_spec=pltpu.PrefetchScalarGridSpec(num_scalar_...  62.3 us
    pallas_call x4, Pallas kernels, over_channels(): pl.pallas_call(kernel, grid_spec=pltpu.PrefetchScalarGridSpec(num_scalar_...  61 us
    all_to_all x5, starting transfers between devices, exchange(): return lax.all_to_all(chunks, ('gx', 'gy'), 0, 0, tiled=True)  24.7 us
    all_to_all x5, waiting for transfers between devices, exchange(): return lax.all_to_all(chunks, ('gx', 'gy'), 0, 0, tiled=True)  16.7 us
    pallas_call x2, Pallas kernels, mix_modes(): pl.pallas_call(functools.partial(mix_kernel, scale), grid_spec=pltpu.Pref...  8.68 us
    pallas_call x1, Pallas kernels, weight_grad(): pl.pallas_call(functools.partial(weight_kernel, scale, len(chunks)), grid...  8.25 us
    pallas_call x1, Pallas kernels, back_mix(): pl.pallas_call(functools.partial(back_kernel, scale, scale_out, len(chunk...  6.06 us
  transfers between devices with their start and end apart: 9, of which 6 were waited for; matrix products, arithmetic and copies ran while one was open for 3% of the time, Pallas kernels for 55%

profile of v4, /device:TPU:0, one launch (start us, length us, event | category | flops | bytes accessed | tf_op | source)
XLA Modules:
  0.0 200.5 jit_solution(15252488137731935060)
XLA Ops:
  0.6 0.0 copy-start
  0.6 0.0 copy-start.3
  0.7 0.5 collective-permute-start
  1.2 0.1 pad_add_fusion.where_ref
  1.3 1.1 constant_dynamic-slice_fusion.1.x_ref
  2.4 1.1 constant_dynamic-slice_fusion.2.y_ref
  3.4 12.4 %forward_modes.1 = bf16[8,16,32,128]{3,2,1,0:T(8,128)(2,1)} custom-call(s32[2]{0:T(128)S(1)} %pad_add_fusion.where_ref, bf16[16,512,1024]{2,1,0:T(8,128)(2,1)} %own_ref.3, bf16[256,1024]{1,0:T(8,128)(2,1)S(1)} %constant_dynamic-slice_fusion.2.y_ref, bf16[2,512,256]{2,1,0:T(8,128)(2,1)S(1)} %constant_dynamic-slice_fusion.1.x_ref), custom_call_target="tpu_custom_call" | custom-call | flops 5368709120 | bytes 33554432 | tf_op jit(solution)/shard_map/forward_modes/pallas_call | solution.py:109
  15.8 6.8 %all-to-all-start = ((bf16[8,16,32,128]{3,2,1,0:T(8,128)(2,1)}), bf16[8,16,32,128]{3,2,1,0:T(8,128)(2,1)S(1)}, u32[]{:S(2)}, u32[]{:S(2)}) async-start(bf16[8,16,32,128]{3,2,1,0:T(8,128)(2,1)} %forward_modes.1), calls=%async_computation | async-start | bytes 2097152 | tf_op jit(solution)/shard_map/all_to_all | solution.py:68
  22.6 0.0 copy-done
  22.6 0.1 constant_dynamic-slice_fusion
  22.7 0.0 copy-done.5
  22.7 0.3 multiply_reduce_fusion
  23.0 1.8 fusion.8.refs_0_
  24.8 1.5 collective-permute-done.other_ref
  26.3 0.0 copy-done.2
  26.3 20.0 %point_mixing.2 = (bf16[16,512,1024]{2,1,0:T(8,128)(2,1)}, f32[8,128]{1,0:T(8,128)}) custom-call(s32[2]{0:T(128)S(1)} %pad_add_fusion.where_ref, bf16[16,512,1024]{2,1,0:T(8,128)(2,1)} %own_ref.3, bf16[16,512,1024]{2,1,0:T(8,128)(2,1)} %collective-permute-done.other_ref, bf16[32,32]{1,0:T(8,128)(2,1)S(1)} %copy-done.2, f32[32,16,1024]{2,1,0:T(8,128)S(1)} %fusion.8.refs_0_), custom_call_target="tpu_custom_call" | custom-call | flops 8589934592 | bytes 52434944 | tf_op jit(solution)/shard_map/point_mixing/pallas_call | solution.py:277
  46.3 2.7 %all-to-all-done = bf16[8,16,32,128]{3,2,1,0:T(8,128)(2,1)S(1)} async-done(((bf16[8,16,32,128]{3,2,1,0:T(8,128)(2,1)}), bf16[8,16,32,128]{3,2,1,0:T(8,128)(2,1)S(1)}, u32[]{:S(2)}, u32[]{:S(2)}) %all-to-all-start) | async-done | bytes 1048608 | tf_op jit(solution)/shard_map/all_to_all | solution.py:68
  49.0 0.1 convert_reduce_fusion
  49.2 0.1 collective-permute-start.1
  49.3 1.3 collective-permute-done.1.other_ref
  50.6 4.3 %mix_modes.3 = bf16[8,8,32,128]{3,2,1,0:T(8,128)(2,1)} custom-call(s32[2]{0:T(128)S(1)} %pad_add_fusion.where_ref, bf16[2,32,16,32,64]{4,3,2,1,0:T(8,128)(2,1)} %weight_ref.9, bf16[16,32,128]{2,1,0:T(8,128)(2,1)S(1)} %multiply_convert_fusion.own_ref, bf16[16,32,128]{2,1,0:T(8,128)(2,1)S(1)} %collective-permute-done.1.other_ref), custom_call_target="tpu_custom_call" | custom-call | flops 4194304 | bytes 4194304 | tf_op jit(solution)/shard_map/mix_modes/pallas_call | solution.py:417
  55.0 4.4 %all-to-all-start.2 = ((bf16[8,8,32,128]{3,2,1,0:T(8,128)(2,1)}), bf16[8,8,32,128]{3,2,1,0:T(8,128)(2,1)S(1)}, u32[]{:S(2)}, u32[]{:S(2)}) async-start(bf16[8,8,32,128]{3,2,1,0:T(8,128)(2,1)} %mix_modes.3), calls=%async_computation.2 | async-start | bytes 1048576 | tf_op jit(solution)/shard_map/all_to_all | solution.py:68
  59.4 4.3 %mix_modes.2 = bf16[8,8,32,128]{3,2,1,0:T(8,128)(2,1)} custom-call(s32[2]{0:T(128)S(1)} %pad_add_fusion.where_ref, bf16[2,32,16,32,64]{4,3,2,1,0:T(8,128)(2,1)} %weight_ref.9, bf16[16,32,128]{2,1,0:T(8,128)(2,1)S(1)} %multiply_convert_fusion.own_ref, bf16[16,32,128]{2,1,0:T(8,128)(2,1)S(1)} %collective-permute-done.1.other_ref), custom_call_target="tpu_custom_call" | custom-call | flops 4194304 | bytes 4194304 | tf_op jit(solution)/shard_map/mix_modes/pallas_call | solution.py:417
  63.7 10.5 %all-to-all-done.2.mode_ref = bf16[8,8,32,128]{3,2,1,0:T(8,128)(2,1)S(1)} async-done(((bf16[8,8,32,128]{3,2,1,0:T(8,128)(2,1)}), bf16[8,8,32,128]{3,2,1,0:T(8,128)(2,1)S(1)}, u32[]{:S(2)}, u32[]{:S(2)}) %all-to-all-start.2) | async-done | bytes 524320 | tf_op jit(solution)/shard_map/all_to_all | solution.py:68
  74.2 3.7 %all-to-all-start.1 = ((bf16[8,8,32,128]{3,2,1,0:T(8,128)(2,1)}), bf16[8,8,32,128]{3,2,1,0:T(8,128)(2,1)S(1)}, u32[]{:S(2)}, u32[]{:S(2)}) async-start(bf16[8,8,32,128]{3,2,1,0:T(8,128)(2,1)} %mix_modes.2), calls=%async_computation.1 | async-start | bytes 1048576 | tf_op jit(solution)/shard_map/all_to_all | solution.py:68
  77.9 16.7 %middle.2 = (bf16[16,512,1024]{2,1,0:T(8,128)(2,1)}, bf16[16,512,1024]{2,1,0:T(8,128)(2,1)}, bf16[8,16,32,128]{3,2,1,0:T(8,128)(2,1)}) custom-call(s32[2]{0:T(128)S(1)} %pad_add_fusion.where_ref, bf16[16,512,1024]{2,1,0:T(8,128)(2,1)} %get-tuple-element.23.mix_ref, bf16[16,512,1024]{2,1,0:T(8,128)(2,1)} %out_grad_ref.3, ...), custom_call_target="tpu_custom_call" | custom-call | flops 5368709120 | bytes 33554432 | tf_op jit(solution)/shard_map/middle/pallas_call | solution.py:109
  94.5 0.0 all-to-all-done.1.mode_ref
  94.6 16.6 %middle.3 = (bf16[16,512,1024]{2,1,0:T(8,128)(2,1)}, bf16[16,512,1024]{2,1,0:T(8,128)(2,1)}, bf16[8,16,32,128]{3,2,1,0:T(8,128)(2,1)}) custom-call(s32[2]{0:T(128)S(1)} %pad_add_fusion.where_ref, bf16[16,512,1024]{2,1,0:T(8,128)(2,1)} %get-tuple-element.23.mix_ref, ...), custom_call_target="tpu_custom_call", output_to_operand_aliasing={{0}: (6, {}), {1}: (7, {}), {2}: (8, {})} | custom-call | flops 5368709120 | bytes 33554432 | tf_op jit(solution)/shard_map/middle/pallas_call | solution.py:109
  111.2 0.0 collective-permute-start.2
  111.2 5.9 %all-to-all-start.3 = ((bf16[8,16,32,128]{3,2,1,0:T(8,128)(2,1)}), bf16[8,16,32,128]{3,2,1,0:T(8,128)(2,1)S(1)}, u32[]{:S(2)}, u32[]{:S(2)}) async-start(bf16[8,16,32,128]{3,2,1,0:T(8,128)(2,1)} %get-tuple-element.31), calls=%async_computation.3 | async-start | bytes 2097152 | tf_op jit(solution)/shard_map/all_to_all | solution.py:68
  117.2 0.1 eq.36
  117.2 0.0 copy-done.4
  117.2 0.3 fusion.class_ref
  117.7 22.4 %cell_sums.1 = f32[16,128]{1,0:T(8,128)S(1)} custom-call(s32[2]{0:T(128)S(1)} %pad_add_fusion.where_ref, bf16[16,512,1024]{2,1,0:T(8,128)(2,1)} %get-tuple-element.29.own_ref.pre_ref, bf16[16,512,1024]{2,1,0:T(8,128)(2,1)} %own_ref.3, bf16[16,512,1024]{2,1,0:T(8,128)(2,1)} %collective-permute-done.other_ref, bf16[32,8,1024]{2,1,0:T(8,128)(2,1)S(1)} %fusion.class_ref), custom_call_target="tpu_custom_call" | custom-call | flops 8589934592 | bytes 50864128 | tf_op jit(solution)/shard_map/cell_sums/pallas_call | solution.py:277
  140.1 3.5 %all-to-all-done.3.refs_0_ = bf16[8,16,32,128]{3,2,1,0:T(8,128)(2,1)S(1)} async-done(((bf16[8,16,32,128]{3,2,1,0:T(8,128)(2,1)}), bf16[8,16,32,128]{3,2,1,0:T(8,128)(2,1)S(1)}, u32[]{:S(2)}, u32[]{:S(2)}) %all-to-all-start.3) | async-done | bytes 1048608 | tf_op jit(solution)/shard_map/all_to_all | solution.py:68
  143.6 6.1 %back_mix.1 = f32[32,32,128]{2,1,0:T(8,128)S(1)} custom-call(s32[2]{0:T(128)S(1)} %pad_add_fusion.where_ref, bf16[2,32,16,32,64]{4,3,2,1,0:T(8,128)(2,1)} %weight_ref.9, bf16[8,16,32,128]{3,2,1,0:T(8,128)(2,1)S(1)} %all-to-all-done.3.refs_0_), custom_call_target="tpu_custom_call" | custom-call | flops 8388608 | bytes 4194304 | tf_op jit(solution)/shard_map/back_mix/pallas_call | solution.py:470
  149.7 0.1 collective-permute-start.3
  149.8 1.5 collective-permute-done.3
  151.3 1.2 broadcast_in_dim.2
  152.5 3.8 %all-to-all-start.4 = ((bf16[8,17,32,128]{3,2,1,0:T(8,128)(2,1)}), bf16[8,17,32,128]{3,2,1,0:T(8,128)(2,1)S(1)}, u32[]{:S(2)}, u32[]{:S(2)}) async-start(bf16[8,17,32,128]{3,2,1,0:T(8,128)(2,1)} %broadcast_in_dim.2), calls=%async_computation.4 | async-start | bytes 2228224 | tf_op jit(solution)/shard_map/all_to_all | solution.py:68
  156.3 8.2 %weight_grad.1 = f32[2,32,16,32,64]{4,3,2,1,0:T(8,128)} custom-call(s32[2]{0:T(128)S(1)} %pad_add_fusion.where_ref, bf16[32,32,128]{2,1,0:T(8,128)(2,1)S(1)} %pad_maximum_fusion.spec_ref, bf16[8,16,32,128]{3,2,1,0:T(8,128)(2,1)S(1)} %all-to-all-done.3.refs_0_), custom_call_target="tpu_custom_call" | custom-call | flops 6291456 | bytes 16777216 | tf_op jit(solution)/shard_map/weight_grad/pallas_call | solution.py:510
  164.5 0.0 collective-permute-done.2.other_ref
  164.5 19.9 %point_mixing.3 = (bf16[16,512,1024]{2,1,0:T(8,128)(2,1)}, f32[8,128]{1,0:T(8,128)S(1)}) custom-call(s32[2]{0:T(128)S(1)} %pad_add_fusion.where_ref, bf16[16,512,1024]{2,1,0:T(8,128)(2,1)} %get-tuple-element.29.own_ref.pre_ref, bf16[16,512,1024]{2,1,0:T(8,128)(2,1)} %collective-permute-done.2.other_ref, bf16[32,32]{1,0:T(8,128)(2,1)S(1)} %copy-done.2), custom_call_target="tpu_custom_call" | custom-call | flops 8589934592 | bytes 50337792 | tf_op jit(solution)/shard_map/point_mixing/pallas_call | solution.py:277
  184.4 0.0 all-to-all-done.4.mode_ref
  184.5 0.0 copy-start.6
  184.5 0.1 slice_bitcast_fusion
  184.6 0.7 copy.19
  185.2 15.3 %last.1 = bf16[16,512,1024]{2,1,0:T(8,128)(2,1)} custom-call(s32[2]{0:T(128)S(1)} %pad_add_fusion.where_ref, bf16[16,512,1024]{2,1,0:T(8,128)(2,1)} %get-tuple-element.30.point_ref, bf16[256,1024]{1,0:T(8,128)(2,1)S(1)} %constant_dynamic-slice_fusion.2.y_ref, bf16[2,512,256]{2,1,0:T(8,128)(2,1)S(1)} %constant_dynamic-slice_fusion.1.x_ref, ...), custom_call_target="tpu_custom_call" | custom-call | flops 5368709120 | bytes 33554432 | tf_op jit(solution)/shard_map/last/pallas_call | solution.py:109
  (19 shorter events, 0.2 us)
Async XLA Ops:
  0.6 22.0 %copy-start = (f32[8,32]{1,0:T(8,128)S(1)}, f32[8,32]{1,0:T(8,128)}, u32[]{:S(2)}) copy-start(f32[8,32]{1,0:T(8,128)} %param.11) | copy-start | bytes 3076
  0.6 22.3 %copy-start.3 = (f32[64,1024,1]{1,0,2:T(8,128)S(1)}, f32[64,1024,1]{1,0,2:T(8,128)}, u32[]{:S(2)}) copy-start(f32[64,1024,1]{1,0,2:T(8,128)} %constant.37) | copy-start | bytes 786436
  0.7 22.0 %copy-start.5 = (s32[32,64]{1,0:T(8,128)S(1)}, s32[32,64]{1,0:T(8,128)}, u32[]{:S(2)}) copy-start(s32[32,64]{1,0:T(8,128)} %param.10) | copy-start | bytes 24580
  0.7 25.7 %copy-start.2 = (bf16[32,32]{1,0:T(8,128)(2,1)S(1)}, bf16[32,32]{1,0:T(8,128)(2,1)}, u32[]{:S(2)}) copy-start(bf16[32,32]{1,0:T(8,128)(2,1)} %weight_ref.8) | copy-start | bytes 6148
  0.7 25.6 %collective-permute-start = (bf16[16,512,1024]{2,1,0:T(8,128)(2,1)}, bf16[16,512,1024]{2,1,0:T(8,128)(2,1)}, u32[]{:S(2)}, u32[]{:S(2)}) collective-permute-start(bf16[16,512,1024]{2,1,0:T(8,128)(2,1)} %own_ref.3), channel_id=1, source_target_pairs={{0,1},{1,0},{2,3},{3,2},{4,5},{5,4},{6,7},{7,6},{8,9},{9,8},{10,11... | collective-permute-start | bytes 50331656 | tf_op jit(solution)/shard_map/ppermute | solution.py:555
  15.8 33.2 %all-to-all-start = ((bf16[8,16,32,128]{3,2,1,0:T(8,128)(2,1)}), bf16[8,16,32,128]{3,2,1,0:T(8,128)(2,1)S(1)}, u32[]{:S(2)}, u32[]{:S(2)}) async-start(bf16[8,16,32,128]{3,2,1,0:T(8,128)(2,1)} %forward_modes.1), calls=%async_computation | async-start | bytes 2097152 | tf_op jit(solution)/shard_map/all_to_all | solution.py:68
  49.2 1.4 collective-permute-start.1
  55.0 19.2 %all-to-all-start.2 = ((bf16[8,8,32,128]{3,2,1,0:T(8,128)(2,1)}), bf16[8,8,32,128]{3,2,1,0:T(8,128)(2,1)S(1)}, u32[]{:S(2)}, u32[]{:S(2)}) async-start(bf16[8,8,32,128]{3,2,1,0:T(8,128)(2,1)} %mix_modes.3), calls=%async_computation.2 | async-start | bytes 1048576 | tf_op jit(solution)/shard_map/all_to_all | solution.py:68
  74.2 20.3 %all-to-all-start.1 = ((bf16[8,8,32,128]{3,2,1,0:T(8,128)(2,1)}), bf16[8,8,32,128]{3,2,1,0:T(8,128)(2,1)S(1)}, u32[]{:S(2)}, u32[]{:S(2)}) async-start(bf16[8,8,32,128]{3,2,1,0:T(8,128)(2,1)} %mix_modes.2), calls=%async_computation.1 | async-start | bytes 1048576 | tf_op jit(solution)/shard_map/all_to_all | solution.py:68
  94.5 22.7 %copy-start.4 = (bf16[64,1024]{1,0:T(8,128)(2,1)S(1)}, bf16[64,1024]{1,0:T(8,128)(2,1)}, u32[]{:S(2)}) copy-start(bf16[64,1024]{1,0:T(8,128)(2,1)} %constant.36) | copy-start | bytes 393220
  111.2 53.3 %collective-permute-start.2 = (bf16[16,512,1024]{2,1,0:T(8,128)(2,1)}, bf16[16,512,1024]{2,1,0:T(8,128)(2,1)}, u32[]{:S(2)}, u32[]{:S(2)}) collective-permute-start(bf16[16,512,1024]{2,1,0:T(8,128)(2,1)} %get-tuple-element.29.own_ref.pre_ref), channel_id=1, source_target_pairs={{0,1},{1,0},{2,3},{3,2},{4,5},{5,4},{6,7},{7,6},{8,9},{9,8},{10,11... | collective-permute-start | bytes 50331656 | tf_op jit(solution)/shard_map/ppermute | solution.py:592
  111.2 32.4 %all-to-all-start.3 = ((bf16[8,16,32,128]{3,2,1,0:T(8,128)(2,1)}), bf16[8,16,32,128]{3,2,1,0:T(8,128)(2,1)S(1)}, u32[]{:S(2)}, u32[]{:S(2)}) async-start(bf16[8,16,32,128]{3,2,1,0:T(8,128)(2,1)} %get-tuple-element.31), calls=%async_computation.3 | async-start | bytes 2097152 | tf_op jit(solution)/shard_map/all_to_all | solution.py:68
  149.7 1.6 collective-permute-start.3
  152.5 31.9 %all-to-all-start.4 = ((bf16[8,17,32,128]{3,2,1,0:T(8,128)(2,1)}), bf16[8,17,32,128]{3,2,1,0:T(8,128)(2,1)S(1)}, u32[]{:S(2)}, u32[]{:S(2)}) async-start(bf16[8,17,32,128]{3,2,1,0:T(8,128)(2,1)} %broadcast_in_dim.2), calls=%async_computation.4 | async-start | bytes 2228224 | tf_op jit(solution)/shard_map/all_to_all | solution.py:68
  184.5 16.0 %copy-start.6 = (f32[16,128]{1,0:T(8,128)}, f32[16,128]{1,0:T(8,128)S(1)}, u32[]{:S(2)}) copy-start(f32[16,128]{1,0:T(8,128)S(1)} %reduce_sum.39) | copy-start | bytes 24580
  185.2 15.3 %copy-start.1 = (f32[8,32]{1,0:T(8,128)S(1)}, f32[8,32]{1,0:T(8,128)}, u32[]{:S(2)}) copy-start(f32[8,32]{1,0:T(8,128)} %param.11) | copy-start | bytes 3076
